TPU v7x, 256 devices: a whole 4x4x8 slice. The times are simulated.
256 devices in a mesh: branch: 8 (over y, core), leaf: 32 (over z, x).
Axes of the slice: x: 4, y: 4, z: 8, core: 2. Of those that a mesh axis runs over, the one named last changes fastest.
Arguments:
- values: bfloat16 [2, 16, 131072], P(None, None, ('branch', 'leaf')), may hold values from -6 to 6
- leaf_basis: bfloat16 [2048, 64, 64], P(('branch', 'leaf')), may hold values from -0.75 to 0.75
- transfer: bfloat16 [3584, 64, 64], P(('branch', 'leaf')), may hold values from -0.625 to 0.625
- local_coupling: bfloat16 [2, 3584, 12, 64, 64], P(None, ('branch', 'leaf')), may hold values from -0.21875 to 0.21875
- coupling_source: int32 [3584, 12], P(('branch', 'leaf')), may hold values from 0 to 23, as said below
- near_field: bfloat16 [2, 2048, 12, 64, 64], P(None, ('branch', 'leaf')), may hold values from -0.21875 to 0.21875
- near_source: int32 [2048, 12], P(('branch', 'leaf')), may hold values from 0 to 23, as said below
- upper_transfer: bfloat16 [8, 62, 64, 64], P('branch'), may hold values from -0.625 to 0.625
- upper_coupling: bfloat16 [2, 8, 62, 64, 64], P(None, 'branch'), may hold values from -0.75 to 0.75
- top_coupling: bfloat16 [2, 8, 7, 64, 64], P(None, 'branch'), may hold values from -0.25 to 0.25
Outputs:
- result: float32 [2, 16, 131072], P(None, None, ('branch', 'leaf'))
Inputs may be any that keep to these rules, and one draw needn't show every extreme that they name: `coupling_source`: entry of row r(l, p, t) lies in t to t + 2 * n_l, so its source is within n_l clusters of the target along the device order. `near_source`: entry of leaf t of a device lies in t to t + 16, so its source leaf is within 8 leaves of the target.
All inputs are finite; a program needn't handle non-finite values.
Results may differ from a plain program's by a relative error of at most 0.027.
Values may be sent and summed in bfloat16 or wider, within the bound.
No kernel may reach another device: no remote copies, remote signals or barrier semaphores. Data moves between devices by JAX's collectives and lax.ppermute only.
A program may use at most 64 MiB of HBM per device.

v0:
```python
import jax
import jax.numpy as jnp
from jax import lax
from jax.sharding import PartitionSpec as P

LOG_LEAF = 3


def with_halo(cells, sides, width):
    for axis, dim in sides:
        count = lax.axis_size(axis)
        ends = count - 1
        head = lax.slice_in_dim(cells, 0, width, axis=dim)
        tail = lax.slice_in_dim(cells, cells.shape[dim] - width, cells.shape[dim], axis=dim)
        cells = jnp.concatenate(
            [
                lax.ppermute(tail, axis, [(i, (i + 1) % count) for i in range(ends)]),
                cells,
                lax.ppermute(head, axis, [((i + 1) % count, i) for i in range(ends)]),
            ],
            axis=dim,
        )
    return cells


def swapped(shard, axis, distance):
    return lax.ppermute(shard, axis, [(i, i ^ 1 << distance) for i in range(lax.axis_size(axis))])


def pick_row(table, index):
    return lax.dynamic_index_in_dim(table, index, 0, keepdims=False)


def per_device(
    values,
    leaf_basis,
    transfer,
    local_coupling,
    coupling_source,
    near_field,
    near_source,
    upper_transfer,
    upper_coupling,
    top_coupling,
):
    f32 = jnp.float32
    bf16 = jnp.bfloat16
    operators, rhs_count, width = values.shape
    leaves, leaf_size, rank = leaf_basis.shape
    value_wide = with_halo(values[None], ((("branch", "leaf"), 0),), 1)
    cells = values.reshape(operators, rhs_count, leaves, leaf_size)
    coef = jnp.einsum("grlq,lqk->lgrk", cells, leaf_basis, preferred_element_type=f32).astype(bf16)
    levels = [coef]
    begins = []
    begin = 0
    for level in range(1, LOG_LEAF + 1):
        count = leaves >> level - 1
        part = jnp.einsum(
            "cgrk,ckm->cgrm",
            levels[-1],
            transfer[begin : begin + count],
            preferred_element_type=f32,
        )
        part = part.reshape(count // 2, 2, operators, rhs_count, rank)
        levels.append((part[:, 0] + part[:, 1]).astype(bf16))
        begins.append(begin)
        begin += count
    device_root = levels[-1][0]
    stack = jnp.concatenate(levels[:-1], axis=0)
    coef_wide = with_halo(stack[None], ((("branch", "leaf"), 0),), 1)
    leaf_count = lax.axis_size("leaf")
    depth = leaf_count.bit_length() - 1
    leaf_index = lax.axis_index("leaf")
    upward = upper_transfer[0]
    offsets = [2 * leaf_count - 2 * (leaf_count >> step) for step in range(depth)]
    siblings = []
    owners = []
    current = device_root
    for step in range(depth):
        owner = offsets[step] + jnp.right_shift(leaf_index, step)
        other = swapped(current, "leaf", step)
        mine = jnp.einsum(
            "grk,km->grm", current, pick_row(upward, owner), preferred_element_type=f32
        )
        theirs = jnp.einsum(
            "grk,km->grm",
            other,
            pick_row(upward, jnp.bitwise_xor(owner, 1)),
            preferred_element_type=f32,
        )
        current = (mine + theirs).astype(bf16)
        siblings.append(other)
        owners.append(owner)
    branch_count = lax.axis_size("branch")
    branch_index = lax.axis_index("branch")
    subtree_roots = lax.all_gather(current[None], "branch", axis=0, tiled=True)
    order = (branch_index + 1 + jnp.arange(branch_count - 1, dtype=jnp.int32)) % branch_count
    others = jnp.take(subtree_roots, order, axis=0)
    down = jnp.einsum(
        "jgrm,gjkm->grk", others, top_coupling[:, 0], preferred_element_type=f32
    ).astype(bf16)
    sibling_mats = upper_coupling[:, 0]
    for step in range(depth - 1, -1, -1):
        owner = owners[step]
        coupling_here = lax.dynamic_index_in_dim(sibling_mats, owner, 1, keepdims=False)
        coupled = jnp.einsum(
            "grm,gkm->grk", siblings[step], coupling_here, preferred_element_type=f32
        )
        carried = jnp.einsum(
            "grm,km->grk", down, pick_row(upward, owner), preferred_element_type=f32
        )
        down = (coupled + carried).astype(bf16)
    parent = down[None]
    for level in range(LOG_LEAF - 1, -1, -1):
        count = leaves >> level
        start = begins[level]
        window_rows = coef_wide[:, start : start + count].reshape(
            3 * count, operators, rhs_count, rank
        )
        picked = jnp.take(window_rows, coupling_source[start : start + count], axis=0)
        coupled = jnp.einsum(
            "cjgrm,gcjkm->cgrk",
            picked,
            local_coupling[:, start : start + count],
            preferred_element_type=f32,
        )
        carried = jnp.einsum(
            "cgrm,ckm->cgrk",
            jnp.repeat(parent, 2, axis=0),
            transfer[start : start + count],
            preferred_element_type=f32,
        )
        parent = (coupled + carried).astype(bf16)
    far = jnp.einsum("lgrk,lqk->grlq", parent, leaf_basis, preferred_element_type=f32)
    spread = value_wide.reshape(3, operators, rhs_count, leaves, leaf_size)
    spread = jnp.transpose(spread, (1, 2, 0, 3, 4)).reshape(
        operators, rhs_count, 3 * leaves, leaf_size
    )
    picked_cells = jnp.take(spread, near_source, axis=2)
    near = jnp.einsum("grljq,gljpq->grlp", picked_cells, near_field, preferred_element_type=f32)
    return (far + near).reshape(operators, rhs_count, width)


def solution(mesh):
    in_specs = (
        P(None, None, ("branch", "leaf")),
        P(("branch", "leaf"), None, None),
        P(("branch", "leaf"), None, None),
        P(None, ("branch", "leaf"), None, None, None),
        P(("branch", "leaf"), None),
        P(None, ("branch", "leaf"), None, None, None),
        P(("branch", "leaf"), None),
        P("branch", None, None, None),
        P(None, "branch", None, None, None),
        P(None, "branch", None, None, None),
    )
    out_specs = P(None, None, ("branch", "leaf"))
    return jax.shard_map(
        per_device, mesh=mesh, in_specs=in_specs, out_specs=out_specs, check_vma=False
    )
```

profile of v0, /device:TPU:1, one launch (start us, length us, event | category | flops | bytes accessed | tf_op | source)
XLA Modules:
  0.0 110.4 jit_solution(4463310574692463625)
XLA Ops:
  0.0 1.0 reshape.160
  1.0 1.0 convolution_convert_fusion
  2.1 1.1 fusion.46
  3.2 1.0 fusion.54
  4.2 4.0 %collective-permute-start = (bf16[1,14,2,16,64]{4,3,2,1,0:T(8,128)(2,1)S(1)}, bf16[1,14,2,16,64]{4,3,2,1,0:T(8,128)(2,1)}, u32[]{:S(2)}, u32[]{:S(2)}) collective-permute-start(bf16[1,14,2,16,64]{4,3,2,1,0:T(8,128)(2,1)S(1)} %maximum_bitcast_fusion.1), channel_id=1, source_target_pairs={{0,1},{1,2},{2,3},{3,4},{4,5},{5,6},{6,7},{7,8},{8,9},{9,10},{10,1... | collective-permute-start | bytes 172040 | tf_op jit(solution)/shard_map/ppermute | solution.py:17
  8.2 9.0 %collective-permute-start.1 = (bf16[1,14,2,16,64]{4,3,2,1,0:T(8,128)(2,1)S(1)}, bf16[1,14,2,16,64]{4,3,2,1,0:T(8,128)(2,1)}, u32[]{:S(2)}, u32[]{:S(2)}) collective-permute-start(bf16[1,14,2,16,64]{4,3,2,1,0:T(8,128)(2,1)S(1)} %maximum_bitcast_fusion.1), channel_id=1, source_target_pairs={{1,0},{2,1},{3,2},{4,3},{5,4},{6,5},{7,6},{8,7},{9,8},{10,9},{11,1... | collective-permute-start | bytes 172040 | tf_op jit(solution)/shard_map/ppermute | solution.py:19
  17.2 1.9 %collective-permute-start.7 = (bf16[1,2,16,512]{3,2,1,0:T(8,128)(2,1)}, bf16[1,2,16,512]{3,2,1,0:T(8,128)(2,1)S(1)}, u32[]{:S(2)}, u32[]{:S(2)}) collective-permute-start(bf16[1,2,16,512]{3,2,1,0:T(8,128)(2,1)} %bitcast.235), channel_id=1, source_target_pairs={{0,1},{1,2},{2,3},{3,4},{4,5},{5,6},{6,7},{7,8},{8,9},{9,10},{10,1... | collective-permute-start | bytes 98312 | tf_op jit(solution)/shard_map/ppermute | solution.py:17
  19.1 7.0 %collective-permute-start.8 = (bf16[1,2,16,512]{3,2,1,0:T(8,128)(2,1)}, bf16[1,2,16,512]{3,2,1,0:T(8,128)(2,1)S(1)}, u32[]{:S(2)}, u32[]{:S(2)}) collective-permute-start(bf16[1,2,16,512]{3,2,1,0:T(8,128)(2,1)} %bitcast.236), channel_id=1, source_target_pairs={{1,0},{2,1},{3,2},{4,3},{5,4},{6,5},{7,6},{8,7},{9,8},{10,9},{11,1... | collective-permute-start | bytes 98312 | tf_op jit(solution)/shard_map/ppermute | solution.py:19
  26.1 0.9 convolution_bitcast_fusion.1
  27.0 0.1 collective-permute-start.2
  27.1 0.7 compare_select_fusion.3
  27.8 1.3 %compare_and_fusion.3 = pred[2,12]{1,0:T(4,128)(4,1)} fusion(s32[14,12]{1,0:T(8,128)} %param.14), kind=kLoop, calls=%fused_computation.182 | loop fusion | flops 144 | bytes 120 | tf_op jit(solution)/shard_map/jit(_take)/and | solution.py:120
  29.1 0.7 compare_select_fusion.2
  29.7 1.3 %compare_and_fusion.4 = pred[4,12]{1,0:T(4,128)(4,1)} fusion(s32[14,12]{1,0:T(8,128)} %param.14), kind=kLoop, calls=%fused_computation.183 | loop fusion | flops 288 | bytes 240 | tf_op jit(solution)/shard_map/jit(_take)/and | solution.py:120
  31.0 0.7 compare_select_fusion
  31.7 1.3 %compare_and_fusion = (pred[8,12]{1,0:T(8,128)(4,1)}, pred[8,12]{1,0:T(8,128)(4,1)}) fusion(s32[8,12]{1,0:T(8,128)} %param.16, s32[14,12]{1,0:T(8,128)} %param.14), kind=kLoop, calls=%fused_computation.154 | loop fusion | flops 1152 | bytes 960 | tf_op jit(solution)/shard_map/jit(_take)/and | solution.py:139
  33.0 0.6 pad_clamp_fusion.1
  33.7 0.6 pad_clamp_fusion.2
  34.4 0.6 pad_clamp_fusion.3
  35.1 0.6 pad_clamp_fusion.4
  35.8 0.6 pad_clamp_fusion
  36.4 0.8 fusion.110
  37.2 0.6 compare_and_fusion.2
  37.8 0.9 concatenate.19
  38.7 0.8 fusion.20
  39.5 0.8 fusion.106
  40.4 3.2 %collective-permute-done.3 = bf16[2,16,64]{2,1,0:T(8,128)(2,1)S(1)} collective-permute-done((bf16[2,16,64]{2,1,0:T(8,128)(2,1)S(1)}, bf16[2,16,64]{2,1,0:T(8,128)(2,1)S(1)}, u32[]{:S(2)}, u32[]{:S(2)}) %collective-permute-start.3) | collective-permute-done | bytes 4128 | tf_op jit(solution)/shard_map/ppermute | solution.py:27
  43.5 0.8 fusion.22
  44.4 0.8 fusion.102
  45.2 1.7 %collective-permute-done.4 = bf16[2,16,64]{2,1,0:T(8,128)(2,1)S(1)} collective-permute-done((bf16[2,16,64]{2,1,0:T(8,128)(2,1)S(1)}, bf16[2,16,64]{2,1,0:T(8,128)(2,1)S(1)}, u32[]{:S(2)}, u32[]{:S(2)}) %collective-permute-start.4) | collective-permute-done | bytes 4128 | tf_op jit(solution)/shard_map/ppermute | solution.py:27
  46.9 0.8 fusion.24
  47.7 0.8 fusion.98
  48.5 2.6 %collective-permute-done.5 = bf16[2,16,64]{2,1,0:T(8,128)(2,1)S(1)} collective-permute-done((bf16[2,16,64]{2,1,0:T(8,128)(2,1)S(1)}, bf16[2,16,64]{2,1,0:T(8,128)(2,1)S(1)}, u32[]{:S(2)}, u32[]{:S(2)}) %collective-permute-start.5) | collective-permute-done | bytes 4128 | tf_op jit(solution)/shard_map/ppermute | solution.py:27
  51.1 0.8 fusion.26
  52.0 3.1 %collective-permute-start.6 = (bf16[2,16,64]{2,1,0:T(8,128)(2,1)S(1)}, bf16[2,16,64]{2,1,0:T(8,128)(2,1)S(1)}, u32[]{:S(2)}, u32[]{:S(2)}) collective-permute-start(bf16[2,16,64]{2,1,0:T(8,128)(2,1)S(1)} %fusion.26), channel_id=1, source_target_pairs={{0,16},{1,17},{2,18},{3,19},{4,20},{5,21},{6,22},{7,23},{8,24},{9,... | collective-permute-start | bytes 12296 | tf_op jit(solution)/shard_map/ppermute | solution.py:27
  55.0 0.8 fusion.94
  55.9 2.5 %collective-permute-done.6 = bf16[2,16,64]{2,1,0:T(8,128)(2,1)S(1)} collective-permute-done((bf16[2,16,64]{2,1,0:T(8,128)(2,1)S(1)}, bf16[2,16,64]{2,1,0:T(8,128)(2,1)S(1)}, u32[]{:S(2)}, u32[]{:S(2)}) %collective-permute-start.6) | collective-permute-done | bytes 4128 | tf_op jit(solution)/shard_map/ppermute | solution.py:27
  58.4 0.8 fusion.28
  59.2 18.3 %all-gather = bf16[16,16,64]{2,1,0:T(8,128)(2,1)S(1)} all-gather(bf16[2,16,64]{2,1,0:T(8,128)(2,1)S(1)} %fusion.28), channel_id=2, replica_groups=mesh['branch'=8,'leaf'=32] {'branch'}, dimensions={0}, use_global_device_ids=true | all-gather | bytes 36864 | tf_op jit(solution)/shard_map/all_gather | solution.py:96
  77.5 0.7 gather_fusion.3
  78.2 1.2 %fusion.30 = f32[2,16,64]{2,1,0:T(8,128)S(1)} fusion(bf16[7,2,16,64]{3,2,1,0:T(8,128)(2,1)S(1)} %gather_fusion.3, pred[7]{0:T(512)(128)(4,1)} %compare_and_fusion.2, bf16[1,62,64,64]{3,2,1,0:T(8,128)(2,1)} %param.17, s32[]{:T(128)S(6)} %select_n.129, bf16[2,1,7,64,64]{4,3,2,1,0:T(8,128)(2,1)} %param.19), kind=kOutput, calls=%fused_computation.47 | convolution fusion | flops 2113536 | bytes 283140 | tf_op jit(solution)/shard_map/grm,km->grk/dot_general | solution.py:109
  79.4 1.1 fusion.31
  80.5 1.0 fusion.32
  81.5 1.0 fusion.33
  82.5 1.0 fusion.34
  83.6 0.9 fusion.19
  84.5 0.1 concatenate.18
  84.6 0.1 concatenate.20
  84.8 1.7 %gather_fusion.4 = bf16[96,2,16,64]{3,2,1,0:T(8,128)(2,1)} fusion(bf16[2,16,24,64]{3,1,2,0:T(8,128)(2,1)S(1)} %copy.57, s32[1024]{0:T(1024)} %pad_clamp_fusion), kind=kCustom, calls=%fused_computation.4 | custom fusion | bytes 786816 | tf_op jit(solution)/shard_map/jit(_take)/gather | solution.py:139
  86.6 2.8 %fusion.7 = f32[2,16,8,64]{3,1,0,2:T(8,128)} fusion(bf16[2,8,12,64,64]{4,3,2,1,0:T(8,128)(2,1)S(1)} %copy-done, bf16[8,12,2,16,64]{4,3,2,1,0:T(8,128)(2,1)} %bitcast.226, pred[8,12]{1,0:T(8,128)(4,1)S(1)} %copy-done.4), kind=kOutput, calls=%fused_computation.14 | convolution fusion | flops 25362432 | bytes 2031712 | tf_op jit(solution)/shard_map/grljq,gljpq->grlp/dot_general | solution.py:140
  89.4 1.0 pad_maximum_fusion
  90.4 0.8 pad_maximum_fusion.2
  91.2 1.4 %gather_fusion.2 = bf16[24,2,16,64]{3,2,1,0:T(8,128)(2,1)} fusion(bf16[6,2,16,64]{3,2,1,0:T(8,128)(2,1)S(1)} %bitcast.227, s32[1024]{0:T(1024)} %pad_clamp_fusion.2), kind=kCustom, calls=%fused_computation.2 | custom fusion | bytes 196704 | tf_op jit(solution)/shard_map/jit(_take)/gather | solution.py:120
  92.6 1.6 %convolution_bitcast_fusion.2 = f32[2,2,16,64]{3,2,1,0:T(8,128)S(1)} fusion(bf16[2,14,12,64,64]{4,3,2,1,0:T(8,128)(2,1)} %param.13, bf16[2,12,2,16,64]{4,3,2,1,0:T(8,128)(2,1)} %bitcast.234, pred[2,12]{1,0:T(4,128)(4,1)S(1)} %copy-done.5), kind=kOutput, calls=%fused_computation.23 | convolution fusion | flops 6340608 | bytes 999448 | tf_op jit(solution)/shard_map/cjgrm,gcjkm->cgrk/dot_general | solution.py:121
  94.2 1.5 %fusion.18 = bf16[2,2,16,64]{3,2,1,0:T(8,128)(2,1)} fusion(f32[2,2,16,64]{3,2,1,0:T(8,128)S(1)} %convolution_bitcast_fusion.2, bf16[14,64,64]{2,1,0:T(8,128)(2,1)} %param.12, bf16[2,16,64]{2,1,0:T(8,128)(2,1)S(1)} %fusion.19), kind=kOutput, calls=%fused_computation.24 | convolution fusion | flops 532480 | bytes 61440 | tf_op jit(solution)/shard_map/cgrm,ckm->cgrk/dot_general | solution.py:127
  95.7 0.8 pad_maximum_fusion.1
  96.5 1.5 %gather_fusion.1 = bf16[48,2,16,64]{3,2,1,0:T(8,128)(2,1)} fusion(bf16[12,2,16,64]{3,2,1,0:T(8,128)(2,1)S(1)} %bitcast.225, s32[1024]{0:T(1024)} %pad_clamp_fusion.3), kind=kCustom, calls=%fused_computation.1 | custom fusion | bytes 393408 | tf_op jit(solution)/shard_map/jit(_take)/gather | solution.py:120
  98.0 2.1 %fusion.14 = f32[4,2,16,64]{3,2,1,0:T(8,128)S(1)} fusion(bf16[2,14,12,64,64]{4,3,2,1,0:T(8,128)(2,1)} %param.13, bf16[4,12,2,16,64]{4,3,2,1,0:T(8,128)(2,1)} %bitcast.230, pred[4,12]{1,0:T(4,128)(4,1)} %compare_and_fusion.4), kind=kOutput, calls=%fused_computation.18 | convolution fusion | flops 12681216 | bytes 1999360 | tf_op jit(solution)/shard_map/cjgrm,gcjkm->cgrk/dot_general | solution.py:121
  100.1 1.0 fusion.17
  101.1 1.7 %gather_fusion = bf16[96,2,16,64]{3,2,1,0:T(8,128)(2,1)} fusion(bf16[24,2,16,64]{3,2,1,0:T(8,128)(2,1)S(1)} %bitcast.224, s32[1024]{0:T(1024)} %pad_clamp_fusion.4), kind=kCustom, calls=%fused_computation | custom fusion | bytes 786816 | tf_op jit(solution)/shard_map/jit(_take)/gather | solution.py:120
  102.8 3.8 %fusion.10 = f32[8,2,16,64]{3,2,1,0:T(8,128)} fusion(bf16[2,14,12,64,64]{4,3,2,1,0:T(8,128)(2,1)} %param.13, bf16[8,12,2,16,64]{4,3,2,1,0:T(8,128)(2,1)} %bitcast.228, pred[8,12]{1,0:T(8,128)(4,1)S(1)} %copy-done.3), kind=kOutput, calls=%fused_computation.15 | convolution fusion | flops 25362432 | bytes 3997792 | tf_op jit(solution)/shard_map/cjgrm,gcjkm->cgrk/dot_general | solution.py:121
  106.7 2.0 %fusion.6 = f32[2,16,8,64]{3,1,0,2:T(8,128)} fusion(f32[2,16,8,64]{3,1,0,2:T(8,128)} %fusion.7, f32[8,2,16,64]{3,2,1,0:T(8,128)} %fusion.10, bf16[8,2,16,64]{3,2,1,0:T(8,128)(2,1)S(1)} %bitcast.232, bf16[8,64,64]{2,1,0:T(8,128)(2,1)} %param.11, bf16[14,64,64]{2,1,0:T(8,128)(2,1)S(1)} %copy-done.1), kind=kOutput, calls=%fused_computation.12 | convolution fusion | flops 4243456 | bytes 458752 | tf_op jit(solution)/shard_map/lgrk,lqk->grlq/dot_general | solution.py:134
  108.7 1.0 copy.60
  109.7 0.7 reshape.171
  (34 shorter events, 0.6 us)
Async XLA Ops:
  0.0 86.6 %copy-start = (bf16[2,8,12,64,64]{4,3,2,1,0:T(8,128)(2,1)S(1)}, bf16[2,8,12,64,64]{4,3,2,1,0:T(8,128)(2,1)}, u32[]{:S(2)}) copy-start(bf16[2,8,12,64,64]{4,3,2,1,0:T(8,128)(2,1)} %param.15) | copy-start | bytes 4718596
  4.2 85.2 %collective-permute-start = (bf16[1,14,2,16,64]{4,3,2,1,0:T(8,128)(2,1)S(1)}, bf16[1,14,2,16,64]{4,3,2,1,0:T(8,128)(2,1)}, u32[]{:S(2)}, u32[]{:S(2)}) collective-permute-start(bf16[1,14,2,16,64]{4,3,2,1,0:T(8,128)(2,1)S(1)} %maximum_bitcast_fusion.1), channel_id=1, source_target_pairs={{0,1},{1,2},{2,3},{3,4},{4,5},{5,6},{6,7},{7,8},{8,9},{9,10},{10,1... | collective-permute-start | bytes 172040 | tf_op jit(solution)/shard_map/ppermute | solution.py:17
  8.2 81.2 %collective-permute-start.1 = (bf16[1,14,2,16,64]{4,3,2,1,0:T(8,128)(2,1)S(1)}, bf16[1,14,2,16,64]{4,3,2,1,0:T(8,128)(2,1)}, u32[]{:S(2)}, u32[]{:S(2)}) collective-permute-start(bf16[1,14,2,16,64]{4,3,2,1,0:T(8,128)(2,1)S(1)} %maximum_bitcast_fusion.1), channel_id=1, source_target_pairs={{1,0},{2,1},{3,2},{4,3},{5,4},{6,5},{7,6},{8,7},{9,8},{10,9},{11,1... | collective-permute-start | bytes 172040 | tf_op jit(solution)/shard_map/ppermute | solution.py:19
  17.2 67.3 %collective-permute-start.7 = (bf16[1,2,16,512]{3,2,1,0:T(8,128)(2,1)}, bf16[1,2,16,512]{3,2,1,0:T(8,128)(2,1)S(1)}, u32[]{:S(2)}, u32[]{:S(2)}) collective-permute-start(bf16[1,2,16,512]{3,2,1,0:T(8,128)(2,1)} %bitcast.235), channel_id=1, source_target_pairs={{0,1},{1,2},{2,3},{3,4},{4,5},{5,6},{6,7},{7,8},{8,9},{9,10},{10,1... | collective-permute-start | bytes 98312 | tf_op jit(solution)/shard_map/ppermute | solution.py:17
  19.1 65.5 %collective-permute-start.8 = (bf16[1,2,16,512]{3,2,1,0:T(8,128)(2,1)}, bf16[1,2,16,512]{3,2,1,0:T(8,128)(2,1)S(1)}, u32[]{:S(2)}, u32[]{:S(2)}) collective-permute-start(bf16[1,2,16,512]{3,2,1,0:T(8,128)(2,1)} %bitcast.236), channel_id=1, source_target_pairs={{1,0},{2,1},{3,2},{4,3},{5,4},{6,5},{7,6},{8,7},{9,8},{10,9},{11,1... | collective-permute-start | bytes 98312 | tf_op jit(solution)/shard_map/ppermute | solution.py:19
  27.0 11.7 %collective-permute-start.2 = (bf16[2,16,64]{2,1,0:T(8,128)(2,1)S(1)}, bf16[2,16,64]{2,1,0:T(8,128)(2,1)S(1)}, u32[]{:S(2)}, u32[]{:S(2)}) collective-permute-start(bf16[2,16,64]{2,1,0:T(8,128)(2,1)S(1)} %fusion.127), channel_id=1, source_target_pairs={{0,1},{1,0},{2,3},{3,2},{4,5},{5,4},{6,7},{7,6},{8,9},{9,8},{10,11... | collective-permute-start | bytes 12296 | tf_op jit(solution)/shard_map/ppermute | solution.py:27
  39.5 4.0 %collective-permute-start.3 = (bf16[2,16,64]{2,1,0:T(8,128)(2,1)S(1)}, bf16[2,16,64]{2,1,0:T(8,128)(2,1)S(1)}, u32[]{:S(2)}, u32[]{:S(2)}) collective-permute-start(bf16[2,16,64]{2,1,0:T(8,128)(2,1)S(1)} %fusion.20), channel_id=1, source_target_pairs={{0,2},{1,3},{2,0},{3,1},{4,6},{5,7},{6,4},{7,5},{8,10},{9,11},{10,... | collective-permute-start | bytes 12296 | tf_op jit(solution)/shard_map/ppermute | solution.py:27
  44.4 2.5 %collective-permute-start.4 = (bf16[2,16,64]{2,1,0:T(8,128)(2,1)S(1)}, bf16[2,16,64]{2,1,0:T(8,128)(2,1)S(1)}, u32[]{:S(2)}, u32[]{:S(2)}) collective-permute-start(bf16[2,16,64]{2,1,0:T(8,128)(2,1)S(1)} %fusion.22), channel_id=1, source_target_pairs={{0,4},{1,5},{2,6},{3,7},{4,0},{5,1},{6,2},{7,3},{8,12},{9,13},{10,... | collective-permute-start | bytes 12296 | tf_op jit(solution)/shard_map/ppermute | solution.py:27
  47.7 3.4 %collective-permute-start.5 = (bf16[2,16,64]{2,1,0:T(8,128)(2,1)S(1)}, bf16[2,16,64]{2,1,0:T(8,128)(2,1)S(1)}, u32[]{:S(2)}, u32[]{:S(2)}) collective-permute-start(bf16[2,16,64]{2,1,0:T(8,128)(2,1)S(1)} %fusion.24), channel_id=1, source_target_pairs={{0,8},{1,9},{2,10},{3,11},{4,12},{5,13},{6,14},{7,15},{8,0},{9,1},... | collective-permute-start | bytes 12296 | tf_op jit(solution)/shard_map/ppermute | solution.py:27
  52.0 6.4 %collective-permute-start.6 = (bf16[2,16,64]{2,1,0:T(8,128)(2,1)S(1)}, bf16[2,16,64]{2,1,0:T(8,128)(2,1)S(1)}, u32[]{:S(2)}, u32[]{:S(2)}) collective-permute-start(bf16[2,16,64]{2,1,0:T(8,128)(2,1)S(1)} %fusion.26), channel_id=1, source_target_pairs={{0,16},{1,17},{2,18},{3,19},{4,20},{5,21},{6,22},{7,23},{8,24},{9,... | collective-permute-start | bytes 12296 | tf_op jit(solution)/shard_map/ppermute | solution.py:27
  80.5 6.1 %copy-start.4 = (pred[8,12]{1,0:T(8,128)(4,1)S(1)}, pred[8,12]{1,0:T(8,128)(4,1)}, u32[]{:S(2)}) copy-start(pred[8,12]{1,0:T(8,128)(4,1)} %get-tuple-element.7) | copy-start | bytes 292
  86.6 6.0 %copy-start.5 = (pred[2,12]{1,0:T(4,128)(4,1)S(1)}, pred[2,12]{1,0:T(4,128)(4,1)}, u32[]{:S(2)}) copy-start(pred[2,12]{1,0:T(4,128)(4,1)} %compare_and_fusion.3) | copy-start | bytes 76
  96.5 3.6 %copy-start.2 = (bf16[2,2,16,64]{3,2,1,0:T(8,128)(2,1)S(1)}, bf16[2,2,16,64]{3,2,1,0:T(8,128)(2,1)}, u32[]{:S(2)}) copy-start(bf16[2,2,16,64]{3,2,1,0:T(8,128)(2,1)} %fusion.18) | copy-start | bytes 24580
  96.5 6.4 %copy-start.3 = (pred[8,12]{1,0:T(8,128)(4,1)S(1)}, pred[8,12]{1,0:T(8,128)(4,1)}, u32[]{:S(2)}) copy-start(pred[8,12]{1,0:T(8,128)(4,1)} %get-tuple-element.8) | copy-start | bytes 292
  102.8 3.9 %copy-start.1 = (bf16[14,64,64]{2,1,0:T(8,128)(2,1)S(1)}, bf16[14,64,64]{2,1,0:T(8,128)(2,1)}, u32[]{:S(2)}) copy-start(bf16[14,64,64]{2,1,0:T(8,128)(2,1)} %param.12) | copy-start | bytes 344068
where the time goes:
time: 112 us; the launch traced here: 110 us
  matrix products  33.5 us (30%)
  starting transfers between devices  25 us (22%)
  blocking collectives  18.3 us (16%)
  other arithmetic  12.2 us (11%)
  local copies, waits for them, and re-layouts  11.2 us (10%)
  waiting for transfers between devices  9.89 us (9%)
    all_gather x1, blocking collectives, per_device(): subtree_roots = lax.all_gather(current[None], 'branch', axis=0, tiled=True)  18.3 us
    ppermute x2, starting transfers between devices, with_halo(): lax.ppermute(head, axis, [((i + 1) % count, i) for i in range(ends)])  16 us
    ppermute x5, waiting for transfers between devices, swapped(): lax.ppermute(shard, axis, [(i, i ^ 1 << distance) for i in range(lax.axis...  9.88 us
    dot_general x3, matrix products, per_device(): jnp.einsum('cjgrm,gcjkm->cgrk', picked, local_coupling[:, start:start + c...  7.56 us
    ppermute x2, starting transfers between devices, with_halo(): lax.ppermute(tail, axis, [(i, (i + 1) % count) for i in range(ends)])  5.87 us
    dot_general x5, matrix products, per_device(): jnp.einsum('grm,km->grk', down, pick_row(upward, owner), preferred_elemen...  5.39 us
    gather x3, local copies, waits for them, and re-layouts, per_device(): picked = jnp.take(window_rows, coupling_source[start:start + count], axis=0)  4.58 us
    dot_general x5, matrix products, per_device(): jnp.einsum('grk,km->grm', other, pick_row(upward, jnp.bitwise_xor(owner,...  4.21 us
  transfers between devices with their start and end apart: 9, of which 4 were waited for; matrix products, arithmetic and copies ran while one was open for 29% of the time, Pallas kernels for 0%

commit v1 on v0

v1 whole, which is shorter than its diff:
```python
import functools

import jax
import jax.numpy as jnp
from jax import lax
from jax.experimental import pallas as pl
from jax.experimental.pallas import tpu as pltpu
from jax.sharding import PartitionSpec as P

f32 = jnp.float32
bf16 = jnp.bfloat16
R = 64
RHS = 16
LEAVES = 8
LOCAL = 14
ROWS = 22
DEPTH = 5
N_LEAF = 32
N_BRANCH = 8
LINKS = 12
ANY = pl.BlockSpec(memory_space=pl.ANY)
VMEM = pl.BlockSpec(memory_space=pltpu.VMEM)
SMEM = pl.BlockSpec(memory_space=pltpu.SMEM)


def dot(a, b):
    return jnp.dot(a, b, preferred_element_type=f32)


def dot_nt(a, b):
    return lax.dot_general(a, b, (((1,), (1,)), ((), ())), preferred_element_type=f32)


def turned(v):
    return jnp.concatenate([v[:, R:], v[:, :R]], axis=1)


def packed(c):
    return jnp.concatenate([c[:RHS], c[RHS:]], axis=1)


def upper_index(leaf, step):
    return 2 * N_LEAF - 2 * (N_LEAF >> step) + jnp.right_shift(leaf, step)


def up_kernel(values, basis, transfer, upper, rows, chain, fan, vals, bas, tra, upp, sem):
    leaf = lax.axis_index("leaf")
    copies = [
        pltpu.make_async_copy(values, vals, sem.at[0]),
        pltpu.make_async_copy(basis, bas, sem.at[1]),
        pltpu.make_async_copy(transfer, tra, sem.at[2]),
    ]
    for step in range(DEPTH):
        copies.append(
            pltpu.make_async_copy(
                upper.at[0, upper_index(leaf, step)], upp.at[step], sem.at[3 + step]
            )
        )
    for copy in copies:
        copy.start()
    copies[0].wait()
    left = lax.broadcasted_iota(jnp.int32, (RHS, 2 * R), 1) < R
    cells = []
    for pair in range(LEAVES // 2):
        x0 = vals[0, :, pl.ds(pair * 2 * R, 2 * R)]
        x1 = vals[1, :, pl.ds(pair * 2 * R, 2 * R)]
        y0, y1 = turned(x0), turned(x1)
        rows[2 * pair] = jnp.where(left, x0, y1)
        rows[2 * pair + 1] = jnp.where(left, y0, x1)
        cells.append(jnp.concatenate([x0[:, :R], x1[:, :R]], axis=0))
        cells.append(jnp.concatenate([y0[:, :R], y1[:, :R]], axis=0))
    copies[1].wait()
    coefs = [dot(cells[i], bas[i]).astype(bf16) for i in range(LEAVES)]
    copies[2].wait()
    begin, place = 0, LEAVES
    while len(coefs) > 1:
        for i, c in enumerate(coefs):
            rows[place + i] = packed(c)
        place += len(coefs)
        merged = [
            (
                dot(coefs[i], tra[begin + i]) + dot(coefs[i + 1], tra[begin + i + 1])
            ).astype(bf16)
            for i in range(0, len(coefs), 2)
        ]
        begin += len(coefs)
        coefs = merged
    coef = coefs[0]
    for step in range(DEPTH):
        chain[step] = packed(coef)
        copies[3 + step].wait()
        coef = dot(coef, upp[step]).astype(bf16)
    top = packed(coef)
    for b in range(N_BRANCH):
        fan[b] = top


def up_call(values, basis, transfer, upper):
    return pl.pallas_call(
        up_kernel,
        out_shape=[
            jax.ShapeDtypeStruct((ROWS, RHS, 2 * R), bf16),
            jax.ShapeDtypeStruct((DEPTH, RHS, 2 * R), bf16),
            jax.ShapeDtypeStruct((N_BRANCH, RHS, 2 * R), bf16),
        ],
        in_specs=[ANY] * 4,
        out_specs=[VMEM] * 3,
        scratch_shapes=[
            pltpu.VMEM((2, RHS, LEAVES * R), bf16),
            pltpu.VMEM((LEAVES, R, R), bf16),
            pltpu.VMEM((LOCAL, R, R), bf16),
            pltpu.VMEM((DEPTH, R, R), bf16),
            pltpu.SemaphoreType.DMA((3 + DEPTH,)),
        ],
        compiler_params=pltpu.CompilerParams(vmem_limit_bytes=56 * 2**20),
        name="up",
    )(values, basis, transfer, upper)


def prep_kernel(upper, couple, top, basis, transfer, over, fold, leafs, upp, cou, tops, sem):
    leaf = lax.axis_index("leaf")
    copies = []
    for step in range(DEPTH):
        index = upper_index(leaf, step)
        copies.append(pltpu.make_async_copy(upper.at[0, index], upp.at[step], sem.at[step]))
        copies.append(
            pltpu.make_async_copy(couple.at[:, 0, index], cou.at[step], sem.at[DEPTH + step])
        )
    last = pltpu.make_async_copy(top, tops, sem.at[2 * DEPTH])
    for copy in copies:
        copy.start()
    last.start()
    zero = jnp.zeros((R, R), bf16)
    tops2 = [transfer[12 + t] for t in range(2)]
    tops1 = [dot(transfer[8 + t], tops2[t // 2]).astype(bf16) for t in range(4)]
    tops0 = [dot(transfer[t], tops1[t // 2]).astype(bf16) for t in range(8)]
    for t in range(LEAVES):
        full = dot(basis[t], tops0[t]).astype(bf16)
        leafs[pl.ds(t * R, R), :] = jnp.concatenate([full, zero], axis=1)
        leafs[pl.ds((LEAVES + t) * R, R), :] = jnp.concatenate([zero, full], axis=1)
    for copy in copies:
        copy.wait()
    down = None
    for step in range(DEPTH + 1):
        lanes = pl.ds(step * 2 * R, 2 * R)
        for g in range(2):
            if step == DEPTH:
                mat = down
            elif step == 0:
                mat = cou[step, g]
            else:
                mat = dot(down, cou[step, g]).astype(bf16)
            pair = [mat, zero] if g == 0 else [zero, mat]
            fold[pl.ds(g * R, R), lanes] = jnp.concatenate(pair, axis=1)
        if step < DEPTH:
            down = upp[0] if step == 0 else dot(down, upp[step]).astype(bf16)
    last.wait()
    for i in range(N_BRANCH - 1):
        lanes = pl.ds(i * 2 * R, 2 * R)
        over[pl.ds(0, R), lanes] = jnp.concatenate([tops[0, 0, i], zero], axis=1)
        over[pl.ds(R, R), lanes] = jnp.concatenate([zero, tops[1, 0, i]], axis=1)


def prep_call(upper, couple, top, basis, transfer):
    return pl.pallas_call(
        prep_kernel,
        out_shape=[
            jax.ShapeDtypeStruct((2 * R, (N_BRANCH - 1) * 2 * R), bf16),
            jax.ShapeDtypeStruct((2 * R, (DEPTH + 1) * 2 * R), bf16),
            jax.ShapeDtypeStruct((2 * LEAVES * R, 2 * R), bf16),
        ],
        in_specs=[ANY] * 3 + [VMEM] * 2,
        out_specs=[VMEM] * 3,
        scratch_shapes=[
            pltpu.VMEM((DEPTH, R, R), bf16),
            pltpu.VMEM((DEPTH, 2, R, R), bf16),
            pltpu.VMEM((2, 1, N_BRANCH - 1, R, R), bf16),
            pltpu.SemaphoreType.DMA((2 * DEPTH + 1,)),
        ],
        compiler_params=pltpu.CompilerParams(vmem_limit_bytes=8 * 2**20),
        cost_estimate=pl.CostEstimate(
            flops=10**8, bytes_accessed=4 * 10**6, transcendentals=0
        ),
        name="prep",
    )(upper, couple, top, basis, transfer)


def mid_kernel(roots, over, chain, out):
    leaf = lax.axis_index("leaf")
    branch = lax.axis_index("branch")
    others = [roots[(branch + 1 + i) % N_BRANCH] for i in range(N_BRANCH - 1)]
    part = dot_nt(jnp.concatenate(others, axis=1), over[...]).astype(bf16)
    for i in range(N_LEAF):
        to = jnp.bitwise_xor(leaf, i)
        out[to, 0] = chain[max(i.bit_length() - 1, 0)]
        out[to, 1] = part


def mid_call(roots, over, chain):
    return pl.pallas_call(
        mid_kernel,
        out_shape=jax.ShapeDtypeStruct((N_LEAF, 2, RHS, 2 * R), bf16),
        in_specs=[VMEM] * 3,
        out_specs=VMEM,
        compiler_params=pltpu.CompilerParams(vmem_limit_bytes=8 * 2**20),
        name="mid",
    )(roots, over, chain)


def local_kernel(
    own, before, after, coupling_source, near_source, coupling, near, transfer, basis,
    base, wide, sums, cells,
):
    left = lax.broadcasted_iota(jnp.int32, (RHS, 2 * R), 1) < R
    for part, ref in enumerate((before, own, after)):
        for row in range(ROWS):
            v = ref[row]
            s = turned(v)
            wide[0, part * ROWS + row] = jnp.where(left, v, s)
            wide[1, part * ROWS + row] = jnp.where(left, s, v)

    def block(picked, mats):
        result = []
        for g in range(2):
            acc = jnp.zeros((RHS, R), f32)
            for j in range(0, LINKS, 4):
                v = jnp.concatenate(
                    [
                        jnp.where(left, wide[g, picked[j]], wide[g, picked[j + 1]]),
                        jnp.where(left, wide[g, picked[j + 2]], wide[g, picked[j + 3]]),
                    ],
                    axis=1,
                )
                m = jnp.concatenate([mats(g, j + n) for n in range(4)], axis=1)
                acc += dot_nt(v, m)
            result.append(acc)
        return jnp.concatenate(result, axis=0)

    def near_body(t, carry):
        picked = []
        for j in range(LINKS):
            s = near_source[t, j]
            picked.append(jnp.right_shift(s, 3) * ROWS + jnp.bitwise_and(s, 7))
        cells[t] = block(picked, lambda g, j: near[g, t, j])
        return carry

    lax.fori_loop(0, LEAVES, near_body, 0)

    def far_body(log, start, t, carry):
        r = start + t
        picked = []
        for j in range(LINKS):
            s = coupling_source[r, j]
            picked.append(
                jnp.right_shift(s, log) * ROWS
                + LEAVES
                + start
                + jnp.bitwise_and(s, (1 << log) - 1)
            )
        sums[r] = block(picked, lambda g, j: coupling[g, r, j])
        return carry

    for log, start in ((1, 12), (2, 8), (3, 0)):
        lax.fori_loop(0, 1 << log, functools.partial(far_body, log, start), 0)
    up2 = [sums[12 + t].astype(bf16) for t in range(2)]
    up1 = [
        (sums[8 + t] + dot_nt(up2[t // 2], transfer[8 + t])).astype(bf16) for t in range(4)
    ]
    up0 = [(sums[t] + dot_nt(up1[t // 2], transfer[t])).astype(bf16) for t in range(8)]
    full = [cells[t] + dot_nt(up0[t], basis[t]) for t in range(8)]
    for pair in range(LEAVES // 2):
        both = jnp.concatenate([full[2 * pair], full[2 * pair + 1]], axis=1)
        for g in range(2):
            base[g, :, pl.ds(pair * 2 * R, 2 * R)] = both[g * RHS : (g + 1) * RHS]


def local_call(own, before, after, coupling_source, near_source, coupling, near, transfer, basis):
    return pl.pallas_call(
        local_kernel,
        out_shape=jax.ShapeDtypeStruct((2, RHS, LEAVES * R), f32),
        in_specs=[VMEM] * 3 + [SMEM] * 2 + [VMEM] * 4,
        out_specs=VMEM,
        scratch_shapes=[
            pltpu.VMEM((2, 3 * ROWS, RHS, 2 * R), bf16),
            pltpu.VMEM((LOCAL, 2 * RHS, R), f32),
            pltpu.VMEM((LEAVES, 2 * RHS, R), f32),
        ],
        compiler_params=pltpu.CompilerParams(vmem_limit_bytes=24 * 2**20),
        cost_estimate=pl.CostEstimate(
            flops=10**8, bytes_accessed=2 * 10**7, transcendentals=0
        ),
        name="local",
    )(own, before, after, coupling_source, near_source, coupling, near, transfer, basis)


def final_kernel(got, fold, leafs, base, out):
    leaf = lax.axis_index("leaf")
    parts = []
    for step in range(DEPTH):
        total = None
        for i in range(1 << step, 2 << step):
            v = got[jnp.bitwise_xor(leaf, i), 0].astype(f32)
            total = v if total is None else total + v
        parts.append(total.astype(bf16))
    total = got[0, 1].astype(f32)
    for i in range(1, N_LEAF):
        total = total + got[i, 1].astype(f32)
    parts.append(total.astype(bf16))
    target = dot_nt(jnp.concatenate(parts, axis=1), fold[...]).astype(bf16)
    far = dot_nt(target, leafs[...])
    width = LEAVES * R
    for g in range(2):
        out[g] = base[g] + far[:, g * width : (g + 1) * width]


def final_call(got, fold, leafs, base):
    return pl.pallas_call(
        final_kernel,
        out_shape=jax.ShapeDtypeStruct((2, RHS, LEAVES * R), f32),
        in_specs=[VMEM] * 4,
        out_specs=VMEM,
        compiler_params=pltpu.CompilerParams(vmem_limit_bytes=8 * 2**20),
        name="final",
    )(got, fold, leafs, base)


def per_device(
    values,
    leaf_basis,
    transfer,
    local_coupling,
    coupling_source,
    near_field,
    near_source,
    upper_transfer,
    upper_coupling,
    top_coupling,
):
    rows, chain, fan = up_call(values, leaf_basis, transfer, upper_transfer)
    roots = lax.all_to_all(fan, "branch", 0, 0, tiled=True)
    last = N_BRANCH * N_LEAF - 1
    ring = ("branch", "leaf")
    before = lax.ppermute(rows, ring, [(i, i + 1) for i in range(last)])
    after = lax.ppermute(rows, ring, [(i + 1, i) for i in range(last)])
    over, fold, leafs = prep_call(
        upper_transfer, upper_coupling, top_coupling, leaf_basis, transfer
    )
    sent = mid_call(roots, over, chain)
    got = lax.all_to_all(sent, "leaf", 0, 0, tiled=True)
    base = local_call(
        rows, before, after, coupling_source, near_source, local_coupling, near_field,
        transfer, leaf_basis,
    )
    return final_call(got, fold, leafs, base)


def solution(mesh):
    in_specs = (
        P(None, None, ("branch", "leaf")),
        P(("branch", "leaf"), None, None),
        P(("branch", "leaf"), None, None),
        P(None, ("branch", "leaf"), None, None, None),
        P(("branch", "leaf"), None),
        P(None, ("branch", "leaf"), None, None, None),
        P(("branch", "leaf"), None),
        P("branch", None, None, None),
        P(None, "branch", None, None, None),
        P(None, "branch", None, None, None),
    )
    out_specs = P(None, None, ("branch", "leaf"))
    return jax.shard_map(
        per_device, mesh=mesh, in_specs=in_specs, out_specs=out_specs, check_vma=False
    )
```

time: 112 us -> 65.7 us (0.59)
  matrix products: 33.5 us -> 0 us
  blocking collectives: 18.3 us -> 0 us
  Pallas kernels: 0 us -> 13.8 us
  other arithmetic: 12.2 us -> 0 us
  local copies, waits for them, and re-layouts: 11.2 us -> 16.8 us
  waiting for transfers between devices: 9.89 us -> 8.26 us
    dot_general x27 -> x0, matrix products: 33.5 us -> none  [the longest x3 7.56 us: per_device(): jnp.einsum('cjgrm,gcjkm->cgrk', picked, local_coupling[:, start:start + c...]
    all_gather x1 -> x0, blocking collectives: 18.3 us -> none  [per_device(): subtree_roots = lax.all_gather(current[None], 'branch', axis=0, tiled=True)]
    all_to_all x0 -> x2, starting transfers between devices: none -> 17.1 us  [the longest x1 10.7 us: per_device(): got = lax.all_to_all(sent, 'leaf', 0, 0, tiled=True)]
    unnamed x12 -> x44, local copies, waits for them, and re-layouts: 0.03 us -> 16.8 us
    ppermute x9 -> x2, starting transfers between devices: 25 us -> 8.85 us  [the longest x1 6.93 us: per_device(): after = lax.ppermute(rows, ring, [(i + 1, i) for i in range(last)])]
    pallas_call x0 -> x5, Pallas kernels: none -> 13.8 us  [the longest x1 6.54 us: local_call(): pl.pallas_call(local_kernel, out_shape=jax.ShapeDtypeStruct((2, RHS, LEAV...]
    gather x5 -> x0, local copies, waits for them, and re-layouts: 7.01 us -> none  [the longest x3 4.58 us: per_device(): picked = jnp.take(window_rows, coupling_source[start:start + count], axis=0)]
    and x4 -> x0, other arithmetic: 4.38 us -> none  [the longest x2 2.53 us: per_device(): picked = jnp.take(window_rows, coupling_source[start:start + count], axis=0)]
  transfers between devices with their start and end apart: 9 -> 4, of which waited for: 4 -> 1; matrix products, arithmetic and copies ran while one was open for 29% -> 0% of each run, Pallas kernels for 0% -> 13%
where the time goes in v1:
time: 65.7 us; the launch traced here: 65 us
  starting transfers between devices  26 us (40%)
  local copies, waits for them, and re-layouts  16.8 us (26%)
  Pallas kernels  13.8 us (21%)
  waiting for transfers between devices  8.26 us (13%)
    unnamed x44, local copies, waits for them, and re-layouts  16.8 us
    all_to_all x1, starting transfers between devices, per_device(): got = lax.all_to_all(sent, 'leaf', 0, 0, tiled=True)  10.7 us
    ppermute x1, waiting for transfers between devices, per_device(): before = lax.ppermute(rows, ring, [(i, i + 1) for i in range(last)])  8.25 us
    ppermute x1, starting transfers between devices, per_device(): after = lax.ppermute(rows, ring, [(i + 1, i) for i in range(last)])  6.93 us
    pallas_call x1, Pallas kernels, local_call(): pl.pallas_call(local_kernel, out_shape=jax.ShapeDtypeStruct((2, RHS, LEAV...  6.54 us
    all_to_all x1, starting transfers between devices, per_device(): roots = lax.all_to_all(fan, 'branch', 0, 0, tiled=True)  6.49 us
    pallas_call x1, Pallas kernels, up_call(): pl.pallas_call(up_kernel, out_shape=[jax.ShapeDtypeStruct((ROWS, RHS, 2 *...  3.27 us
    pallas_call x1, Pallas kernels, final_call(): pl.pallas_call(final_kernel, out_shape=jax.ShapeDtypeStruct((2, RHS, LEAV...  1.98 us
  transfers between devices with their start and end apart: 4, of which 1 were waited for; matrix products, arithmetic and copies ran while one was open for 0% of the time, Pallas kernels for 13%

profile of v1, /device:TPU:1, one launch (start us, length us, event | category | flops | bytes accessed | tf_op | source)
XLA Modules:
  0.0 65.0 jit_solution(10655634041702880051)
XLA Ops:
  0.0 0.0 copy-start.4
  0.0 0.0 copy-start.7
  0.0 0.0 copy-start.21
  0.0 0.0 copy-start.20
  0.0 3.3 %up.1 = (bf16[22,16,128]{2,1,0:T(8,128)(2,1)}, bf16[5,16,128]{2,1,0:T(8,128)(2,1)}, bf16[8,16,128]{2,1,0:T(8,128)(2,1)}) custom-call(bf16[2,16,512]{2,1,0:T(8,128)(2,1)} %values.1, bf16[8,64,64]{2,1,0:T(8,128)(2,1)} %basis.5, bf16[14,64,64]{2,1,0:T(8,128)(2,1)} %transfer.5, bf16[1,62,64,64]{3,2,1,0:T(8,128)(2,1)} %upper.3), custom_call_target="tpu_custom_call" | custom-call | tf_op jit(solution)/shard_map/up/pallas_call | solution.py:99
  3.3 6.5 %all-to-all-start = ((bf16[8,16,128]{2,1,0:T(8,128)(2,1)}), bf16[8,16,128]{2,1,0:T(8,128)(2,1)S(1)}, u32[]{:S(2)}, u32[]{:S(2)}) async-start(bf16[8,16,128]{2,1,0:T(8,128)(2,1)} %get-tuple-element.11), calls=%async_computation | async-start | bytes 65536 | tf_op jit(solution)/shard_map/all_to_all | solution.py:340
  9.8 0.0 copy-start.1
  9.8 1.2 %copy-done.1 = bf16[1,62,64,64]{3,2,1,0:T(8,128)(2,1)S(1)} copy-done((bf16[1,62,64,64]{3,2,1,0:T(8,128)(2,1)S(1)}, bf16[1,62,64,64]{3,2,1,0:T(8,128)(2,1)}, u32[]{:S(2)}) %copy-start.1) | copy-done | bytes 507928
  11.0 0.0 copy-start.3
  11.0 0.9 %copy-done.3 = bf16[14,64,64]{2,1,0:T(8,128)(2,1)S(1)} copy-done((bf16[14,64,64]{2,1,0:T(8,128)(2,1)S(1)}, bf16[14,64,64]{2,1,0:T(8,128)(2,1)}, u32[]{:S(2)}) %copy-start.3) | copy-done | bytes 114712
  11.9 0.0 copy-start.5
  11.9 1.6 %copy-done.5 = bf16[2,1,62,64,64]{4,3,2,1,0:T(8,128)(2,1)S(1)} copy-done((bf16[2,1,62,64,64]{4,3,2,1,0:T(8,128)(2,1)S(1)}, bf16[2,1,62,64,64]{4,3,2,1,0:T(8,128)(2,1)}, u32[]{:S(2)}) %copy-start.5) | copy-done | bytes 1015832
  13.5 0.0 copy-start.6
  13.5 0.9 %copy-done.6 = bf16[8,64,64]{2,1,0:T(8,128)(2,1)S(1)} copy-done((bf16[8,64,64]{2,1,0:T(8,128)(2,1)S(1)}, bf16[8,64,64]{2,1,0:T(8,128)(2,1)}, u32[]{:S(2)}) %copy-start.6) | copy-done | bytes 65560
  14.4 0.0 copy-start.13
  14.4 0.9 %copy-done.13 = bf16[2,1,7,64,64]{4,3,2,1,0:T(8,128)(2,1)S(1)} copy-done((bf16[2,1,7,64,64]{4,3,2,1,0:T(8,128)(2,1)S(1)}, bf16[2,1,7,64,64]{4,3,2,1,0:T(8,128)(2,1)}, u32[]{:S(2)}) %copy-start.13) | copy-done | bytes 114712
  15.3 0.0 copy-start.2
  15.4 1.8 %prep.1 = (bf16[128,896]{1,0:T(8,128)(2,1)S(1)}, bf16[128,768]{1,0:T(8,128)(2,1)S(1)}, bf16[1024,128]{1,0:T(8,128)(2,1)S(1)}) custom-call(bf16[1,62,64,64]{3,2,1,0:T(8,128)(2,1)S(1)} %copy-done.1, bf16[2,1,62,64,64]{4,3,2,1,0:T(8,128)(2,1)S(1)} %copy-done.5, bf16[2,1,7,64,64]{4,3,2,1,0:T(8,128)(2,1)S(1)} %copy-done.13, bf16[8,64,64]{2,1,0:T(8,128)(2,1)S(1)} %copy-done.6, ...), custom_call_target="tpu_custom_call" | custom-call | flops 100000000 | bytes 4000000 | tf_op jit(solution)/shard_map/prep/pallas_call | solution.py:165
  17.2 0.0 copy-start.11
  17.2 0.7 %copy-done.11 = bf16[1024,128]{1,0:T(8,128)(2,1)} copy-done((bf16[1024,128]{1,0:T(8,128)(2,1)}, bf16[1024,128]{1,0:T(8,128)(2,1)S(1)}, u32[]{:S(2)}) %copy-start.11) | copy-done | bytes 262168
  17.9 0.0 copy-start.14
  17.9 0.7 %copy-done.14 = bf16[128,896]{1,0:T(8,128)(2,1)} copy-done((bf16[128,896]{1,0:T(8,128)(2,1)}, bf16[128,896]{1,0:T(8,128)(2,1)S(1)}, u32[]{:S(2)}) %copy-start.14) | copy-done | bytes 229400
  18.6 0.0 copy-start.16
  18.6 0.7 %copy-done.16 = bf16[128,768]{1,0:T(8,128)(2,1)} copy-done((bf16[128,768]{1,0:T(8,128)(2,1)}, bf16[128,768]{1,0:T(8,128)(2,1)S(1)}, u32[]{:S(2)}) %copy-start.16) | copy-done | bytes 196632
  19.2 0.0 all-to-all-done.roots
  19.2 0.0 copy-start.15
  19.2 0.9 %copy-done.15 = bf16[128,896]{1,0:T(8,128)(2,1)S(1)} copy-done((bf16[128,896]{1,0:T(8,128)(2,1)S(1)}, bf16[128,896]{1,0:T(8,128)(2,1)}, u32[]{:S(2)}) %copy-start.15) | copy-done | bytes 229400
  20.2 0.0 copy-start.19
  20.2 0.7 %copy-done.19 = bf16[5,16,128]{2,1,0:T(8,128)(2,1)S(1)} copy-done((bf16[5,16,128]{2,1,0:T(8,128)(2,1)S(1)}, bf16[5,16,128]{2,1,0:T(8,128)(2,1)}, u32[]{:S(2)}) %copy-start.19) | copy-done | bytes 20504
  20.9 0.2 mid.1
  21.1 0.0 copy-start.8
  21.1 0.7 %copy-done.8 = bf16[32,2,16,128]{3,2,1,0:T(8,128)(2,1)} copy-done((bf16[32,2,16,128]{3,2,1,0:T(8,128)(2,1)}, bf16[32,2,16,128]{3,2,1,0:T(8,128)(2,1)S(1)}, u32[]{:S(2)}) %copy-start.8) | copy-done | bytes 262168
  21.8 10.7 %all-to-all-start.1 = ((bf16[32,2,16,128]{3,2,1,0:T(8,128)(2,1)}), bf16[32,2,16,128]{3,2,1,0:T(8,128)(2,1)}, u32[]{:S(2)}, u32[]{:S(2)}) async-start(bf16[32,2,16,128]{3,2,1,0:T(8,128)(2,1)} %copy-done.8), calls=%async_computation.1 | async-start | bytes 524288 | tf_op jit(solution)/shard_map/all_to_all | solution.py:349
  32.5 6.9 %collective-permute-start.1 = (bf16[22,16,128]{2,1,0:T(8,128)(2,1)}, bf16[22,16,128]{2,1,0:T(8,128)(2,1)S(1)}, u32[]{:S(2)}, u32[]{:S(2)}) collective-permute-start(bf16[22,16,128]{2,1,0:T(8,128)(2,1)} %get-tuple-element.16.own), channel_id=1, source_target_pairs={{1,0},{2,1},{3,2},{4,3},{5,4},{6,5},{7,6},{8,7},{9,8},{10,9},{11,1... | collective-permute-start | bytes 270344 | tf_op jit(solution)/shard_map/ppermute | solution.py:344
  39.4 1.9 %collective-permute-start = (bf16[22,16,128]{2,1,0:T(8,128)(2,1)}, bf16[22,16,128]{2,1,0:T(8,128)(2,1)S(1)}, u32[]{:S(2)}, u32[]{:S(2)}) collective-permute-start(bf16[22,16,128]{2,1,0:T(8,128)(2,1)} %get-tuple-element.16.own), channel_id=1, source_target_pairs={{0,1},{1,2},{2,3},{3,4},{4,5},{5,6},{6,7},{7,8},{8,9},{9,10},{10,1... | collective-permute-start | bytes 270344 | tf_op jit(solution)/shard_map/ppermute | solution.py:343
  41.4 0.0 collective-permute-done.1.after
  41.4 8.3 %collective-permute-done.before = bf16[22,16,128]{2,1,0:T(8,128)(2,1)S(1)} collective-permute-done((bf16[22,16,128]{2,1,0:T(8,128)(2,1)}, bf16[22,16,128]{2,1,0:T(8,128)(2,1)S(1)}, u32[]{:S(2)}, u32[]{:S(2)}) %collective-permute-start) | collective-permute-done | bytes 90144 | tf_op jit(solution)/shard_map/ppermute | solution.py:343
  49.6 0.0 copy-done.4
  49.6 0.0 copy-done.7
  49.6 0.0 copy-done.21
  49.6 0.0 copy-done.20
  49.7 0.0 copy-done.2
  49.7 0.0 copy-start
  49.7 2.6 %copy-done = bf16[2,14,12,64,64]{4,3,2,1,0:T(8,128)(2,1)S(1)} copy-done((bf16[2,14,12,64,64]{4,3,2,1,0:T(8,128)(2,1)S(1)}, bf16[2,14,12,64,64]{4,3,2,1,0:T(8,128)(2,1)}, u32[]{:S(2)}) %copy-start) | copy-done | bytes 2752536
  52.2 0.0 copy-start.18
  52.2 0.9 %copy-done.18 = bf16[22,16,128]{2,1,0:T(8,128)(2,1)S(1)} copy-done((bf16[22,16,128]{2,1,0:T(8,128)(2,1)S(1)}, bf16[22,16,128]{2,1,0:T(8,128)(2,1)}, u32[]{:S(2)}) %copy-start.18) | copy-done | bytes 90136
  53.1 6.5 %local.1.base = f32[2,16,512]{2,1,0:T(8,128)S(1)} custom-call(bf16[22,16,128]{2,1,0:T(8,128)(2,1)S(1)} %copy-done.18, bf16[22,16,128]{2,1,0:T(8,128)(2,1)S(1)} %collective-permute-done.before, bf16[22,16,128]{2,1,0:T(8,128)(2,1)S(1)} %collective-permute-done.1.after, s32[14,12]{1,0:T(8,128)S(1)} %copy-done.20, s32[8,12]{1,0:T(8,128)S(1)} %copy-done.21, ...), custom_call_target="tpu_custom_call" | custom-call | flops 100000000 | bytes 20000000 | tf_op jit(solution)/shard_map/local/pallas_call | solution.py:278
  59.7 0.0 copy-start.9
  59.7 0.6 copy-done.9
  60.3 0.0 all-to-all-done.1.got
  60.3 0.0 copy-start.10
  60.3 0.8 %copy-done.10 = f32[2,16,512]{2,1,0:T(8,128)S(1)} copy-done((f32[2,16,512]{2,1,0:T(8,128)S(1)}, f32[2,16,512]{2,1,0:T(8,128)}, u32[]{:S(2)}) %copy-start.10) | copy-done | bytes 65560
  61.2 0.0 copy-start.12
  61.2 0.9 %copy-done.12 = bf16[1024,128]{1,0:T(8,128)(2,1)S(1)} copy-done((bf16[1024,128]{1,0:T(8,128)(2,1)S(1)}, bf16[1024,128]{1,0:T(8,128)(2,1)}, u32[]{:S(2)}) %copy-start.12) | copy-done | bytes 262168
  62.1 0.0 copy-start.17
  62.1 0.9 %copy-done.17 = bf16[128,768]{1,0:T(8,128)(2,1)S(1)} copy-done((bf16[128,768]{1,0:T(8,128)(2,1)S(1)}, bf16[128,768]{1,0:T(8,128)(2,1)}, u32[]{:S(2)}) %copy-start.17) | copy-done | bytes 196632
  63.0 2.0 %final.1 = f32[2,16,512]{2,1,0:T(8,128)} custom-call(bf16[32,2,16,128]{3,2,1,0:T(8,128)(2,1)} %all-to-all-done.1.got, bf16[128,768]{1,0:T(8,128)(2,1)S(1)} %copy-done.17, bf16[1024,128]{1,0:T(8,128)(2,1)S(1)} %copy-done.12, f32[2,16,512]{2,1,0:T(8,128)S(1)} %copy-done.10), custom_call_target="tpu_custom_call" | custom-call | tf_op jit(solution)/shard_map/final/pallas_call | solution.py:317
Async XLA Ops:
  0.0 49.6 %copy-start.4 = (bf16[14,64,64]{2,1,0:T(8,128)(2,1)S(1)}, bf16[14,64,64]{2,1,0:T(8,128)(2,1)}, u32[]{:S(2)}) copy-start(bf16[14,64,64]{2,1,0:T(8,128)(2,1)} %transfer.5) | copy-start | bytes 344068
  0.0 49.6 %copy-start.7 = (bf16[8,64,64]{2,1,0:T(8,128)(2,1)S(1)}, bf16[8,64,64]{2,1,0:T(8,128)(2,1)}, u32[]{:S(2)}) copy-start(bf16[8,64,64]{2,1,0:T(8,128)(2,1)} %basis.5) | copy-start | bytes 196612
  0.0 49.6 %copy-start.21 = (s32[8,12]{1,0:T(8,128)S(1)}, s32[8,12]{1,0:T(8,128)}, u32[]{:S(2)}) copy-start(s32[8,12]{1,0:T(8,128)} %near_source.1) | copy-start | bytes 1156
  0.0 49.6 %copy-start.20 = (s32[14,12]{1,0:T(8,128)S(1)}, s32[14,12]{1,0:T(8,128)}, u32[]{:S(2)}) copy-start(s32[14,12]{1,0:T(8,128)} %coupling_source.1) | copy-start | bytes 2020
  3.3 15.9 %all-to-all-start = ((bf16[8,16,128]{2,1,0:T(8,128)(2,1)}), bf16[8,16,128]{2,1,0:T(8,128)(2,1)S(1)}, u32[]{:S(2)}, u32[]{:S(2)}) async-start(bf16[8,16,128]{2,1,0:T(8,128)(2,1)} %get-tuple-element.11), calls=%async_computation | async-start | bytes 65536 | tf_op jit(solution)/shard_map/all_to_all | solution.py:340
  9.8 1.2 %copy-start.1 = (bf16[1,62,64,64]{3,2,1,0:T(8,128)(2,1)S(1)}, bf16[1,62,64,64]{3,2,1,0:T(8,128)(2,1)}, u32[]{:S(2)}) copy-start(bf16[1,62,64,64]{3,2,1,0:T(8,128)(2,1)} %upper.3) | copy-start | bytes 1523716
  11.0 0.9 %copy-start.3 = (bf16[14,64,64]{2,1,0:T(8,128)(2,1)S(1)}, bf16[14,64,64]{2,1,0:T(8,128)(2,1)}, u32[]{:S(2)}) copy-start(bf16[14,64,64]{2,1,0:T(8,128)(2,1)} %transfer.5) | copy-start | bytes 344068
  11.9 1.6 %copy-start.5 = (bf16[2,1,62,64,64]{4,3,2,1,0:T(8,128)(2,1)S(1)}, bf16[2,1,62,64,64]{4,3,2,1,0:T(8,128)(2,1)}, u32[]{:S(2)}) copy-start(bf16[2,1,62,64,64]{4,3,2,1,0:T(8,128)(2,1)} %couple.1) | copy-start | bytes 3047428
  13.5 0.9 %copy-start.6 = (bf16[8,64,64]{2,1,0:T(8,128)(2,1)S(1)}, bf16[8,64,64]{2,1,0:T(8,128)(2,1)}, u32[]{:S(2)}) copy-start(bf16[8,64,64]{2,1,0:T(8,128)(2,1)} %basis.5) | copy-start | bytes 196612
  14.4 0.9 %copy-start.13 = (bf16[2,1,7,64,64]{4,3,2,1,0:T(8,128)(2,1)S(1)}, bf16[2,1,7,64,64]{4,3,2,1,0:T(8,128)(2,1)}, u32[]{:S(2)}) copy-start(bf16[2,1,7,64,64]{4,3,2,1,0:T(8,128)(2,1)} %top.1) | copy-start | bytes 344068
  15.3 34.3 %copy-start.2 = (bf16[2,8,12,64,64]{4,3,2,1,0:T(8,128)(2,1)S(1)}, bf16[2,8,12,64,64]{4,3,2,1,0:T(8,128)(2,1)}, u32[]{:S(2)}) copy-start(bf16[2,8,12,64,64]{4,3,2,1,0:T(8,128)(2,1)} %near.1) | copy-start | bytes 4718596
  17.2 0.7 %copy-start.11 = (bf16[1024,128]{1,0:T(8,128)(2,1)}, bf16[1024,128]{1,0:T(8,128)(2,1)S(1)}, u32[]{:S(2)}) copy-start(bf16[1024,128]{1,0:T(8,128)(2,1)S(1)} %get-tuple-element.15.leafs) | copy-start | bytes 786436
  17.9 0.7 %copy-start.14 = (bf16[128,896]{1,0:T(8,128)(2,1)}, bf16[128,896]{1,0:T(8,128)(2,1)S(1)}, u32[]{:S(2)}) copy-start(bf16[128,896]{1,0:T(8,128)(2,1)S(1)} %get-tuple-element.12.over) | copy-start | bytes 688132
  18.6 0.7 %copy-start.16 = (bf16[128,768]{1,0:T(8,128)(2,1)}, bf16[128,768]{1,0:T(8,128)(2,1)S(1)}, u32[]{:S(2)}) copy-start(bf16[128,768]{1,0:T(8,128)(2,1)S(1)} %get-tuple-element.14.fold) | copy-start | bytes 589828
  19.2 0.9 %copy-start.15 = (bf16[128,896]{1,0:T(8,128)(2,1)S(1)}, bf16[128,896]{1,0:T(8,128)(2,1)}, u32[]{:S(2)}) copy-start(bf16[128,896]{1,0:T(8,128)(2,1)} %copy-done.14) | copy-start | bytes 688132
  20.2 0.7 %copy-start.19 = (bf16[5,16,128]{2,1,0:T(8,128)(2,1)S(1)}, bf16[5,16,128]{2,1,0:T(8,128)(2,1)}, u32[]{:S(2)}) copy-start(bf16[5,16,128]{2,1,0:T(8,128)(2,1)} %get-tuple-element.13.chain) | copy-start | bytes 61444
  21.1 0.7 %copy-start.8 = (bf16[32,2,16,128]{3,2,1,0:T(8,128)(2,1)}, bf16[32,2,16,128]{3,2,1,0:T(8,128)(2,1)S(1)}, u32[]{:S(2)}) copy-start(bf16[32,2,16,128]{3,2,1,0:T(8,128)(2,1)S(1)} %mid.1) | copy-start | bytes 786436
  21.8 38.5 %all-to-all-start.1 = ((bf16[32,2,16,128]{3,2,1,0:T(8,128)(2,1)}), bf16[32,2,16,128]{3,2,1,0:T(8,128)(2,1)}, u32[]{:S(2)}, u32[]{:S(2)}) async-start(bf16[32,2,16,128]{3,2,1,0:T(8,128)(2,1)} %copy-done.8), calls=%async_computation.1 | async-start | bytes 524288 | tf_op jit(solution)/shard_map/all_to_all | solution.py:349
  32.5 8.9 %collective-permute-start.1 = (bf16[22,16,128]{2,1,0:T(8,128)(2,1)}, bf16[22,16,128]{2,1,0:T(8,128)(2,1)S(1)}, u32[]{:S(2)}, u32[]{:S(2)}) collective-permute-start(bf16[22,16,128]{2,1,0:T(8,128)(2,1)} %get-tuple-element.16.own), channel_id=1, source_target_pairs={{1,0},{2,1},{3,2},{4,3},{5,4},{6,5},{7,6},{8,7},{9,8},{10,9},{11,1... | collective-permute-start | bytes 270344 | tf_op jit(solution)/shard_map/ppermute | solution.py:344
  39.4 10.2 %collective-permute-start = (bf16[22,16,128]{2,1,0:T(8,128)(2,1)}, bf16[22,16,128]{2,1,0:T(8,128)(2,1)S(1)}, u32[]{:S(2)}, u32[]{:S(2)}) collective-permute-start(bf16[22,16,128]{2,1,0:T(8,128)(2,1)} %get-tuple-element.16.own), channel_id=1, source_target_pairs={{0,1},{1,2},{2,3},{3,4},{4,5},{5,6},{6,7},{7,8},{8,9},{9,10},{10,1... | collective-permute-start | bytes 270344 | tf_op jit(solution)/shard_map/ppermute | solution.py:343
  49.7 2.6 %copy-start = (bf16[2,14,12,64,64]{4,3,2,1,0:T(8,128)(2,1)S(1)}, bf16[2,14,12,64,64]{4,3,2,1,0:T(8,128)(2,1)}, u32[]{:S(2)}) copy-start(bf16[2,14,12,64,64]{4,3,2,1,0:T(8,128)(2,1)} %coupling.1) | copy-start | bytes 8257540
  52.2 0.9 %copy-start.18 = (bf16[22,16,128]{2,1,0:T(8,128)(2,1)S(1)}, bf16[22,16,128]{2,1,0:T(8,128)(2,1)}, u32[]{:S(2)}) copy-start(bf16[22,16,128]{2,1,0:T(8,128)(2,1)} %get-tuple-element.16.own) | copy-start | bytes 270340
  59.7 0.6 copy-start.9
  60.3 0.8 %copy-start.10 = (f32[2,16,512]{2,1,0:T(8,128)S(1)}, f32[2,16,512]{2,1,0:T(8,128)}, u32[]{:S(2)}) copy-start(f32[2,16,512]{2,1,0:T(8,128)} %copy-done.9) | copy-start | bytes 196612
  61.2 0.9 %copy-start.12 = (bf16[1024,128]{1,0:T(8,128)(2,1)S(1)}, bf16[1024,128]{1,0:T(8,128)(2,1)}, u32[]{:S(2)}) copy-start(bf16[1024,128]{1,0:T(8,128)(2,1)} %copy-done.11) | copy-start | bytes 786436
  62.1 0.9 %copy-start.17 = (bf16[128,768]{1,0:T(8,128)(2,1)S(1)}, bf16[128,768]{1,0:T(8,128)(2,1)}, u32[]{:S(2)}) copy-start(bf16[128,768]{1,0:T(8,128)(2,1)} %copy-done.16) | copy-start | bytes 589828

commit v2 on v1

--- a/solution.py
+++ b/solution.py
@@ -20,7 +20,11 @@
 LINKS = 12
 ANY = pl.BlockSpec(memory_space=pl.ANY)
 VMEM = pl.BlockSpec(memory_space=pltpu.VMEM)
-SMEM = pl.BlockSpec(memory_space=pltpu.SMEM)
+MB = 2**20
+
+
+def hbm(*arrays):
+    return [pltpu.with_memory_space_constraint(a, pltpu.HBM) for a in arrays]
 
 
 def dot(a, b):
@@ -99,9 +103,9 @@
     return pl.pallas_call(
         up_kernel,
         out_shape=[
-            jax.ShapeDtypeStruct((ROWS, RHS, 2 * R), bf16),
-            jax.ShapeDtypeStruct((DEPTH, RHS, 2 * R), bf16),
-            jax.ShapeDtypeStruct((N_BRANCH, RHS, 2 * R), bf16),
+            pltpu.VMEM((ROWS, RHS, 2 * R), bf16),
+            pltpu.VMEM((DEPTH, RHS, 2 * R), bf16),
+            pltpu.VMEM((N_BRANCH, RHS, 2 * R), bf16),
         ],
         in_specs=[ANY] * 4,
         out_specs=[VMEM] * 3,
@@ -112,12 +116,14 @@
             pltpu.VMEM((DEPTH, R, R), bf16),
             pltpu.SemaphoreType.DMA((3 + DEPTH,)),
         ],
-        compiler_params=pltpu.CompilerParams(vmem_limit_bytes=56 * 2**20),
+        compiler_params=pltpu.CompilerParams(vmem_limit_bytes=8 * MB),
         name="up",
-    )(values, basis, transfer, upper)
-
-
-def prep_kernel(upper, couple, top, basis, transfer, over, fold, leafs, upp, cou, tops, sem):
+    )(*hbm(values, basis, transfer, upper))
+
+
+def prep_kernel(
+    upper, couple, top, basis, transfer, over, fold, leafs, upp, cou, tops, bas, tra, sem
+):
     leaf = lax.axis_index("leaf")
     copies = []
     for step in range(DEPTH):
@@ -127,15 +133,20 @@
             pltpu.make_async_copy(couple.at[:, 0, index], cou.at[step], sem.at[DEPTH + step])
         )
     last = pltpu.make_async_copy(top, tops, sem.at[2 * DEPTH])
-    for copy in copies:
+    first = [
+        pltpu.make_async_copy(transfer, tra, sem.at[2 * DEPTH + 1]),
+        pltpu.make_async_copy(basis, bas, sem.at[2 * DEPTH + 2]),
+    ]
+    for copy in first + copies + [last]:
         copy.start()
-    last.start()
     zero = jnp.zeros((R, R), bf16)
-    tops2 = [transfer[12 + t] for t in range(2)]
-    tops1 = [dot(transfer[8 + t], tops2[t // 2]).astype(bf16) for t in range(4)]
-    tops0 = [dot(transfer[t], tops1[t // 2]).astype(bf16) for t in range(8)]
+    for copy in first:
+        copy.wait()
+    tops2 = [tra[12 + t] for t in range(2)]
+    tops1 = [dot(tra[8 + t], tops2[t // 2]).astype(bf16) for t in range(4)]
+    tops0 = [dot(tra[t], tops1[t // 2]).astype(bf16) for t in range(8)]
     for t in range(LEAVES):
-        full = dot(basis[t], tops0[t]).astype(bf16)
+        full = dot(bas[t], tops0[t]).astype(bf16)
         leafs[pl.ds(t * R, R), :] = jnp.concatenate([full, zero], axis=1)
         leafs[pl.ds((LEAVES + t) * R, R), :] = jnp.concatenate([zero, full], axis=1)
     for copy in copies:
@@ -165,24 +176,26 @@
     return pl.pallas_call(
         prep_kernel,
         out_shape=[
-            jax.ShapeDtypeStruct((2 * R, (N_BRANCH - 1) * 2 * R), bf16),
-            jax.ShapeDtypeStruct((2 * R, (DEPTH + 1) * 2 * R), bf16),
-            jax.ShapeDtypeStruct((2 * LEAVES * R, 2 * R), bf16),
+            pltpu.VMEM((2 * R, (N_BRANCH - 1) * 2 * R), bf16),
+            pltpu.VMEM((2 * R, (DEPTH + 1) * 2 * R), bf16),
+            pltpu.VMEM((2 * LEAVES * R, 2 * R), bf16),
         ],
-        in_specs=[ANY] * 3 + [VMEM] * 2,
+        in_specs=[ANY] * 5,
         out_specs=[VMEM] * 3,
         scratch_shapes=[
             pltpu.VMEM((DEPTH, R, R), bf16),
             pltpu.VMEM((DEPTH, 2, R, R), bf16),
             pltpu.VMEM((2, 1, N_BRANCH - 1, R, R), bf16),
-            pltpu.SemaphoreType.DMA((2 * DEPTH + 1,)),
+            pltpu.VMEM((LEAVES, R, R), bf16),
+            pltpu.VMEM((LOCAL, R, R), bf16),
+            pltpu.SemaphoreType.DMA((2 * DEPTH + 3,)),
         ],
-        compiler_params=pltpu.CompilerParams(vmem_limit_bytes=8 * 2**20),
+        compiler_params=pltpu.CompilerParams(vmem_limit_bytes=8 * MB),
         cost_estimate=pl.CostEstimate(
             flops=10**8, bytes_accessed=4 * 10**6, transcendentals=0
         ),
         name="prep",
-    )(upper, couple, top, basis, transfer)
+    )(*hbm(upper, couple, top, basis, transfer))
 
 
 def mid_kernel(roots, over, chain, out):
@@ -199,18 +212,27 @@
 def mid_call(roots, over, chain):
     return pl.pallas_call(
         mid_kernel,
-        out_shape=jax.ShapeDtypeStruct((N_LEAF, 2, RHS, 2 * R), bf16),
+        out_shape=pltpu.VMEM((N_LEAF, 2, RHS, 2 * R), bf16),
         in_specs=[VMEM] * 3,
         out_specs=VMEM,
-        compiler_params=pltpu.CompilerParams(vmem_limit_bytes=8 * 2**20),
+        compiler_params=pltpu.CompilerParams(vmem_limit_bytes=8 * MB),
         name="mid",
     )(roots, over, chain)
 
 
 def local_kernel(
-    own, before, after, coupling_source, near_source, coupling, near, transfer, basis,
-    base, wide, sums, cells,
+    own, before, after, coupling, near, coupling_source, near_source, transfer, basis,
+    base, wide, sums, cells, nea, cosrc, nesrc, tra, bas, sem,
 ):
+    fields = [pltpu.make_async_copy(near.at[g], nea.at[g], sem.at[4 + g]) for g in range(2)]
+    copies = [
+        pltpu.make_async_copy(near_source, nesrc, sem.at[0]),
+        pltpu.make_async_copy(coupling_source, cosrc, sem.at[1]),
+        pltpu.make_async_copy(transfer, tra, sem.at[2]),
+        pltpu.make_async_copy(basis, bas, sem.at[3]),
+    ]
+    for copy in copies + fields:
+        copy.start()
     left = lax.broadcasted_iota(jnp.int32, (RHS, 2 * R), 1) < R
     for part, ref in enumerate((before, own, after)):
         for row in range(ROWS):
@@ -236,21 +258,14 @@
             result.append(acc)
         return jnp.concatenate(result, axis=0)
 
-    def near_body(t, carry):
-        picked = []
-        for j in range(LINKS):
-            s = near_source[t, j]
-            picked.append(jnp.right_shift(s, 3) * ROWS + jnp.bitwise_and(s, 7))
-        cells[t] = block(picked, lambda g, j: near[g, t, j])
-        return carry
-
-    lax.fori_loop(0, LEAVES, near_body, 0)
+    for copy in copies:
+        copy.wait()
 
     def far_body(log, start, t, carry):
         r = start + t
         picked = []
         for j in range(LINKS):
-            s = coupling_source[r, j]
+            s = cosrc[r, j]
             picked.append(
                 jnp.right_shift(s, log) * ROWS
                 + LEAVES
@@ -262,12 +277,24 @@
 
     for log, start in ((1, 12), (2, 8), (3, 0)):
         lax.fori_loop(0, 1 << log, functools.partial(far_body, log, start), 0)
+
+    def near_body(t, carry):
+        picked = []
+        for j in range(LINKS):
+            s = nesrc[t, j]
+            picked.append(jnp.right_shift(s, 3) * ROWS + jnp.bitwise_and(s, 7))
+        cells[t] = block(picked, lambda g, j: nea[g, t, j])
+        return carry
+
+    for field in fields:
+        field.wait()
+    lax.fori_loop(0, LEAVES, near_body, 0)
     up2 = [sums[12 + t].astype(bf16) for t in range(2)]
     up1 = [
-        (sums[8 + t] + dot_nt(up2[t // 2], transfer[8 + t])).astype(bf16) for t in range(4)
+        (sums[8 + t] + dot_nt(up2[t // 2], tra[8 + t])).astype(bf16) for t in range(4)
     ]
-    up0 = [(sums[t] + dot_nt(up1[t // 2], transfer[t])).astype(bf16) for t in range(8)]
-    full = [cells[t] + dot_nt(up0[t], basis[t]) for t in range(8)]
+    up0 = [(sums[t] + dot_nt(up1[t // 2], tra[t])).astype(bf16) for t in range(8)]
+    full = [cells[t] + dot_nt(up0[t], bas[t]) for t in range(8)]
     for pair in range(LEAVES // 2):
         both = jnp.concatenate([full[2 * pair], full[2 * pair + 1]], axis=1)
         for g in range(2):
@@ -277,20 +304,29 @@
 def local_call(own, before, after, coupling_source, near_source, coupling, near, transfer, basis):
     return pl.pallas_call(
         local_kernel,
-        out_shape=jax.ShapeDtypeStruct((2, RHS, LEAVES * R), f32),
-        in_specs=[VMEM] * 3 + [SMEM] * 2 + [VMEM] * 4,
+        out_shape=pltpu.VMEM((2, RHS, LEAVES * R), f32),
+        in_specs=[VMEM] * 4 + [ANY] * 5,
         out_specs=VMEM,
         scratch_shapes=[
             pltpu.VMEM((2, 3 * ROWS, RHS, 2 * R), bf16),
             pltpu.VMEM((LOCAL, 2 * RHS, R), f32),
             pltpu.VMEM((LEAVES, 2 * RHS, R), f32),
+            pltpu.VMEM((2, LEAVES, LINKS, R, R), bf16),
+            pltpu.SMEM((LOCAL, LINKS), jnp.int32),
+            pltpu.SMEM((LEAVES, LINKS), jnp.int32),
+            pltpu.VMEM((LOCAL, R, R), bf16),
+            pltpu.VMEM((LEAVES, R, R), bf16),
+            pltpu.SemaphoreType.DMA((6,)),
         ],
-        compiler_params=pltpu.CompilerParams(vmem_limit_bytes=24 * 2**20),
+        compiler_params=pltpu.CompilerParams(vmem_limit_bytes=24 * MB),
         cost_estimate=pl.CostEstimate(
             flops=10**8, bytes_accessed=2 * 10**7, transcendentals=0
         ),
         name="local",
-    )(own, before, after, coupling_source, near_source, coupling, near, transfer, basis)
+    )(
+        own, before, after, coupling,
+        *hbm(near, coupling_source, near_source, transfer, basis),
+    )
 
 
 def final_kernel(got, fold, leafs, base, out):
@@ -319,7 +355,7 @@
         out_shape=jax.ShapeDtypeStruct((2, RHS, LEAVES * R), f32),
         in_specs=[VMEM] * 4,
         out_specs=VMEM,
-        compiler_params=pltpu.CompilerParams(vmem_limit_bytes=8 * 2**20),
+        compiler_params=pltpu.CompilerParams(vmem_limit_bytes=8 * MB),
         name="final",
     )(got, fold, leafs, base)
 
@@ -345,6 +381,7 @@
     over, fold, leafs = prep_call(
         upper_transfer, upper_coupling, top_coupling, leaf_basis, transfer
     )
+    roots, before, after = lax.optimization_barrier((roots, before, after))
     sent = mid_call(roots, over, chain)
     got = lax.all_to_all(sent, "leaf", 0, 0, tiled=True)
     base = local_call(

time: 65.7 us -> 46.5 us (0.71)
  local copies, waits for them, and re-layouts: 16.8 us -> 2.56 us
  waiting for transfers between devices: 8.26 us -> 4.38 us
  starting transfers between devices: 26 us -> 24.6 us
    unnamed x44 -> x2, local copies, waits for them, and re-layouts: 16.8 us -> 2.56 us
    ppermute x1, waiting for transfers between devices: 8.25 us -> 0.01 us  [per_device(): before = lax.ppermute(rows, ring, [(i, i + 1) for i in range(last)])]
    ppermute x1, starting transfers between devices: 6.93 us -> 11.1 us  [per_device(): after = lax.ppermute(rows, ring, [(i + 1, i) for i in range(last)])]
    all_to_all x1, starting transfers between devices: 10.7 us -> 6.99 us  [per_device(): got = lax.all_to_all(sent, 'leaf', 0, 0, tiled=True)]
    all_to_all x1, waiting for transfers between devices: 0.01 us -> 2.49 us  [per_device(): roots = lax.all_to_all(fan, 'branch', 0, 0, tiled=True)]
    all_to_all x1, starting transfers between devices: 6.49 us -> 4.59 us  [per_device(): roots = lax.all_to_all(fan, 'branch', 0, 0, tiled=True)]
    all_to_all x1, waiting for transfers between devices: 0.01 us -> 1.88 us  [per_device(): got = lax.all_to_all(sent, 'leaf', 0, 0, tiled=True)]
    pallas_call x4, Pallas kernels: 11.8 us -> 13.3 us  [the longest x1 6.78 us: local_call(): pl.pallas_call(local_kernel, out_shape=pltpu.VMEM((2, RHS, LEAVES * R), f...]
  transfers between devices with their start and end apart: 4 -> 4, of which waited for: 1 -> 2; matrix products, arithmetic and copies ran while one was open for 0% -> 0% of each run, Pallas kernels for 13% -> 20%
where the time goes in v2:
time: 46.5 us; the launch traced here: 45.9 us
  starting transfers between devices  24.6 us (53%)
  Pallas kernels  14.3 us (31%)
  waiting for transfers between devices  4.38 us (9%)
  local copies, waits for them, and re-layouts  2.56 us (6%)
    ppermute x1, starting transfers between devices, per_device(): after = lax.ppermute(rows, ring, [(i + 1, i) for i in range(last)])  11.1 us
    all_to_all x1, starting transfers between devices, per_device(): got = lax.all_to_all(sent, 'leaf', 0, 0, tiled=True)  6.99 us
    pallas_call x1, Pallas kernels, local_call(): pl.pallas_call(local_kernel, out_shape=pltpu.VMEM((2, RHS, LEAVES * R), f...  6.78 us
    all_to_all x1, starting transfers between devices, per_device(): roots = lax.all_to_all(fan, 'branch', 0, 0, tiled=True)  4.59 us
    pallas_call x1, Pallas kernels, up_call(): pl.pallas_call(up_kernel, out_shape=[pltpu.VMEM((ROWS, RHS, 2 * R), bf16)...  3.22 us
    unnamed x2, local copies, waits for them, and re-layouts  2.56 us
    all_to_all x1, waiting for transfers between devices, per_device(): roots = lax.all_to_all(fan, 'branch', 0, 0, tiled=True)  2.49 us
    pallas_call x1, Pallas kernels, prep_call(): pl.pallas_call(prep_kernel, out_shape=[pltpu.VMEM((2 * R, (N_BRANCH - 1)...  2.36 us
  transfers between devices with their start and end apart: 4, of which 2 were waited for; matrix products, arithmetic and copies ran while one was open for 0% of the time, Pallas kernels for 20%

profile of v2, /device:TPU:1, one launch (start us, length us, event | category | flops | bytes accessed | tf_op | source)
XLA Modules:
  0.0 45.9 jit_solution(5397824809963034048)
XLA Ops:
  0.0 3.2 %up.1 = (bf16[22,16,128]{2,1,0:T(8,128)(2,1)S(1)}, bf16[5,16,128]{2,1,0:T(8,128)(2,1)S(1)}, bf16[8,16,128]{2,1,0:T(8,128)(2,1)}) custom-call(bf16[2,16,512]{2,1,0:T(8,128)(2,1)} %values.1, bf16[8,64,64]{2,1,0:T(8,128)(2,1)} %basis.5, bf16[14,64,64]{2,1,0:T(8,128)(2,1)} %transfer.5, bf16[1,62,64,64]{3,2,1,0:T(8,128)(2,1)} %upper.3), custom_call_target="tpu_custom_call" | custom-call | tf_op jit(solution)/shard_map/up/pallas_call | solution.py:103
  3.2 11.1 %collective-permute-start.1 = (bf16[22,16,128]{2,1,0:T(8,128)(2,1)S(1)}, bf16[22,16,128]{2,1,0:T(8,128)(2,1)S(1)}, u32[]{:S(2)}, u32[]{:S(2)}) collective-permute-start(bf16[22,16,128]{2,1,0:T(8,128)(2,1)S(1)} %get-tuple-element.15.own), channel_id=1, source_target_pairs={{1,0},{2,1},{3,2},{4,3},{5,4},{6,5},{7,6},{8,7},{9,8},{10,9},{11,1... | collective-permute-start | bytes 270344 | tf_op jit(solution)/shard_map/ppermute | solution.py:380
  14.3 1.9 %collective-permute-start = (bf16[22,16,128]{2,1,0:T(8,128)(2,1)S(1)}, bf16[22,16,128]{2,1,0:T(8,128)(2,1)S(1)}, u32[]{:S(2)}, u32[]{:S(2)}) collective-permute-start(bf16[22,16,128]{2,1,0:T(8,128)(2,1)S(1)} %get-tuple-element.15.own), channel_id=1, source_target_pairs={{0,1},{1,2},{2,3},{3,4},{4,5},{5,6},{6,7},{7,8},{8,9},{9,10},{10,1... | collective-permute-start | bytes 270344 | tf_op jit(solution)/shard_map/ppermute | solution.py:379
  16.2 4.6 %all-to-all-start = ((bf16[8,16,128]{2,1,0:T(8,128)(2,1)}), bf16[8,16,128]{2,1,0:T(8,128)(2,1)S(1)}, u32[]{:S(2)}, u32[]{:S(2)}) async-start(bf16[8,16,128]{2,1,0:T(8,128)(2,1)} %get-tuple-element.14), calls=%async_computation | async-start | bytes 65536 | tf_op jit(solution)/shard_map/all_to_all | solution.py:376
  20.8 2.4 %prep.1 = (bf16[128,896]{1,0:T(8,128)(2,1)S(1)}, bf16[128,768]{1,0:T(8,128)(2,1)S(1)}, bf16[1024,128]{1,0:T(8,128)(2,1)S(1)}) custom-call(bf16[1,62,64,64]{3,2,1,0:T(8,128)(2,1)} %upper.3, bf16[2,1,62,64,64]{4,3,2,1,0:T(8,128)(2,1)} %couple.1, bf16[2,1,7,64,64]{4,3,2,1,0:T(8,128)(2,1)} %top.1, bf16[8,64,64]{2,1,0:T(8,128)(2,1)} %basis.5, ...), custom_call_target="tpu_custom_call" | custom-call | flops 100000000 | bytes 4000000 | tf_op jit(solution)/shard_map/prep/pallas_call | solution.py:176
  23.2 2.5 %all-to-all-done.roots = bf16[8,16,128]{2,1,0:T(8,128)(2,1)S(1)} async-done(((bf16[8,16,128]{2,1,0:T(8,128)(2,1)}), bf16[8,16,128]{2,1,0:T(8,128)(2,1)S(1)}, u32[]{:S(2)}, u32[]{:S(2)}) %all-to-all-start) | async-done | bytes 32800 | tf_op jit(solution)/shard_map/all_to_all | solution.py:376
  25.7 0.0 collective-permute-done.1.after
  25.7 0.0 collective-permute-done.before
  25.7 0.9 %mid.1 = bf16[32,2,16,128]{3,2,1,0:T(8,128)(2,1)} custom-call(bf16[8,16,128]{2,1,0:T(8,128)(2,1)S(1)} %all-to-all-done.roots, bf16[128,896]{1,0:T(8,128)(2,1)S(1)} %get-tuple-element.17.over, bf16[5,16,128]{2,1,0:T(8,128)(2,1)S(1)} %get-tuple-element.18.chain), custom_call_target="tpu_custom_call" | custom-call | tf_op jit(solution)/shard_map/mid/pallas_call | solution.py:213
  26.6 7.0 %all-to-all-start.1 = ((bf16[32,2,16,128]{3,2,1,0:T(8,128)(2,1)}), bf16[32,2,16,128]{3,2,1,0:T(8,128)(2,1)S(1)}, u32[]{:S(2)}, u32[]{:S(2)}) async-start(bf16[32,2,16,128]{3,2,1,0:T(8,128)(2,1)} %mid.1), calls=%async_computation.1 | async-start | bytes 524288 | tf_op jit(solution)/shard_map/all_to_all | solution.py:386
  33.6 0.0 copy-start
  33.6 2.6 %copy-done = bf16[2,14,12,64,64]{4,3,2,1,0:T(8,128)(2,1)S(1)} copy-done((bf16[2,14,12,64,64]{4,3,2,1,0:T(8,128)(2,1)S(1)}, bf16[2,14,12,64,64]{4,3,2,1,0:T(8,128)(2,1)}, u32[]{:S(2)}) %copy-start) | copy-done | bytes 2752536
  36.2 6.8 %local.1.base = f32[2,16,512]{2,1,0:T(8,128)S(1)} custom-call(bf16[22,16,128]{2,1,0:T(8,128)(2,1)S(1)} %get-tuple-element.15.own, bf16[22,16,128]{2,1,0:T(8,128)(2,1)S(1)} %collective-permute-done.before, bf16[22,16,128]{2,1,0:T(8,128)(2,1)S(1)} %collective-permute-done.1.after, bf16[2,14,12,64,64]{4,3,2,1,0:T(8,128)(2,1)S(1)} %copy-done, ...), custom_call_target="tpu_custom_call" | custom-call | flops 100000000 | bytes 20000000 | tf_op jit(solution)/shard_map/local/pallas_call | solution.py:305
  42.9 1.9 %all-to-all-done.1.got = bf16[32,2,16,128]{3,2,1,0:T(8,128)(2,1)S(1)} async-done(((bf16[32,2,16,128]{3,2,1,0:T(8,128)(2,1)}), bf16[32,2,16,128]{3,2,1,0:T(8,128)(2,1)S(1)}, u32[]{:S(2)}, u32[]{:S(2)}) %all-to-all-start.1) | async-done | bytes 262176 | tf_op jit(solution)/shard_map/all_to_all | solution.py:386
  44.8 1.0 %final.1 = f32[2,16,512]{2,1,0:T(8,128)} custom-call(bf16[32,2,16,128]{3,2,1,0:T(8,128)(2,1)S(1)} %all-to-all-done.1.got, bf16[128,768]{1,0:T(8,128)(2,1)S(1)} %get-tuple-element.19.fold, bf16[1024,128]{1,0:T(8,128)(2,1)S(1)} %get-tuple-element.20.leafs, f32[2,16,512]{2,1,0:T(8,128)S(1)} %local.1.base), custom_call_target="tpu_custom_call" | custom-call | tf_op jit(solution)/shard_map/final/pallas_call | solution.py:353
Async XLA Ops:
  3.2 22.5 %collective-permute-start.1 = (bf16[22,16,128]{2,1,0:T(8,128)(2,1)S(1)}, bf16[22,16,128]{2,1,0:T(8,128)(2,1)S(1)}, u32[]{:S(2)}, u32[]{:S(2)}) collective-permute-start(bf16[22,16,128]{2,1,0:T(8,128)(2,1)S(1)} %get-tuple-element.15.own), channel_id=1, source_target_pairs={{1,0},{2,1},{3,2},{4,3},{5,4},{6,5},{7,6},{8,7},{9,8},{10,9},{11,1... | collective-permute-start | bytes 270344 | tf_op jit(solution)/shard_map/ppermute | solution.py:380
  14.3 11.4 %collective-permute-start = (bf16[22,16,128]{2,1,0:T(8,128)(2,1)S(1)}, bf16[22,16,128]{2,1,0:T(8,128)(2,1)S(1)}, u32[]{:S(2)}, u32[]{:S(2)}) collective-permute-start(bf16[22,16,128]{2,1,0:T(8,128)(2,1)S(1)} %get-tuple-element.15.own), channel_id=1, source_target_pairs={{0,1},{1,2},{2,3},{3,4},{4,5},{5,6},{6,7},{7,8},{8,9},{9,10},{10,1... | collective-permute-start | bytes 270344 | tf_op jit(solution)/shard_map/ppermute | solution.py:379
  16.2 9.4 %all-to-all-start = ((bf16[8,16,128]{2,1,0:T(8,128)(2,1)}), bf16[8,16,128]{2,1,0:T(8,128)(2,1)S(1)}, u32[]{:S(2)}, u32[]{:S(2)}) async-start(bf16[8,16,128]{2,1,0:T(8,128)(2,1)} %get-tuple-element.14), calls=%async_computation | async-start | bytes 65536 | tf_op jit(solution)/shard_map/all_to_all | solution.py:376
  26.6 18.2 %all-to-all-start.1 = ((bf16[32,2,16,128]{3,2,1,0:T(8,128)(2,1)}), bf16[32,2,16,128]{3,2,1,0:T(8,128)(2,1)S(1)}, u32[]{:S(2)}, u32[]{:S(2)}) async-start(bf16[32,2,16,128]{3,2,1,0:T(8,128)(2,1)} %mid.1), calls=%async_computation.1 | async-start | bytes 524288 | tf_op jit(solution)/shard_map/all_to_all | solution.py:386
  33.6 2.6 %copy-start = (bf16[2,14,12,64,64]{4,3,2,1,0:T(8,128)(2,1)S(1)}, bf16[2,14,12,64,64]{4,3,2,1,0:T(8,128)(2,1)}, u32[]{:S(2)}) copy-start(bf16[2,14,12,64,64]{4,3,2,1,0:T(8,128)(2,1)} %coupling.1) | copy-start | bytes 8257540

commit v3 on v2

--- a/solution.py
+++ b/solution.py
@@ -18,6 +18,7 @@
 N_LEAF = 32
 N_BRANCH = 8
 LINKS = 12
+UNROLL = 4
 ANY = pl.BlockSpec(memory_space=pl.ANY)
 VMEM = pl.BlockSpec(memory_space=pltpu.VMEM)
 MB = 2**20
@@ -222,16 +223,22 @@
 
 def local_kernel(
     own, before, after, coupling, near, coupling_source, near_source, transfer, basis,
-    base, wide, sums, cells, nea, cosrc, nesrc, tra, bas, sem,
+    base, wide, sums, cells, cou, nea, cosrc, nesrc, tra, bas, sem,
 ):
-    fields = [pltpu.make_async_copy(near.at[g], nea.at[g], sem.at[4 + g]) for g in range(2)]
-    copies = [
-        pltpu.make_async_copy(near_source, nesrc, sem.at[0]),
-        pltpu.make_async_copy(coupling_source, cosrc, sem.at[1]),
+    smalls = [
+        pltpu.make_async_copy(coupling_source, cosrc, sem.at[0]),
+        pltpu.make_async_copy(near_source, nesrc, sem.at[1]),
         pltpu.make_async_copy(transfer, tra, sem.at[2]),
         pltpu.make_async_copy(basis, bas, sem.at[3]),
     ]
-    for copy in copies + fields:
+    bigs = []
+    for n, (source, into, start, count) in enumerate(
+        ((coupling, cou, 8, 6), (coupling, cou, 0, 4), (coupling, cou, 4, 4),
+         (near, nea, 0, 4), (near, nea, 4, 4))
+    ):
+        span = pl.ds(start, count)
+        bigs.append(pltpu.make_async_copy(source.at[:, span], into.at[:, span], sem.at[4 + n]))
+    for copy in smalls[:2] + bigs + smalls[2:]:
         copy.start()
     left = lax.broadcasted_iota(jnp.int32, (RHS, 2 * R), 1) < R
     for part, ref in enumerate((before, own, after)):
@@ -244,7 +251,7 @@
     def block(picked, mats):
         result = []
         for g in range(2):
-            acc = jnp.zeros((RHS, R), f32)
+            acc = None
             for j in range(0, LINKS, 4):
                 v = jnp.concatenate(
                     [
@@ -254,14 +261,12 @@
                     axis=1,
                 )
                 m = jnp.concatenate([mats(g, j + n) for n in range(4)], axis=1)
-                acc += dot_nt(v, m)
+                part = dot_nt(v, m)
+                acc = part if acc is None else acc + part
             result.append(acc)
         return jnp.concatenate(result, axis=0)
 
-    for copy in copies:
-        copy.wait()
-
-    def far_body(log, start, t, carry):
+    def far_body(log, start, t):
         r = start + t
         picked = []
         for j in range(LINKS):
@@ -272,23 +277,37 @@
                 + start
                 + jnp.bitwise_and(s, (1 << log) - 1)
             )
-        sums[r] = block(picked, lambda g, j: coupling[g, r, j])
-        return carry
-
-    for log, start in ((1, 12), (2, 8), (3, 0)):
-        lax.fori_loop(0, 1 << log, functools.partial(far_body, log, start), 0)
-
-    def near_body(t, carry):
+        sums[r] = block(picked, lambda g, j: cou[g, r, j])
+
+    def near_body(t):
         picked = []
         for j in range(LINKS):
             s = nesrc[t, j]
             picked.append(jnp.right_shift(s, 3) * ROWS + jnp.bitwise_and(s, 7))
         cells[t] = block(picked, lambda g, j: nea[g, t, j])
-        return carry
-
-    for field in fields:
-        field.wait()
-    lax.fori_loop(0, LEAVES, near_body, 0)
+
+    def each(body, first, count):
+        def step(i, carry):
+            body(first + i)
+            return carry
+
+        lax.fori_loop(0, count, step, 0, unroll=min(UNROLL, count))
+
+    for copy in smalls[:2]:
+        copy.wait()
+    bigs[0].wait()
+    each(functools.partial(far_body, 1, 12), 0, 2)
+    each(functools.partial(far_body, 2, 8), 0, 4)
+    bigs[1].wait()
+    each(functools.partial(far_body, 3, 0), 0, 4)
+    bigs[2].wait()
+    each(functools.partial(far_body, 3, 0), 4, 4)
+    bigs[3].wait()
+    each(near_body, 0, 4)
+    bigs[4].wait()
+    each(near_body, 4, 4)
+    for copy in smalls[2:]:
+        copy.wait()
     up2 = [sums[12 + t].astype(bf16) for t in range(2)]
     up1 = [
         (sums[8 + t] + dot_nt(up2[t // 2], tra[8 + t])).astype(bf16) for t in range(4)
@@ -305,18 +324,19 @@
     return pl.pallas_call(
         local_kernel,
         out_shape=pltpu.VMEM((2, RHS, LEAVES * R), f32),
-        in_specs=[VMEM] * 4 + [ANY] * 5,
+        in_specs=[VMEM] * 3 + [ANY] * 6,
         out_specs=VMEM,
         scratch_shapes=[
             pltpu.VMEM((2, 3 * ROWS, RHS, 2 * R), bf16),
             pltpu.VMEM((LOCAL, 2 * RHS, R), f32),
             pltpu.VMEM((LEAVES, 2 * RHS, R), f32),
+            pltpu.VMEM((2, LOCAL, LINKS, R, R), bf16),
             pltpu.VMEM((2, LEAVES, LINKS, R, R), bf16),
             pltpu.SMEM((LOCAL, LINKS), jnp.int32),
             pltpu.SMEM((LEAVES, LINKS), jnp.int32),
             pltpu.VMEM((LOCAL, R, R), bf16),
             pltpu.VMEM((LEAVES, R, R), bf16),
-            pltpu.SemaphoreType.DMA((6,)),
+            pltpu.SemaphoreType.DMA((9,)),
         ],
         compiler_params=pltpu.CompilerParams(vmem_limit_bytes=24 * MB),
         cost_estimate=pl.CostEstimate(
@@ -324,8 +344,8 @@
         ),
         name="local",
     )(
-        own, before, after, coupling,
-        *hbm(near, coupling_source, near_source, transfer, basis),
+        own, before, after,
+        *hbm(coupling, near, coupling_source, near_source, transfer, basis),
     )
 
 
@@ -381,8 +401,8 @@
     over, fold, leafs = prep_call(
         upper_transfer, upper_coupling, top_coupling, leaf_basis, transfer
     )
-    roots, before, after = lax.optimization_barrier((roots, before, after))
     sent = mid_call(roots, over, chain)
+    sent, before, after = lax.optimization_barrier((sent, before, after))
     got = lax.all_to_all(sent, "leaf", 0, 0, tiled=True)
     base = local_call(
         rows, before, after, coupling_source, near_source, local_coupling, near_field,

time: 46.5 us -> 45.5 us (0.978)
  waiting for transfers between devices: 4.38 us -> 9.1 us
  local copies, waits for them, and re-layouts: 2.56 us -> 0 us
  Pallas kernels: 14.3 us -> 12 us
  starting transfers between devices: 24.6 us -> 23.7 us
    all_to_all x1, waiting for transfers between devices: 1.88 us -> 6.74 us  [per_device(): got = lax.all_to_all(sent, 'leaf', 0, 0, tiled=True)]
    unnamed x2 -> x0, local copies, waits for them, and re-layouts: 2.56 us -> none
    pallas_call x1, Pallas kernels: 6.78 us -> 4.49 us  [local_call(): pl.pallas_call(local_kernel, out_shape=pltpu.VMEM((2, RHS, LEAVES * R), f...]
    ppermute x1, starting transfers between devices: 1.92 us -> 3.95 us  [per_device(): before = lax.ppermute(rows, ring, [(i, i + 1) for i in range(last)])]
    ppermute x1, starting transfers between devices: 11.1 us -> 9.04 us  [per_device(): after = lax.ppermute(rows, ring, [(i + 1, i) for i in range(last)])]
    all_to_all x1, starting transfers between devices: 6.99 us -> 6.14 us  [per_device(): got = lax.all_to_all(sent, 'leaf', 0, 0, tiled=True)]
  transfers between devices with their start and end apart: 4 -> 4, of which waited for: 2 -> 2; matrix products, arithmetic and copies ran while one was open for 0% -> 0% of each run, Pallas kernels for 20% -> 17%
where the time goes in v3:
time: 45.5 us; the launch traced here: 44.9 us
  starting transfers between devices  23.7 us (52%)
  Pallas kernels  12 us (26%)
  waiting for transfers between devices  9.1 us (20%)
    ppermute x1, starting transfers between devices, per_device(): after = lax.ppermute(rows, ring, [(i + 1, i) for i in range(last)])  9.04 us
    all_to_all x1, waiting for transfers between devices, per_device(): got = lax.all_to_all(sent, 'leaf', 0, 0, tiled=True)  6.74 us
    all_to_all x1, starting transfers between devices, per_device(): got = lax.all_to_all(sent, 'leaf', 0, 0, tiled=True)  6.14 us
    all_to_all x1, starting transfers between devices, per_device(): roots = lax.all_to_all(fan, 'branch', 0, 0, tiled=True)  4.59 us
    pallas_call x1, Pallas kernels, local_call(): pl.pallas_call(local_kernel, out_shape=pltpu.VMEM((2, RHS, LEAVES * R), f...  4.49 us
    ppermute x1, starting transfers between devices, per_device(): before = lax.ppermute(rows, ring, [(i, i + 1) for i in range(last)])  3.95 us
    pallas_call x1, Pallas kernels, up_call(): pl.pallas_call(up_kernel, out_shape=[pltpu.VMEM((ROWS, RHS, 2 * R), bf16)...  3.22 us
    pallas_call x1, Pallas kernels, prep_call(): pl.pallas_call(prep_kernel, out_shape=[pltpu.VMEM((2 * R, (N_BRANCH - 1)...  2.36 us
  transfers between devices with their start and end apart: 4, of which 2 were waited for; matrix products, arithmetic and copies ran while one was open for 0% of the time, Pallas kernels for 17%

profile of v3, /device:TPU:1, one launch (start us, length us, event | category | flops | bytes accessed | tf_op | source)
XLA Modules:
  0.0 44.9 jit_solution(714540455655029804)
XLA Ops:
  0.0 3.2 %up.1 = (bf16[22,16,128]{2,1,0:T(8,128)(2,1)S(1)}, bf16[5,16,128]{2,1,0:T(8,128)(2,1)S(1)}, bf16[8,16,128]{2,1,0:T(8,128)(2,1)}) custom-call(bf16[2,16,512]{2,1,0:T(8,128)(2,1)} %values.1, bf16[8,64,64]{2,1,0:T(8,128)(2,1)} %basis.5, bf16[14,64,64]{2,1,0:T(8,128)(2,1)} %transfer.5, bf16[1,62,64,64]{3,2,1,0:T(8,128)(2,1)} %upper.3), custom_call_target="tpu_custom_call" | custom-call | tf_op jit(solution)/shard_map/up/pallas_call | solution.py:104
  3.2 3.9 %collective-permute-start = (bf16[22,16,128]{2,1,0:T(8,128)(2,1)S(1)}, bf16[22,16,128]{2,1,0:T(8,128)(2,1)S(1)}, u32[]{:S(2)}, u32[]{:S(2)}) collective-permute-start(bf16[22,16,128]{2,1,0:T(8,128)(2,1)S(1)} %get-tuple-element.17.own), channel_id=1, source_target_pairs={{0,1},{1,2},{2,3},{3,4},{4,5},{5,6},{6,7},{7,8},{8,9},{9,10},{10,1... | collective-permute-start | bytes 270344 | tf_op jit(solution)/shard_map/ppermute | solution.py:399
  7.2 9.0 %collective-permute-start.1 = (bf16[22,16,128]{2,1,0:T(8,128)(2,1)S(1)}, bf16[22,16,128]{2,1,0:T(8,128)(2,1)S(1)}, u32[]{:S(2)}, u32[]{:S(2)}) collective-permute-start(bf16[22,16,128]{2,1,0:T(8,128)(2,1)S(1)} %get-tuple-element.17.own), channel_id=1, source_target_pairs={{1,0},{2,1},{3,2},{4,3},{5,4},{6,5},{7,6},{8,7},{9,8},{10,9},{11,1... | collective-permute-start | bytes 270344 | tf_op jit(solution)/shard_map/ppermute | solution.py:400
  16.2 4.6 %all-to-all-start = ((bf16[8,16,128]{2,1,0:T(8,128)(2,1)}), bf16[8,16,128]{2,1,0:T(8,128)(2,1)S(1)}, u32[]{:S(2)}, u32[]{:S(2)}) async-start(bf16[8,16,128]{2,1,0:T(8,128)(2,1)} %get-tuple-element.14), calls=%async_computation | async-start | bytes 65536 | tf_op jit(solution)/shard_map/all_to_all | solution.py:396
  20.8 2.4 %prep.1 = (bf16[128,896]{1,0:T(8,128)(2,1)S(1)}, bf16[128,768]{1,0:T(8,128)(2,1)S(1)}, bf16[1024,128]{1,0:T(8,128)(2,1)S(1)}) custom-call(bf16[1,62,64,64]{3,2,1,0:T(8,128)(2,1)} %upper.3, bf16[2,1,62,64,64]{4,3,2,1,0:T(8,128)(2,1)} %couple.1, bf16[2,1,7,64,64]{4,3,2,1,0:T(8,128)(2,1)} %top.1, bf16[8,64,64]{2,1,0:T(8,128)(2,1)} %basis.5, ...), custom_call_target="tpu_custom_call" | custom-call | flops 100000000 | bytes 4000000 | tf_op jit(solution)/shard_map/prep/pallas_call | solution.py:177
  23.2 2.4 %all-to-all-done.roots = bf16[8,16,128]{2,1,0:T(8,128)(2,1)S(1)} async-done(((bf16[8,16,128]{2,1,0:T(8,128)(2,1)}), bf16[8,16,128]{2,1,0:T(8,128)(2,1)S(1)}, u32[]{:S(2)}, u32[]{:S(2)}) %all-to-all-start) | async-done | bytes 32800 | tf_op jit(solution)/shard_map/all_to_all | solution.py:396
  25.5 0.9 %mid.1 = bf16[32,2,16,128]{3,2,1,0:T(8,128)(2,1)} custom-call(bf16[8,16,128]{2,1,0:T(8,128)(2,1)S(1)} %all-to-all-done.roots, bf16[128,896]{1,0:T(8,128)(2,1)S(1)} %get-tuple-element.15.over, bf16[5,16,128]{2,1,0:T(8,128)(2,1)S(1)} %get-tuple-element.16.chain), custom_call_target="tpu_custom_call" | custom-call | tf_op jit(solution)/shard_map/mid/pallas_call | solution.py:214
  26.5 0.0 collective-permute-done.before
  26.5 0.0 collective-permute-done.1.after
  26.5 6.1 %all-to-all-start.1 = ((bf16[32,2,16,128]{3,2,1,0:T(8,128)(2,1)}), bf16[32,2,16,128]{3,2,1,0:T(8,128)(2,1)S(1)}, u32[]{:S(2)}, u32[]{:S(2)}) async-start(bf16[32,2,16,128]{3,2,1,0:T(8,128)(2,1)} %mid.1), calls=%async_computation.1 | async-start | bytes 524288 | tf_op jit(solution)/shard_map/all_to_all | solution.py:406
  32.6 4.5 %local.1.base = f32[2,16,512]{2,1,0:T(8,128)S(1)} custom-call(bf16[22,16,128]{2,1,0:T(8,128)(2,1)S(1)} %get-tuple-element.17.own, bf16[22,16,128]{2,1,0:T(8,128)(2,1)S(1)} %collective-permute-done.before, bf16[22,16,128]{2,1,0:T(8,128)(2,1)S(1)} %collective-permute-done.1.after, bf16[2,14,12,64,64]{4,3,2,1,0:T(8,128)(2,1)} %coupling.1, ...), custom_call_target="tpu_custom_call" | custom-call | flops 100000000 | bytes 20000000 | tf_op jit(solution)/shard_map/local/pallas_call | solution.py:324
  37.1 6.7 %all-to-all-done.1.got = bf16[32,2,16,128]{3,2,1,0:T(8,128)(2,1)S(1)} async-done(((bf16[32,2,16,128]{3,2,1,0:T(8,128)(2,1)}), bf16[32,2,16,128]{3,2,1,0:T(8,128)(2,1)S(1)}, u32[]{:S(2)}, u32[]{:S(2)}) %all-to-all-start.1) | async-done | bytes 262176 | tf_op jit(solution)/shard_map/all_to_all | solution.py:406
  43.9 1.0 %final.1 = f32[2,16,512]{2,1,0:T(8,128)} custom-call(bf16[32,2,16,128]{3,2,1,0:T(8,128)(2,1)S(1)} %all-to-all-done.1.got, bf16[128,768]{1,0:T(8,128)(2,1)S(1)} %get-tuple-element.19.fold, bf16[1024,128]{1,0:T(8,128)(2,1)S(1)} %get-tuple-element.20.leafs, f32[2,16,512]{2,1,0:T(8,128)S(1)} %local.1.base), custom_call_target="tpu_custom_call" | custom-call | tf_op jit(solution)/shard_map/final/pallas_call | solution.py:373
Async XLA Ops:
  3.2 23.2 %collective-permute-start = (bf16[22,16,128]{2,1,0:T(8,128)(2,1)S(1)}, bf16[22,16,128]{2,1,0:T(8,128)(2,1)S(1)}, u32[]{:S(2)}, u32[]{:S(2)}) collective-permute-start(bf16[22,16,128]{2,1,0:T(8,128)(2,1)S(1)} %get-tuple-element.17.own), channel_id=1, source_target_pairs={{0,1},{1,2},{2,3},{3,4},{4,5},{5,6},{6,7},{7,8},{8,9},{9,10},{10,1... | collective-permute-start | bytes 270344 | tf_op jit(solution)/shard_map/ppermute | solution.py:399
  7.2 19.3 %collective-permute-start.1 = (bf16[22,16,128]{2,1,0:T(8,128)(2,1)S(1)}, bf16[22,16,128]{2,1,0:T(8,128)(2,1)S(1)}, u32[]{:S(2)}, u32[]{:S(2)}) collective-permute-start(bf16[22,16,128]{2,1,0:T(8,128)(2,1)S(1)} %get-tuple-element.17.own), channel_id=1, source_target_pairs={{1,0},{2,1},{3,2},{4,3},{5,4},{6,5},{7,6},{8,7},{9,8},{10,9},{11,1... | collective-permute-start | bytes 270344 | tf_op jit(solution)/shard_map/ppermute | solution.py:400
  16.2 9.3 %all-to-all-start = ((bf16[8,16,128]{2,1,0:T(8,128)(2,1)}), bf16[8,16,128]{2,1,0:T(8,128)(2,1)S(1)}, u32[]{:S(2)}, u32[]{:S(2)}) async-start(bf16[8,16,128]{2,1,0:T(8,128)(2,1)} %get-tuple-element.14), calls=%async_computation | async-start | bytes 65536 | tf_op jit(solution)/shard_map/all_to_all | solution.py:396
  26.5 17.4 %all-to-all-start.1 = ((bf16[32,2,16,128]{3,2,1,0:T(8,128)(2,1)}), bf16[32,2,16,128]{3,2,1,0:T(8,128)(2,1)S(1)}, u32[]{:S(2)}, u32[]{:S(2)}) async-start(bf16[32,2,16,128]{3,2,1,0:T(8,128)(2,1)} %mid.1), calls=%async_computation.1 | async-start | bytes 524288 | tf_op jit(solution)/shard_map/all_to_all | solution.py:406

commit v4 on v3

--- a/solution.py
+++ b/solution.py
@@ -48,101 +48,127 @@
     return 2 * N_LEAF - 2 * (N_LEAF >> step) + jnp.right_shift(leaf, step)
 
 
-def up_kernel(values, basis, transfer, upper, rows, chain, fan, vals, bas, tra, upp, sem):
+def up_kernel(
+    values, basis, transfer, upper, top, vals, coefs, chain, fan, downs, tops, bas, tra, upp, sem
+):
     leaf = lax.axis_index("leaf")
-    copies = [
+    firsts = [
+        pltpu.make_async_copy(
+            upper.at[0, upper_index(leaf, step)], upp.at[step], sem.at[4 + step]
+        )
+        for step in range(DEPTH)
+    ]
+    firsts += [
         pltpu.make_async_copy(values, vals, sem.at[0]),
         pltpu.make_async_copy(basis, bas, sem.at[1]),
         pltpu.make_async_copy(transfer, tra, sem.at[2]),
     ]
+    last = pltpu.make_async_copy(top, tops, sem.at[3])
+    for copy in firsts + [last]:
+        copy.start()
+    for copy in firsts:
+        copy.wait()
+    down = upp[0]
+    downs[0] = down
+    for step in range(1, DEPTH):
+        down = dot(down, upp[step]).astype(bf16)
+        downs[step] = down
+    level = []
+    for pair in range(LEAVES // 2):
+        x0 = vals[0, :, pl.ds(pair * 2 * R, 2 * R)]
+        x1 = vals[1, :, pl.ds(pair * 2 * R, 2 * R)]
+        for half in range(2):
+            lanes = slice(half * R, (half + 1) * R)
+            cell = jnp.concatenate([x0[:, lanes], x1[:, lanes]], axis=0)
+            level.append(dot(cell, bas[2 * pair + half]).astype(bf16))
+    begin = 0
+    while len(level) > 1:
+        for i, c in enumerate(level):
+            coefs[begin + i] = c
+        merged = [
+            (dot(level[i], tra[begin + i]) + dot(level[i + 1], tra[begin + i + 1])).astype(bf16)
+            for i in range(0, len(level), 2)
+        ]
+        begin += len(level)
+        level = merged
+    root = level[0]
+    chain[0] = packed(root)
+    for step in range(1, DEPTH + 1):
+        part = packed(dot(root, downs[step - 1]).astype(bf16))
+        if step < DEPTH:
+            chain[step] = part
+        else:
+            for b in range(N_BRANCH):
+                fan[b] = part
+    last.wait()
+
+
+def up_call(values, basis, transfer, upper, top):
+    return pl.pallas_call(
+        up_kernel,
+        out_shape=[
+            pltpu.VMEM((2, RHS, LEAVES * R), bf16),
+            pltpu.VMEM((LOCAL, 2 * RHS, R), bf16),
+            pltpu.VMEM((DEPTH, RHS, 2 * R), bf16),
+            pltpu.VMEM((N_BRANCH, RHS, 2 * R), bf16),
+            pltpu.VMEM((DEPTH, R, R), bf16),
+            pltpu.VMEM((2, 1, N_BRANCH - 1, R, R), bf16),
+        ],
+        in_specs=[ANY] * 5,
+        out_specs=[VMEM] * 6,
+        scratch_shapes=[
+            pltpu.VMEM((LEAVES, R, R), bf16),
+            pltpu.VMEM((LOCAL, R, R), bf16),
+            pltpu.VMEM((DEPTH, R, R), bf16),
+            pltpu.SemaphoreType.DMA((4 + DEPTH,)),
+        ],
+        compiler_params=pltpu.CompilerParams(vmem_limit_bytes=8 * MB),
+        name="up",
+    )(*hbm(values, basis, transfer, upper, top))
+
+
+def pack_kernel(vals, coefs, rows):
+    left = lax.broadcasted_iota(jnp.int32, (RHS, 2 * R), 1) < R
+    for pair in range(LEAVES // 2):
+        x0 = vals[0, :, pl.ds(pair * 2 * R, 2 * R)]
+        x1 = vals[1, :, pl.ds(pair * 2 * R, 2 * R)]
+        rows[2 * pair] = jnp.where(left, x0, turned(x1))
+        rows[2 * pair + 1] = jnp.where(left, turned(x0), x1)
+    for i in range(LOCAL):
+        rows[LEAVES + i] = packed(coefs[i])
+
+
+def pack_call(vals, coefs):
+    return pl.pallas_call(
+        pack_kernel,
+        out_shape=pltpu.VMEM((ROWS, RHS, 2 * R), bf16),
+        in_specs=[VMEM] * 2,
+        out_specs=VMEM,
+        compiler_params=pltpu.CompilerParams(vmem_limit_bytes=8 * MB),
+        cost_estimate=pl.CostEstimate(
+            flops=10**8, bytes_accessed=4 * 10**6, transcendentals=0
+        ),
+        name="pack",
+    )(vals, coefs)
+
+
+def prep_kernel(couple, downs, basis, transfer, fold, leafs, cou, bas, tra, sem):
+    leaf = lax.axis_index("leaf")
+    copies = [
+        pltpu.make_async_copy(transfer, tra, sem.at[DEPTH]),
+        pltpu.make_async_copy(basis, bas, sem.at[DEPTH + 1]),
+    ]
     for step in range(DEPTH):
         copies.append(
             pltpu.make_async_copy(
-                upper.at[0, upper_index(leaf, step)], upp.at[step], sem.at[3 + step]
+                couple.at[:, 0, upper_index(leaf, step)], cou.at[step], sem.at[step]
             )
         )
     for copy in copies:
         copy.start()
-    copies[0].wait()
-    left = lax.broadcasted_iota(jnp.int32, (RHS, 2 * R), 1) < R
-    cells = []
-    for pair in range(LEAVES // 2):
-        x0 = vals[0, :, pl.ds(pair * 2 * R, 2 * R)]
-        x1 = vals[1, :, pl.ds(pair * 2 * R, 2 * R)]
-        y0, y1 = turned(x0), turned(x1)
-        rows[2 * pair] = jnp.where(left, x0, y1)
-        rows[2 * pair + 1] = jnp.where(left, y0, x1)
-        cells.append(jnp.concatenate([x0[:, :R], x1[:, :R]], axis=0))
-        cells.append(jnp.concatenate([y0[:, :R], y1[:, :R]], axis=0))
-    copies[1].wait()
-    coefs = [dot(cells[i], bas[i]).astype(bf16) for i in range(LEAVES)]
-    copies[2].wait()
-    begin, place = 0, LEAVES
-    while len(coefs) > 1:
-        for i, c in enumerate(coefs):
-            rows[place + i] = packed(c)
-        place += len(coefs)
-        merged = [
-            (
-                dot(coefs[i], tra[begin + i]) + dot(coefs[i + 1], tra[begin + i + 1])
-            ).astype(bf16)
-            for i in range(0, len(coefs), 2)
-        ]
-        begin += len(coefs)
-        coefs = merged
-    coef = coefs[0]
-    for step in range(DEPTH):
-        chain[step] = packed(coef)
-        copies[3 + step].wait()
-        coef = dot(coef, upp[step]).astype(bf16)
-    top = packed(coef)
-    for b in range(N_BRANCH):
-        fan[b] = top
-
-
-def up_call(values, basis, transfer, upper):
-    return pl.pallas_call(
-        up_kernel,
-        out_shape=[
-            pltpu.VMEM((ROWS, RHS, 2 * R), bf16),
-            pltpu.VMEM((DEPTH, RHS, 2 * R), bf16),
-            pltpu.VMEM((N_BRANCH, RHS, 2 * R), bf16),
-        ],
-        in_specs=[ANY] * 4,
-        out_specs=[VMEM] * 3,
-        scratch_shapes=[
-            pltpu.VMEM((2, RHS, LEAVES * R), bf16),
-            pltpu.VMEM((LEAVES, R, R), bf16),
-            pltpu.VMEM((LOCAL, R, R), bf16),
-            pltpu.VMEM((DEPTH, R, R), bf16),
-            pltpu.SemaphoreType.DMA((3 + DEPTH,)),
-        ],
-        compiler_params=pltpu.CompilerParams(vmem_limit_bytes=8 * MB),
-        name="up",
-    )(*hbm(values, basis, transfer, upper))
-
-
-def prep_kernel(
-    upper, couple, top, basis, transfer, over, fold, leafs, upp, cou, tops, bas, tra, sem
-):
-    leaf = lax.axis_index("leaf")
-    copies = []
-    for step in range(DEPTH):
-        index = upper_index(leaf, step)
-        copies.append(pltpu.make_async_copy(upper.at[0, index], upp.at[step], sem.at[step]))
-        copies.append(
-            pltpu.make_async_copy(couple.at[:, 0, index], cou.at[step], sem.at[DEPTH + step])
-        )
-    last = pltpu.make_async_copy(top, tops, sem.at[2 * DEPTH])
-    first = [
-        pltpu.make_async_copy(transfer, tra, sem.at[2 * DEPTH + 1]),
-        pltpu.make_async_copy(basis, bas, sem.at[2 * DEPTH + 2]),
-    ]
-    for copy in first + copies + [last]:
-        copy.start()
+    for copy in copies:
+        copy.wait()
     zero = jnp.zeros((R, R), bf16)
-    for copy in first:
-        copy.wait()
     tops2 = [tra[12 + t] for t in range(2)]
     tops1 = [dot(tra[8 + t], tops2[t // 2]).astype(bf16) for t in range(4)]
     tops0 = [dot(tra[t], tops1[t // 2]).astype(bf16) for t in range(8)]
@@ -150,67 +176,61 @@
         full = dot(bas[t], tops0[t]).astype(bf16)
         leafs[pl.ds(t * R, R), :] = jnp.concatenate([full, zero], axis=1)
         leafs[pl.ds((LEAVES + t) * R, R), :] = jnp.concatenate([zero, full], axis=1)
-    for copy in copies:
-        copy.wait()
-    down = None
     for step in range(DEPTH + 1):
         lanes = pl.ds(step * 2 * R, 2 * R)
         for g in range(2):
             if step == DEPTH:
-                mat = down
+                mat = downs[DEPTH - 1]
             elif step == 0:
                 mat = cou[step, g]
             else:
-                mat = dot(down, cou[step, g]).astype(bf16)
+                mat = dot(downs[step - 1], cou[step, g]).astype(bf16)
             pair = [mat, zero] if g == 0 else [zero, mat]
             fold[pl.ds(g * R, R), lanes] = jnp.concatenate(pair, axis=1)
-        if step < DEPTH:
-            down = upp[0] if step == 0 else dot(down, upp[step]).astype(bf16)
-    last.wait()
-    for i in range(N_BRANCH - 1):
-        lanes = pl.ds(i * 2 * R, 2 * R)
-        over[pl.ds(0, R), lanes] = jnp.concatenate([tops[0, 0, i], zero], axis=1)
-        over[pl.ds(R, R), lanes] = jnp.concatenate([zero, tops[1, 0, i]], axis=1)
-
-
-def prep_call(upper, couple, top, basis, transfer):
+
+
+def prep_call(couple, downs, basis, transfer):
+    couple, basis, transfer = hbm(couple, basis, transfer)
     return pl.pallas_call(
         prep_kernel,
         out_shape=[
-            pltpu.VMEM((2 * R, (N_BRANCH - 1) * 2 * R), bf16),
             pltpu.VMEM((2 * R, (DEPTH + 1) * 2 * R), bf16),
             pltpu.VMEM((2 * LEAVES * R, 2 * R), bf16),
         ],
-        in_specs=[ANY] * 5,
-        out_specs=[VMEM] * 3,
+        in_specs=[ANY, VMEM, ANY, ANY],
+        out_specs=[VMEM] * 2,
         scratch_shapes=[
-            pltpu.VMEM((DEPTH, R, R), bf16),
             pltpu.VMEM((DEPTH, 2, R, R), bf16),
-            pltpu.VMEM((2, 1, N_BRANCH - 1, R, R), bf16),
             pltpu.VMEM((LEAVES, R, R), bf16),
             pltpu.VMEM((LOCAL, R, R), bf16),
-            pltpu.SemaphoreType.DMA((2 * DEPTH + 3,)),
+            pltpu.SemaphoreType.DMA((DEPTH + 2,)),
         ],
         compiler_params=pltpu.CompilerParams(vmem_limit_bytes=8 * MB),
         cost_estimate=pl.CostEstimate(
             flops=10**8, bytes_accessed=4 * 10**6, transcendentals=0
         ),
         name="prep",
-    )(*hbm(upper, couple, top, basis, transfer))
-
-
-def mid_kernel(roots, over, chain, out):
+    )(couple, downs, basis, transfer)
+
+
+def mid_kernel(roots, tops, chain, out):
     leaf = lax.axis_index("leaf")
     branch = lax.axis_index("branch")
     others = [roots[(branch + 1 + i) % N_BRANCH] for i in range(N_BRANCH - 1)]
-    part = dot_nt(jnp.concatenate(others, axis=1), over[...]).astype(bf16)
+    parts = []
+    for g in range(2):
+        lanes = slice(g * R, (g + 1) * R)
+        v = jnp.concatenate([other[:, lanes] for other in others], axis=1)
+        m = jnp.concatenate([tops[g, 0, i] for i in range(N_BRANCH - 1)], axis=1)
+        parts.append(dot_nt(v, m))
+    part = jnp.concatenate(parts, axis=1).astype(bf16)
     for i in range(N_LEAF):
         to = jnp.bitwise_xor(leaf, i)
         out[to, 0] = chain[max(i.bit_length() - 1, 0)]
         out[to, 1] = part
 
 
-def mid_call(roots, over, chain):
+def mid_call(roots, tops, chain):
     return pl.pallas_call(
         mid_kernel,
         out_shape=pltpu.VMEM((N_LEAF, 2, RHS, 2 * R), bf16),
@@ -218,7 +238,7 @@
         out_specs=VMEM,
         compiler_params=pltpu.CompilerParams(vmem_limit_bytes=8 * MB),
         name="mid",
-    )(roots, over, chain)
+    )(roots, tops, chain)
 
 
 def local_kernel(
@@ -392,18 +412,19 @@
     upper_coupling,
     top_coupling,
 ):
-    rows, chain, fan = up_call(values, leaf_basis, transfer, upper_transfer)
+    vals, coefs, chain, fan, downs, tops = up_call(
+        values, leaf_basis, transfer, upper_transfer, top_coupling
+    )
     roots = lax.all_to_all(fan, "branch", 0, 0, tiled=True)
+    rows = pack_call(vals, coefs)
     last = N_BRANCH * N_LEAF - 1
     ring = ("branch", "leaf")
     before = lax.ppermute(rows, ring, [(i, i + 1) for i in range(last)])
     after = lax.ppermute(rows, ring, [(i + 1, i) for i in range(last)])
-    over, fold, leafs = prep_call(
-        upper_transfer, upper_coupling, top_coupling, leaf_basis, transfer
-    )
-    sent = mid_call(roots, over, chain)
+    sent = mid_call(roots, tops, chain)
     sent, before, after = lax.optimization_barrier((sent, before, after))
     got = lax.all_to_all(sent, "leaf", 0, 0, tiled=True)
+    fold, leafs = prep_call(upper_coupling, downs, leaf_basis, transfer)
     base = local_call(
         rows, before, after, coupling_source, near_source, local_coupling, near_field,
         transfer, leaf_basis,

time: 45.5 us -> 45.6 us (level)
  blocking collectives: 0 us -> 9.22 us
  waiting for transfers between devices: 9.1 us -> 5.1 us
  starting transfers between devices: 23.7 us -> 20 us
  Pallas kernels: 12 us -> 10.5 us
    all_to_all x0 -> x1, blocking collectives: none -> 9.22 us  [per_device(): roots = lax.all_to_all(fan, 'branch', 0, 0, tiled=True)]
    all_to_all x1 -> x0, starting transfers between devices: 4.59 us -> none  [per_device(): roots = lax.all_to_all(fan, 'branch', 0, 0, tiled=True)]
    all_to_all x1 -> x0, waiting for transfers between devices: 2.36 us -> none  [per_device(): roots = lax.all_to_all(fan, 'branch', 0, 0, tiled=True)]
    ppermute x1, starting transfers between devices: 3.95 us -> 1.92 us  [per_device(): before = lax.ppermute(rows, ring, [(i, i + 1) for i in range(last)])]
    ppermute x1, starting transfers between devices: 9.04 us -> 11.1 us  [per_device(): after = lax.ppermute(rows, ring, [(i + 1, i) for i in range(last)])]
    all_to_all x1, waiting for transfers between devices: 6.74 us -> 5.1 us  [per_device(): got = lax.all_to_all(sent, 'leaf', 0, 0, tiled=True)]
    pallas_call x2 -> x3, Pallas kernels: 5.57 us -> 4 us  [the longest x1 2.27 us: up_call(): pl.pallas_call(up_kernel, out_shape=[pltpu.VMEM((2, RHS, LEAVES * R), bf1...]
    all_to_all x1, starting transfers between devices: 6.14 us -> 7 us  [per_device(): got = lax.all_to_all(sent, 'leaf', 0, 0, tiled=True)]
  transfers between devices with their start and end apart: 4 -> 3, of which waited for: 2 -> 1; matrix products, arithmetic and copies ran while one was open for 0% -> 0% of each run, Pallas kernels for 17% -> 16%
where the time goes in v4:
time: 45.6 us; the launch traced here: 44.9 us
  starting transfers between devices  20 us (44%)
  Pallas kernels  10.5 us (23%)
  blocking collectives  9.22 us (20%)
  waiting for transfers between devices  5.1 us (11%)
    ppermute x1, starting transfers between devices, per_device(): after = lax.ppermute(rows, ring, [(i + 1, i) for i in range(last)])  11.1 us
    all_to_all x1, blocking collectives, per_device(): roots = lax.all_to_all(fan, 'branch', 0, 0, tiled=True)  9.22 us
    all_to_all x1, starting transfers between devices, per_device(): got = lax.all_to_all(sent, 'leaf', 0, 0, tiled=True)  7 us
    all_to_all x1, waiting for transfers between devices, per_device(): got = lax.all_to_all(sent, 'leaf', 0, 0, tiled=True)  5.1 us
    pallas_call x1, Pallas kernels, local_call(): pl.pallas_call(local_kernel, out_shape=pltpu.VMEM((2, RHS, LEAVES * R), f...  4.49 us
    pallas_call x1, Pallas kernels, up_call(): pl.pallas_call(up_kernel, out_shape=[pltpu.VMEM((2, RHS, LEAVES * R), bf1...  2.27 us
    ppermute x1, starting transfers between devices, per_device(): before = lax.ppermute(rows, ring, [(i, i + 1) for i in range(last)])  1.92 us
    pallas_call x1, Pallas kernels, prep_call(): pl.pallas_call(prep_kernel, out_shape=[pltpu.VMEM((2 * R, (DEPTH + 1) * 2...  1.63 us
  transfers between devices with their start and end apart: 3, of which 1 were waited for; matrix products, arithmetic and copies ran while one was open for 0% of the time, Pallas kernels for 16%

profile of v4, /device:TPU:1, one launch (start us, length us, event | category | flops | bytes accessed | tf_op | source)
XLA Modules:
  0.0 44.9 jit_solution(14046153734704650820)
XLA Ops:
  0.0 2.3 %up.1 = (bf16[2,16,512]{2,1,0:T(8,128)(2,1)S(1)}, bf16[14,32,64]{2,1,0:T(8,128)(2,1)S(1)}, bf16[5,16,128]{2,1,0:T(8,128)(2,1)S(1)}, bf16[8,16,128]{2,1,0:T(8,128...) custom-call(bf16[2,16,512]{2,1,0:T(8,128)(2,1)} %values.1, bf16[8,64,64]{2,1,0:T(8,128)(2,1)} %basis.5, ...), custom_call_target="tpu_custom_call" | custom-call | tf_op jit(solution)/shard_map/up/pallas_call | solution.py:107
  2.3 0.1 pack.1.own
  2.4 11.1 %collective-permute-start.1 = (bf16[22,16,128]{2,1,0:T(8,128)(2,1)S(1)}, bf16[22,16,128]{2,1,0:T(8,128)(2,1)S(1)}, u32[]{:S(2)}, u32[]{:S(2)}) collective-permute-start(bf16[22,16,128]{2,1,0:T(8,128)(2,1)S(1)} %pack.1.own), channel_id=1, source_target_pairs={{1,0},{2,1},{3,2},{4,3},{5,4},{6,5},{7,6},{8,7},{9,8},{10,9},{11,1... | collective-permute-start | bytes 270344 | tf_op jit(solution)/shard_map/ppermute | solution.py:423
  13.5 1.9 %collective-permute-start = (bf16[22,16,128]{2,1,0:T(8,128)(2,1)S(1)}, bf16[22,16,128]{2,1,0:T(8,128)(2,1)S(1)}, u32[]{:S(2)}, u32[]{:S(2)}) collective-permute-start(bf16[22,16,128]{2,1,0:T(8,128)(2,1)S(1)} %pack.1.own), channel_id=1, source_target_pairs={{0,1},{1,2},{2,3},{3,4},{4,5},{5,6},{6,7},{7,8},{8,9},{9,10},{10,1... | collective-permute-start | bytes 270344 | tf_op jit(solution)/shard_map/ppermute | solution.py:422
  15.4 9.2 %all_to_all.10.roots = bf16[8,16,128]{2,1,0:T(8,128)(2,1)S(1)} all-to-all(bf16[8,16,128]{2,1,0:T(8,128)(2,1)S(1)} %get-tuple-element.16), channel_id=1, replica_groups=mesh['branch'=8,'leaf'=32] {'branch'}, dimensions={0} | all-to-all | bytes 65536 | tf_op jit(solution)/shard_map/all_to_all | solution.py:418
  24.6 1.0 %mid.1 = bf16[32,2,16,128]{3,2,1,0:T(8,128)(2,1)} custom-call(bf16[8,16,128]{2,1,0:T(8,128)(2,1)S(1)} %all_to_all.10.roots, bf16[2,1,7,64,64]{4,3,2,1,0:T(8,128)(2,1)S(1)} %get-tuple-element.17.tops, bf16[5,16,128]{2,1,0:T(8,128)(2,1)S(1)} %get-tuple-element.18.chain), custom_call_target="tpu_custom_call" | custom-call | tf_op jit(solution)/shard_map/mid/pallas_call | solution.py:234
  25.6 0.0 collective-permute-done.1.after
  25.6 0.0 collective-permute-done.before
  25.6 7.0 %all-to-all-start.1 = ((bf16[32,2,16,128]{3,2,1,0:T(8,128)(2,1)}), bf16[32,2,16,128]{3,2,1,0:T(8,128)(2,1)S(1)}, u32[]{:S(2)}, u32[]{:S(2)}) async-start(bf16[32,2,16,128]{3,2,1,0:T(8,128)(2,1)} %mid.1), calls=%async_computation.1 | async-start | bytes 524288 | tf_op jit(solution)/shard_map/all_to_all | solution.py:426
  32.6 1.6 %prep.1 = (bf16[128,768]{1,0:T(8,128)(2,1)S(1)}, bf16[1024,128]{1,0:T(8,128)(2,1)S(1)}) custom-call(bf16[2,1,62,64,64]{4,3,2,1,0:T(8,128)(2,1)} %couple.1, bf16[5,64,64]{2,1,0:T(8,128)(2,1)S(1)} %get-tuple-element.22.downs, bf16[8,64,64]{2,1,0:T(8,128)(2,1)} %basis.5, bf16[14,64,64]{2,1,0:T(8,128)(2,1)} %transfer.5), custom_call_target="tpu_custom_call" | custom-call | flops 100000000 | bytes 4000000 | tf_op jit(solution)/shard_map/prep/pallas_call | solution.py:194
  34.3 4.5 %local.1.base = f32[2,16,512]{2,1,0:T(8,128)S(1)} custom-call(bf16[22,16,128]{2,1,0:T(8,128)(2,1)S(1)} %pack.1.own, bf16[22,16,128]{2,1,0:T(8,128)(2,1)S(1)} %collective-permute-done.before, bf16[22,16,128]{2,1,0:T(8,128)(2,1)S(1)} %collective-permute-done.1.after, bf16[2,14,12,64,64]{4,3,2,1,0:T(8,128)(2,1)} %coupling.1, bf16[2,8,12,64,64]{4,3,2,1,0:T(8,128)(2,1)} %near.1, ...), custom_call_target="tpu_custom_call" | custom-call | flops 100000000 | bytes 20000000 | tf_op jit(solution)/shard_map/local/pallas_call | solution.py:344
  38.8 5.1 %all-to-all-done.1.got = bf16[32,2,16,128]{3,2,1,0:T(8,128)(2,1)S(1)} async-done(((bf16[32,2,16,128]{3,2,1,0:T(8,128)(2,1)}), bf16[32,2,16,128]{3,2,1,0:T(8,128)(2,1)S(1)}, u32[]{:S(2)}, u32[]{:S(2)}) %all-to-all-start.1) | async-done | bytes 262176 | tf_op jit(solution)/shard_map/all_to_all | solution.py:426
  43.9 1.0 %final.1 = f32[2,16,512]{2,1,0:T(8,128)} custom-call(bf16[32,2,16,128]{3,2,1,0:T(8,128)(2,1)S(1)} %all-to-all-done.1.got, bf16[128,768]{1,0:T(8,128)(2,1)S(1)} %get-tuple-element.23.fold, bf16[1024,128]{1,0:T(8,128)(2,1)S(1)} %get-tuple-element.24.leafs, f32[2,16,512]{2,1,0:T(8,128)S(1)} %local.1.base), custom_call_target="tpu_custom_call" | custom-call | tf_op jit(solution)/shard_map/final/pallas_call | solution.py:393
Async XLA Ops:
  2.4 23.3 %collective-permute-start.1 = (bf16[22,16,128]{2,1,0:T(8,128)(2,1)S(1)}, bf16[22,16,128]{2,1,0:T(8,128)(2,1)S(1)}, u32[]{:S(2)}, u32[]{:S(2)}) collective-permute-start(bf16[22,16,128]{2,1,0:T(8,128)(2,1)S(1)} %pack.1.own), channel_id=1, source_target_pairs={{1,0},{2,1},{3,2},{4,3},{5,4},{6,5},{7,6},{8,7},{9,8},{10,9},{11,1... | collective-permute-start | bytes 270344 | tf_op jit(solution)/shard_map/ppermute | solution.py:423
  13.5 12.2 %collective-permute-start = (bf16[22,16,128]{2,1,0:T(8,128)(2,1)S(1)}, bf16[22,16,128]{2,1,0:T(8,128)(2,1)S(1)}, u32[]{:S(2)}, u32[]{:S(2)}) collective-permute-start(bf16[22,16,128]{2,1,0:T(8,128)(2,1)S(1)} %pack.1.own), channel_id=1, source_target_pairs={{0,1},{1,2},{2,3},{3,4},{4,5},{5,6},{6,7},{7,8},{8,9},{9,10},{10,1... | collective-permute-start | bytes 270344 | tf_op jit(solution)/shard_map/ppermute | solution.py:422
  25.6 18.2 %all-to-all-start.1 = ((bf16[32,2,16,128]{3,2,1,0:T(8,128)(2,1)}), bf16[32,2,16,128]{3,2,1,0:T(8,128)(2,1)S(1)}, u32[]{:S(2)}, u32[]{:S(2)}) async-start(bf16[32,2,16,128]{3,2,1,0:T(8,128)(2,1)} %mid.1), calls=%async_computation.1 | async-start | bytes 524288 | tf_op jit(solution)/shard_map/all_to_all | solution.py:426

commit v5 on v4

--- a/solution.py
+++ b/solution.py
@@ -242,7 +242,7 @@
 
 
 def local_kernel(
-    own, before, after, coupling, near, coupling_source, near_source, transfer, basis,
+    own, even, odd, coupling, near, coupling_source, near_source, transfer, basis,
     base, wide, sums, cells, cou, nea, cosrc, nesrc, tra, bas, sem,
 ):
     smalls = [
@@ -261,7 +261,8 @@
     for copy in smalls[:2] + bigs + smalls[2:]:
         copy.start()
     left = lax.broadcasted_iota(jnp.int32, (RHS, 2 * R), 1) < R
-    for part, ref in enumerate((before, own, after)):
+    here = jnp.bitwise_and(lax.axis_index("leaf"), 1)
+    for part, ref in ((1, own), (2 - 2 * here, even), (2 * here, odd)):
         for row in range(ROWS):
             v = ref[row]
             s = turned(v)
@@ -340,7 +341,7 @@
             base[g, :, pl.ds(pair * 2 * R, 2 * R)] = both[g * RHS : (g + 1) * RHS]
 
 
-def local_call(own, before, after, coupling_source, near_source, coupling, near, transfer, basis):
+def local_call(own, even, odd, coupling_source, near_source, coupling, near, transfer, basis):
     return pl.pallas_call(
         local_kernel,
         out_shape=pltpu.VMEM((2, RHS, LEAVES * R), f32),
@@ -364,7 +365,7 @@
         ),
         name="local",
     )(
-        own, before, after,
+        own, even, odd,
         *hbm(coupling, near, coupling_source, near_source, transfer, basis),
     )
 
@@ -416,17 +417,20 @@
         values, leaf_basis, transfer, upper_transfer, top_coupling
     )
     roots = lax.all_to_all(fan, "branch", 0, 0, tiled=True)
+    fold, leafs = prep_call(upper_coupling, downs, leaf_basis, transfer)
     rows = pack_call(vals, coefs)
-    last = N_BRANCH * N_LEAF - 1
+    count = N_BRANCH * N_LEAF
     ring = ("branch", "leaf")
-    before = lax.ppermute(rows, ring, [(i, i + 1) for i in range(last)])
-    after = lax.ppermute(rows, ring, [(i + 1, i) for i in range(last)])
+    even = lax.ppermute(rows, ring, [(i, i ^ 1) for i in range(count)])
+    odd = lax.ppermute(
+        rows, ring, [(i, ((i + 1) ^ 1) - 1) for i in range(1, count - 1)]
+    )
+    roots, fold, leafs = lax.optimization_barrier((roots, fold, leafs))
     sent = mid_call(roots, tops, chain)
-    sent, before, after = lax.optimization_barrier((sent, before, after))
+    sent, even, odd = lax.optimization_barrier((sent, even, odd))
     got = lax.all_to_all(sent, "leaf", 0, 0, tiled=True)
-    fold, leafs = prep_call(upper_coupling, downs, leaf_basis, transfer)
     base = local_call(
-        rows, before, after, coupling_source, near_source, local_coupling, near_field,
+        rows, even, odd, coupling_source, near_source, local_coupling, near_field,
         transfer, leaf_basis,
     )
     return final_call(got, fold, leafs, base)

time: 45.6 us -> 42.9 us (0.941)
  blocking collectives: 9.22 us -> 0 us
  waiting for transfers between devices: 5.1 us -> 9.81 us
  starting transfers between devices: 20 us -> 21.2 us
  Pallas kernels: 10.5 us -> 11.2 us
    all_to_all x1 -> x0, blocking collectives: 9.22 us -> none  [per_device(): roots = lax.all_to_all(fan, 'branch', 0, 0, tiled=True)]
    all_to_all x0 -> x1, starting transfers between devices: none -> 4.59 us  [per_device(): roots = lax.all_to_all(fan, 'branch', 0, 0, tiled=True)]
    all_to_all x0 -> x1, waiting for transfers between devices: none -> 3.07 us  [per_device(): roots = lax.all_to_all(fan, 'branch', 0, 0, tiled=True)]
    all_to_all x1, starting transfers between devices: 7 us -> 4.6 us  [per_device(): got = lax.all_to_all(sent, 'leaf', 0, 0, tiled=True)]
    all_to_all x1, waiting for transfers between devices: 5.1 us -> 6.73 us  [per_device(): got = lax.all_to_all(sent, 'leaf', 0, 0, tiled=True)]
    ppermute x2, starting transfers between devices: 13 us -> 12 us  [the longest x1 9.85 us: per_device(): lax.ppermute(rows, ring, [(i, (i + 1 ^ 1) - 1) for i in range(1, count -...]
    pallas_call x1, Pallas kernels: 2.27 us -> 2.89 us  [up_call(): pl.pallas_call(up_kernel, out_shape=[pltpu.VMEM((2, RHS, LEAVES * R), bf1...]
  transfers between devices with their start and end apart: 3 -> 4, of which waited for: 1 -> 2; matrix products, arithmetic and copies ran while one was open for 0% -> 0% of each run, Pallas kernels for 16% -> 17%
where the time goes in v5:
time: 42.9 us; the launch traced here: 42.2 us
  starting transfers between devices  21.2 us (49%)
  Pallas kernels  11.2 us (26%)
  waiting for transfers between devices  9.81 us (23%)
    ppermute x1, starting transfers between devices, per_device(): lax.ppermute(rows, ring, [(i, (i + 1 ^ 1) - 1) for i in range(1, count -...  9.85 us
    all_to_all x1, waiting for transfers between devices, per_device(): got = lax.all_to_all(sent, 'leaf', 0, 0, tiled=True)  6.73 us
    all_to_all x1, starting transfers between devices, per_device(): got = lax.all_to_all(sent, 'leaf', 0, 0, tiled=True)  4.6 us
    all_to_all x1, starting transfers between devices, per_device(): roots = lax.all_to_all(fan, 'branch', 0, 0, tiled=True)  4.59 us
    pallas_call x1, Pallas kernels, local_call(): pl.pallas_call(local_kernel, out_shape=pltpu.VMEM((2, RHS, LEAVES * R), f...  4.5 us
    all_to_all x1, waiting for transfers between devices, per_device(): roots = lax.all_to_all(fan, 'branch', 0, 0, tiled=True)  3.07 us
    pallas_call x1, Pallas kernels, up_call(): pl.pallas_call(up_kernel, out_shape=[pltpu.VMEM((2, RHS, LEAVES * R), bf1...  2.89 us
    ppermute x1, starting transfers between devices, per_device(): even = lax.ppermute(rows, ring, [(i, i ^ 1) for i in range(count)])  2.13 us
  transfers between devices with their start and end apart: 4, of which 2 were waited for; matrix products, arithmetic and copies ran while one was open for 0% of the time, Pallas kernels for 17%

profile of v5, /device:TPU:1, one launch (start us, length us, event | category | flops | bytes accessed | tf_op | source)
XLA Modules:
  0.0 42.2 jit_solution(17826502672157472869)
XLA Ops:
  0.0 2.9 %up.1 = (bf16[2,16,512]{2,1,0:T(8,128)(2,1)S(1)}, bf16[14,32,64]{2,1,0:T(8,128)(2,1)S(1)}, bf16[5,16,128]{2,1,0:T(8,128)(2,1)S(1)}, bf16[8,16,128]{2,1,0:T(8,128...) custom-call(bf16[2,16,512]{2,1,0:T(8,128)(2,1)} %values.1, bf16[8,64,64]{2,1,0:T(8,128)(2,1)} %basis.5, ...), custom_call_target="tpu_custom_call" | custom-call | tf_op jit(solution)/shard_map/up/pallas_call | solution.py:107
  2.9 0.1 pack.1.own
  3.0 2.1 %collective-permute-start = (bf16[22,16,128]{2,1,0:T(8,128)(2,1)S(1)}, bf16[22,16,128]{2,1,0:T(8,128)(2,1)S(1)}, u32[]{:S(2)}, u32[]{:S(2)}) collective-permute-start(bf16[22,16,128]{2,1,0:T(8,128)(2,1)S(1)} %pack.1.own), channel_id=1, source_target_pairs={{0,1},{1,0},{2,3},{3,2},{4,5},{5,4},{6,7},{7,6},{8,9},{9,8},{10,11... | collective-permute-start | bytes 270344 | tf_op jit(solution)/shard_map/ppermute | solution.py:424
  5.1 9.8 %collective-permute-start.1 = (bf16[22,16,128]{2,1,0:T(8,128)(2,1)S(1)}, bf16[22,16,128]{2,1,0:T(8,128)(2,1)S(1)}, u32[]{:S(2)}, u32[]{:S(2)}) collective-permute-start(bf16[22,16,128]{2,1,0:T(8,128)(2,1)S(1)} %pack.1.own), channel_id=1, source_target_pairs={{1,2},{2,1},{3,4},{4,3},{5,6},{6,5},{7,8},{8,7},{9,10},{10,9},{11,... | collective-permute-start | bytes 270344 | tf_op jit(solution)/shard_map/ppermute | solution.py:425
  15.0 4.6 %all-to-all-start = ((bf16[8,16,128]{2,1,0:T(8,128)(2,1)}), bf16[8,16,128]{2,1,0:T(8,128)(2,1)S(1)}, u32[]{:S(2)}, u32[]{:S(2)}) async-start(bf16[8,16,128]{2,1,0:T(8,128)(2,1)} %get-tuple-element.19), calls=%async_computation | async-start | bytes 65536 | tf_op jit(solution)/shard_map/all_to_all | solution.py:419
  19.6 1.6 %prep.1 = (bf16[128,768]{1,0:T(8,128)(2,1)S(1)}, bf16[1024,128]{1,0:T(8,128)(2,1)S(1)}) custom-call(bf16[2,1,62,64,64]{4,3,2,1,0:T(8,128)(2,1)} %couple.1, bf16[5,64,64]{2,1,0:T(8,128)(2,1)S(1)} %get-tuple-element.20.downs, bf16[8,64,64]{2,1,0:T(8,128)(2,1)} %basis.5, bf16[14,64,64]{2,1,0:T(8,128)(2,1)} %transfer.5), custom_call_target="tpu_custom_call" | custom-call | flops 100000000 | bytes 4000000 | tf_op jit(solution)/shard_map/prep/pallas_call | solution.py:194
  21.2 3.1 %all-to-all-done.roots = bf16[8,16,128]{2,1,0:T(8,128)(2,1)S(1)} async-done(((bf16[8,16,128]{2,1,0:T(8,128)(2,1)}), bf16[8,16,128]{2,1,0:T(8,128)(2,1)S(1)}, u32[]{:S(2)}, u32[]{:S(2)}) %all-to-all-start) | async-done | bytes 32800 | tf_op jit(solution)/shard_map/all_to_all | solution.py:419
  24.3 1.0 %mid.1 = bf16[32,2,16,128]{3,2,1,0:T(8,128)(2,1)} custom-call(bf16[8,16,128]{2,1,0:T(8,128)(2,1)S(1)} %all-to-all-done.roots, bf16[2,1,7,64,64]{4,3,2,1,0:T(8,128)(2,1)S(1)} %get-tuple-element.24.tops, bf16[5,16,128]{2,1,0:T(8,128)(2,1)S(1)} %get-tuple-element.25.chain), custom_call_target="tpu_custom_call" | custom-call | tf_op jit(solution)/shard_map/mid/pallas_call | solution.py:234
  25.3 0.0 collective-permute-done.even
  25.3 0.0 collective-permute-done.1.odd
  25.3 4.6 %all-to-all-start.1 = ((bf16[32,2,16,128]{3,2,1,0:T(8,128)(2,1)}), bf16[32,2,16,128]{3,2,1,0:T(8,128)(2,1)S(1)}, u32[]{:S(2)}, u32[]{:S(2)}) async-start(bf16[32,2,16,128]{3,2,1,0:T(8,128)(2,1)} %mid.1), calls=%async_computation.1 | async-start | bytes 524288 | tf_op jit(solution)/shard_map/all_to_all | solution.py:431
  29.9 4.5 %local.1.base = f32[2,16,512]{2,1,0:T(8,128)S(1)} custom-call(bf16[22,16,128]{2,1,0:T(8,128)(2,1)S(1)} %pack.1.own, bf16[22,16,128]{2,1,0:T(8,128)(2,1)S(1)} %collective-permute-done.even, bf16[22,16,128]{2,1,0:T(8,128)(2,1)S(1)} %collective-permute-done.1.odd, bf16[2,14,12,64,64]{4,3,2,1,0:T(8,128)(2,1)} %coupling.1, bf16[2,8,12,64,64]{4,3,2,1,0:T(8,128)(2,1)} %near.1, ...), custom_call_target="tpu_custom_call" | custom-call | flops 100000000 | bytes 20000000 | tf_op jit(solution)/shard_map/local/pallas_call | solution.py:345
  34.4 6.7 %all-to-all-done.1.got = bf16[32,2,16,128]{3,2,1,0:T(8,128)(2,1)S(1)} async-done(((bf16[32,2,16,128]{3,2,1,0:T(8,128)(2,1)}), bf16[32,2,16,128]{3,2,1,0:T(8,128)(2,1)S(1)}, u32[]{:S(2)}, u32[]{:S(2)}) %all-to-all-start.1) | async-done | bytes 262176 | tf_op jit(solution)/shard_map/all_to_all | solution.py:431
  41.2 1.0 %final.1 = f32[2,16,512]{2,1,0:T(8,128)} custom-call(bf16[32,2,16,128]{3,2,1,0:T(8,128)(2,1)S(1)} %all-to-all-done.1.got, bf16[128,768]{1,0:T(8,128)(2,1)S(1)} %get-tuple-element.29.fold, bf16[1024,128]{1,0:T(8,128)(2,1)S(1)} %get-tuple-element.30.leafs, f32[2,16,512]{2,1,0:T(8,128)S(1)} %local.1.base), custom_call_target="tpu_custom_call" | custom-call | tf_op jit(solution)/shard_map/final/pallas_call | solution.py:394
Async XLA Ops:
  3.0 22.3 %collective-permute-start = (bf16[22,16,128]{2,1,0:T(8,128)(2,1)S(1)}, bf16[22,16,128]{2,1,0:T(8,128)(2,1)S(1)}, u32[]{:S(2)}, u32[]{:S(2)}) collective-permute-start(bf16[22,16,128]{2,1,0:T(8,128)(2,1)S(1)} %pack.1.own), channel_id=1, source_target_pairs={{0,1},{1,0},{2,3},{3,2},{4,5},{5,4},{6,7},{7,6},{8,9},{9,8},{10,11... | collective-permute-start | bytes 270344 | tf_op jit(solution)/shard_map/ppermute | solution.py:424
  5.1 20.2 %collective-permute-start.1 = (bf16[22,16,128]{2,1,0:T(8,128)(2,1)S(1)}, bf16[22,16,128]{2,1,0:T(8,128)(2,1)S(1)}, u32[]{:S(2)}, u32[]{:S(2)}) collective-permute-start(bf16[22,16,128]{2,1,0:T(8,128)(2,1)S(1)} %pack.1.own), channel_id=1, source_target_pairs={{1,2},{2,1},{3,4},{4,3},{5,6},{6,5},{7,8},{8,7},{9,10},{10,9},{11,... | collective-permute-start | bytes 270344 | tf_op jit(solution)/shard_map/ppermute | solution.py:425
  15.0 9.3 %all-to-all-start = ((bf16[8,16,128]{2,1,0:T(8,128)(2,1)}), bf16[8,16,128]{2,1,0:T(8,128)(2,1)S(1)}, u32[]{:S(2)}, u32[]{:S(2)}) async-start(bf16[8,16,128]{2,1,0:T(8,128)(2,1)} %get-tuple-element.19), calls=%async_computation | async-start | bytes 65536 | tf_op jit(solution)/shard_map/all_to_all | solution.py:419
  25.3 15.8 %all-to-all-start.1 = ((bf16[32,2,16,128]{3,2,1,0:T(8,128)(2,1)}), bf16[32,2,16,128]{3,2,1,0:T(8,128)(2,1)S(1)}, u32[]{:S(2)}, u32[]{:S(2)}) async-start(bf16[32,2,16,128]{3,2,1,0:T(8,128)(2,1)} %mid.1), calls=%async_computation.1 | async-start | bytes 524288 | tf_op jit(solution)/shard_map/all_to_all | solution.py:431

commit v6 on v5

--- a/solution.py
+++ b/solution.py
@@ -152,23 +152,78 @@
     )(vals, coefs)
 
 
-def prep_kernel(couple, downs, basis, transfer, fold, leafs, cou, bas, tra, sem):
+def cast_kernel(upper, couple, chain, pushed, carry, own, sib, cou, sem):
     leaf = lax.axis_index("leaf")
-    copies = [
-        pltpu.make_async_copy(transfer, tra, sem.at[DEPTH]),
-        pltpu.make_async_copy(basis, bas, sem.at[DEPTH + 1]),
-    ]
+    copies = []
     for step in range(DEPTH):
-        copies.append(
-            pltpu.make_async_copy(
-                couple.at[:, 0, upper_index(leaf, step)], cou.at[step], sem.at[step]
-            )
-        )
+        here = upper_index(leaf, step)
+        there = jnp.bitwise_xor(here, 1)
+        copies += [
+            pltpu.make_async_copy(upper.at[0, here], own.at[step], sem.at[3 * step]),
+            pltpu.make_async_copy(upper.at[0, there], sib.at[step], sem.at[3 * step + 1]),
+            pltpu.make_async_copy(couple.at[:, 0, there], cou.at[step], sem.at[3 * step + 2]),
+        ]
     for copy in copies:
         copy.start()
     for copy in copies:
         copy.wait()
     zero = jnp.zeros((R, R), bf16)
+
+    def place(step, mat):
+        carry[pl.ds(2 * step * R, R), :] = jnp.concatenate([mat, zero], axis=1)
+        carry[pl.ds((2 * step + 1) * R, R), :] = jnp.concatenate([zero, mat], axis=1)
+
+    path = own[DEPTH - 1]
+    place(DEPTH - 1, sib[DEPTH - 1])
+    for step in range(DEPTH - 2, -1, -1):
+        place(step, dot(sib[step], path).astype(bf16))
+        path = dot(own[step], path).astype(bf16)
+    place(DEPTH, path)
+    for step in range(DEPTH):
+        v = chain[step]
+        pushed[step] = jnp.concatenate(
+            [dot_nt(v[:, g * R : (g + 1) * R], cou[step, g]) for g in range(2)], axis=1
+        )
+
+
+def cast_call(upper, couple, chain):
+    return pl.pallas_call(
+        cast_kernel,
+        out_shape=[
+            pltpu.VMEM((DEPTH, RHS, 2 * R), f32),
+            pltpu.VMEM(((DEPTH + 1) * 2 * R, 2 * R), bf16),
+        ],
+        in_specs=[ANY, ANY, VMEM],
+        out_specs=[VMEM] * 2,
+        scratch_shapes=[
+            pltpu.VMEM((DEPTH, R, R), bf16),
+            pltpu.VMEM((DEPTH, R, R), bf16),
+            pltpu.VMEM((DEPTH, 2, R, R), bf16),
+            pltpu.SemaphoreType.DMA((3 * DEPTH,)),
+        ],
+        compiler_params=pltpu.CompilerParams(vmem_limit_bytes=8 * MB),
+        cost_estimate=pl.CostEstimate(
+            flops=10**8, bytes_accessed=4 * 10**6, transcendentals=0
+        ),
+        name="cast",
+    )(*hbm(upper, couple), chain)
+
+
+def prep_kernel(downs, basis, transfer, fold, leafs, bas, tra, sem):
+    copies = [
+        pltpu.make_async_copy(transfer, tra, sem.at[0]),
+        pltpu.make_async_copy(basis, bas, sem.at[1]),
+    ]
+    for copy in copies:
+        copy.start()
+    zero = jnp.zeros((R, R), bf16)
+    for step in range(DEPTH - 1):
+        lanes = pl.ds(step * 2 * R, 2 * R)
+        mat = downs[step]
+        fold[pl.ds(0, R), lanes] = jnp.concatenate([mat, zero], axis=1)
+        fold[pl.ds(R, R), lanes] = jnp.concatenate([zero, mat], axis=1)
+    for copy in copies:
+        copy.wait()
     tops2 = [tra[12 + t] for t in range(2)]
     tops1 = [dot(tra[8 + t], tops2[t // 2]).astype(bf16) for t in range(4)]
     tops0 = [dot(tra[t], tops1[t // 2]).astype(bf16) for t in range(8)]
@@ -176,44 +231,32 @@
         full = dot(bas[t], tops0[t]).astype(bf16)
         leafs[pl.ds(t * R, R), :] = jnp.concatenate([full, zero], axis=1)
         leafs[pl.ds((LEAVES + t) * R, R), :] = jnp.concatenate([zero, full], axis=1)
-    for step in range(DEPTH + 1):
-        lanes = pl.ds(step * 2 * R, 2 * R)
-        for g in range(2):
-            if step == DEPTH:
-                mat = downs[DEPTH - 1]
-            elif step == 0:
-                mat = cou[step, g]
-            else:
-                mat = dot(downs[step - 1], cou[step, g]).astype(bf16)
-            pair = [mat, zero] if g == 0 else [zero, mat]
-            fold[pl.ds(g * R, R), lanes] = jnp.concatenate(pair, axis=1)
-
-
-def prep_call(couple, downs, basis, transfer):
-    couple, basis, transfer = hbm(couple, basis, transfer)
+
+
+def prep_call(downs, basis, transfer):
+    basis, transfer = hbm(basis, transfer)
     return pl.pallas_call(
         prep_kernel,
         out_shape=[
-            pltpu.VMEM((2 * R, (DEPTH + 1) * 2 * R), bf16),
+            pltpu.VMEM((2 * R, (DEPTH - 1) * 2 * R), bf16),
             pltpu.VMEM((2 * LEAVES * R, 2 * R), bf16),
         ],
-        in_specs=[ANY, VMEM, ANY, ANY],
+        in_specs=[VMEM, ANY, ANY],
         out_specs=[VMEM] * 2,
         scratch_shapes=[
-            pltpu.VMEM((DEPTH, 2, R, R), bf16),
             pltpu.VMEM((LEAVES, R, R), bf16),
             pltpu.VMEM((LOCAL, R, R), bf16),
-            pltpu.SemaphoreType.DMA((DEPTH + 2,)),
+            pltpu.SemaphoreType.DMA((2,)),
         ],
         compiler_params=pltpu.CompilerParams(vmem_limit_bytes=8 * MB),
         cost_estimate=pl.CostEstimate(
             flops=10**8, bytes_accessed=4 * 10**6, transcendentals=0
         ),
         name="prep",
-    )(couple, downs, basis, transfer)
-
-
-def mid_kernel(roots, tops, chain, out):
+    )(downs, basis, transfer)
+
+
+def mid_kernel(roots, tops, pushed, carry, out):
     leaf = lax.axis_index("leaf")
     branch = lax.axis_index("branch")
     others = [roots[(branch + 1 + i) % N_BRANCH] for i in range(N_BRANCH - 1)]
@@ -224,21 +267,23 @@
         m = jnp.concatenate([tops[g, 0, i] for i in range(N_BRANCH - 1)], axis=1)
         parts.append(dot_nt(v, m))
     part = jnp.concatenate(parts, axis=1).astype(bf16)
-    for i in range(N_LEAF):
-        to = jnp.bitwise_xor(leaf, i)
-        out[to, 0] = chain[max(i.bit_length() - 1, 0)]
-        out[to, 1] = part
-
-
-def mid_call(roots, tops, chain):
+    far = dot_nt(part, carry[...])
+    pieces = [far[:, k * 2 * R : (k + 1) * 2 * R] for k in range(DEPTH + 1)]
+    given = [(pieces[k] + pushed[k]).astype(bf16) for k in range(DEPTH)]
+    out[leaf] = pieces[DEPTH].astype(bf16)
+    for i in range(1, N_LEAF):
+        out[jnp.bitwise_xor(leaf, i)] = given[i.bit_length() - 1]
+
+
+def mid_call(roots, tops, pushed, carry):
     return pl.pallas_call(
         mid_kernel,
-        out_shape=pltpu.VMEM((N_LEAF, 2, RHS, 2 * R), bf16),
-        in_specs=[VMEM] * 3,
+        out_shape=pltpu.VMEM((N_LEAF, RHS, 2 * R), bf16),
+        in_specs=[VMEM] * 4,
         out_specs=VMEM,
         compiler_params=pltpu.CompilerParams(vmem_limit_bytes=8 * MB),
         name="mid",
-    )(roots, tops, chain)
+    )(roots, tops, pushed, carry)
 
 
 def local_kernel(
@@ -372,18 +417,15 @@
 
 def final_kernel(got, fold, leafs, base, out):
     leaf = lax.axis_index("leaf")
+    near = got[leaf].astype(f32) + got[jnp.bitwise_xor(leaf, 1)].astype(f32)
     parts = []
-    for step in range(DEPTH):
+    for step in range(1, DEPTH):
         total = None
         for i in range(1 << step, 2 << step):
-            v = got[jnp.bitwise_xor(leaf, i), 0].astype(f32)
+            v = got[jnp.bitwise_xor(leaf, i)].astype(f32)
             total = v if total is None else total + v
         parts.append(total.astype(bf16))
-    total = got[0, 1].astype(f32)
-    for i in range(1, N_LEAF):
-        total = total + got[i, 1].astype(f32)
-    parts.append(total.astype(bf16))
-    target = dot_nt(jnp.concatenate(parts, axis=1), fold[...]).astype(bf16)
+    target = (near + dot_nt(jnp.concatenate(parts, axis=1), fold[...])).astype(bf16)
     far = dot_nt(target, leafs[...])
     width = LEAVES * R
     for g in range(2):
@@ -417,7 +459,7 @@
         values, leaf_basis, transfer, upper_transfer, top_coupling
     )
     roots = lax.all_to_all(fan, "branch", 0, 0, tiled=True)
-    fold, leafs = prep_call(upper_coupling, downs, leaf_basis, transfer)
+    pushed, carry = cast_call(upper_transfer, upper_coupling, chain)
     rows = pack_call(vals, coefs)
     count = N_BRANCH * N_LEAF
     ring = ("branch", "leaf")
@@ -425,10 +467,11 @@
     odd = lax.ppermute(
         rows, ring, [(i, ((i + 1) ^ 1) - 1) for i in range(1, count - 1)]
     )
-    roots, fold, leafs = lax.optimization_barrier((roots, fold, leafs))
-    sent = mid_call(roots, tops, chain)
+    roots, pushed, carry = lax.optimization_barrier((roots, pushed, carry))
+    sent = mid_call(roots, tops, pushed, carry)
     sent, even, odd = lax.optimization_barrier((sent, even, odd))
     got = lax.all_to_all(sent, "leaf", 0, 0, tiled=True)
+    fold, leafs = prep_call(downs, leaf_basis, transfer)
     base = local_call(
         rows, even, odd, coupling_source, near_source, local_coupling, near_field,
         transfer, leaf_basis,

time: 42.9 us -> 40.8 us (0.951)
  waiting for transfers between devices: 9.81 us -> 6.29 us
  Pallas kernels: 11.2 us -> 12.8 us
    all_to_all x1, waiting for transfers between devices: 6.73 us -> 3.3 us  [per_device(): got = lax.all_to_all(sent, 'leaf', 0, 0, tiled=True)]
    pallas_call x2 -> x3, Pallas kernels: 2.66 us -> 4.39 us  [the longest x1 1.73 us: cast_call(): pl.pallas_call(cast_kernel, out_shape=[pltpu.VMEM((DEPTH, RHS, 2 * R), f3...]
  transfers between devices with their start and end apart: 4 -> 4, of which waited for: 2 -> 2; matrix products, arithmetic and copies ran while one was open for 0% -> 0% of each run, Pallas kernels for 17% -> 22%
where the time goes in v6:
time: 40.8 us; the launch traced here: 40.3 us
  starting transfers between devices  21.2 us (52%)
  Pallas kernels  12.8 us (31%)
  waiting for transfers between devices  6.29 us (15%)
    ppermute x1, starting transfers between devices, per_device(): lax.ppermute(rows, ring, [(i, (i + 1 ^ 1) - 1) for i in range(1, count -...  9.85 us
    all_to_all x1, starting transfers between devices, per_device(): got = lax.all_to_all(sent, 'leaf', 0, 0, tiled=True)  4.6 us
    all_to_all x1, starting transfers between devices, per_device(): roots = lax.all_to_all(fan, 'branch', 0, 0, tiled=True)  4.59 us
    pallas_call x1, Pallas kernels, local_call(): pl.pallas_call(local_kernel, out_shape=pltpu.VMEM((2, RHS, LEAVES * R), f...  4.49 us
    all_to_all x1, waiting for transfers between devices, per_device(): got = lax.all_to_all(sent, 'leaf', 0, 0, tiled=True)  3.3 us
    all_to_all x1, waiting for transfers between devices, per_device(): roots = lax.all_to_all(fan, 'branch', 0, 0, tiled=True)  2.98 us
    pallas_call x1, Pallas kernels, up_call(): pl.pallas_call(up_kernel, out_shape=[pltpu.VMEM((2, RHS, LEAVES * R), bf1...  2.89 us
    ppermute x1, starting transfers between devices, per_device(): even = lax.ppermute(rows, ring, [(i, i ^ 1) for i in range(count)])  2.13 us
  transfers between devices with their start and end apart: 4, of which 2 were waited for; matrix products, arithmetic and copies ran while one was open for 0% of the time, Pallas kernels for 22%

profile of v6, /device:TPU:1, one launch (start us, length us, event | category | flops | bytes accessed | tf_op | source)
XLA Modules:
  0.0 40.3 jit_solution(16610695832909143375)
XLA Ops:
  0.0 2.9 %up.1 = (bf16[2,16,512]{2,1,0:T(8,128)(2,1)S(1)}, bf16[14,32,64]{2,1,0:T(8,128)(2,1)S(1)}, bf16[5,16,128]{2,1,0:T(8,128)(2,1)S(1)}, bf16[8,16,128]{2,1,0:T(8,128...) custom-call(bf16[2,16,512]{2,1,0:T(8,128)(2,1)} %values.1, bf16[8,64,64]{2,1,0:T(8,128)(2,1)} %basis.5, ...), custom_call_target="tpu_custom_call" | custom-call | tf_op jit(solution)/shard_map/up/pallas_call | solution.py:107
  2.9 0.1 pack.1.own
  3.0 2.1 %collective-permute-start = (bf16[22,16,128]{2,1,0:T(8,128)(2,1)S(1)}, bf16[22,16,128]{2,1,0:T(8,128)(2,1)S(1)}, u32[]{:S(2)}, u32[]{:S(2)}) collective-permute-start(bf16[22,16,128]{2,1,0:T(8,128)(2,1)S(1)} %pack.1.own), channel_id=1, source_target_pairs={{0,1},{1,0},{2,3},{3,2},{4,5},{5,4},{6,7},{7,6},{8,9},{9,8},{10,11... | collective-permute-start | bytes 270344 | tf_op jit(solution)/shard_map/ppermute | solution.py:466
  5.1 9.8 %collective-permute-start.1 = (bf16[22,16,128]{2,1,0:T(8,128)(2,1)S(1)}, bf16[22,16,128]{2,1,0:T(8,128)(2,1)S(1)}, u32[]{:S(2)}, u32[]{:S(2)}) collective-permute-start(bf16[22,16,128]{2,1,0:T(8,128)(2,1)S(1)} %pack.1.own), channel_id=1, source_target_pairs={{1,2},{2,1},{3,4},{4,3},{5,6},{6,5},{7,8},{8,7},{9,10},{10,9},{11,... | collective-permute-start | bytes 270344 | tf_op jit(solution)/shard_map/ppermute | solution.py:467
  15.0 4.6 %all-to-all-start = ((bf16[8,16,128]{2,1,0:T(8,128)(2,1)}), bf16[8,16,128]{2,1,0:T(8,128)(2,1)S(1)}, u32[]{:S(2)}, u32[]{:S(2)}) async-start(bf16[8,16,128]{2,1,0:T(8,128)(2,1)} %get-tuple-element.21), calls=%async_computation | async-start | bytes 65536 | tf_op jit(solution)/shard_map/all_to_all | solution.py:461
  19.6 1.7 %cast.1 = (f32[5,16,128]{2,1,0:T(8,128)S(1)}, bf16[768,128]{1,0:T(8,128)(2,1)S(1)}) custom-call(bf16[1,62,64,64]{3,2,1,0:T(8,128)(2,1)} %upper.3, bf16[2,1,62,64,64]{4,3,2,1,0:T(8,128)(2,1)} %couple.1, bf16[5,16,128]{2,1,0:T(8,128)(2,1)S(1)} %get-tuple-element.22.chain), custom_call_target="tpu_custom_call" | custom-call | flops 100000000 | bytes 4000000 | tf_op jit(solution)/shard_map/cast/pallas_call | solution.py:190
  21.3 3.0 %all-to-all-done.roots = bf16[8,16,128]{2,1,0:T(8,128)(2,1)S(1)} async-done(((bf16[8,16,128]{2,1,0:T(8,128)(2,1)}), bf16[8,16,128]{2,1,0:T(8,128)(2,1)S(1)}, u32[]{:S(2)}, u32[]{:S(2)}) %all-to-all-start) | async-done | bytes 32800 | tf_op jit(solution)/shard_map/all_to_all | solution.py:461
  24.3 1.1 %mid.1 = bf16[32,16,128]{2,1,0:T(8,128)(2,1)} custom-call(bf16[8,16,128]{2,1,0:T(8,128)(2,1)S(1)} %all-to-all-done.roots, bf16[2,1,7,64,64]{4,3,2,1,0:T(8,128)(2,1)S(1)} %get-tuple-element.26.tops, f32[5,16,128]{2,1,0:T(8,128)S(1)} %get-tuple-element.27.pushed, bf16[768,128]{1,0:T(8,128)(2,1)S(1)} %get-tuple-element.28.carry), custom_call_target="tpu_custom_call" | custom-call | tf_op jit(solution)/shard_map/mid/pallas_call | solution.py:279
  25.4 0.0 collective-permute-done.even
  25.4 0.0 collective-permute-done.1.odd
  25.4 4.6 %all-to-all-start.1 = ((bf16[32,16,128]{2,1,0:T(8,128)(2,1)}), bf16[32,16,128]{2,1,0:T(8,128)(2,1)S(1)}, u32[]{:S(2)}, u32[]{:S(2)}) async-start(bf16[32,16,128]{2,1,0:T(8,128)(2,1)} %mid.1), calls=%async_computation.1 | async-start | bytes 262144 | tf_op jit(solution)/shard_map/all_to_all | solution.py:473
  30.0 1.5 %prep.1 = (bf16[128,512]{1,0:T(8,128)(2,1)S(1)}, bf16[1024,128]{1,0:T(8,128)(2,1)S(1)}) custom-call(bf16[5,64,64]{2,1,0:T(8,128)(2,1)S(1)} %get-tuple-element.32.downs, bf16[8,64,64]{2,1,0:T(8,128)(2,1)} %basis.5, bf16[14,64,64]{2,1,0:T(8,128)(2,1)} %transfer.5), custom_call_target="tpu_custom_call" | custom-call | flops 100000000 | bytes 4000000 | tf_op jit(solution)/shard_map/prep/pallas_call | solution.py:238
  31.6 4.5 %local.1.base = f32[2,16,512]{2,1,0:T(8,128)S(1)} custom-call(bf16[22,16,128]{2,1,0:T(8,128)(2,1)S(1)} %pack.1.own, bf16[22,16,128]{2,1,0:T(8,128)(2,1)S(1)} %collective-permute-done.even, bf16[22,16,128]{2,1,0:T(8,128)(2,1)S(1)} %collective-permute-done.1.odd, bf16[2,14,12,64,64]{4,3,2,1,0:T(8,128)(2,1)} %coupling.1, bf16[2,8,12,64,64]{4,3,2,1,0:T(8,128)(2,1)} %near.1, ...), custom_call_target="tpu_custom_call" | custom-call | flops 100000000 | bytes 20000000 | tf_op jit(solution)/shard_map/local/pallas_call | solution.py:390
  36.1 3.3 %all-to-all-done.1.got = bf16[32,16,128]{2,1,0:T(8,128)(2,1)S(1)} async-done(((bf16[32,16,128]{2,1,0:T(8,128)(2,1)}), bf16[32,16,128]{2,1,0:T(8,128)(2,1)S(1)}, u32[]{:S(2)}, u32[]{:S(2)}) %all-to-all-start.1) | async-done | bytes 131104 | tf_op jit(solution)/shard_map/all_to_all | solution.py:473
  39.4 0.9 %final.1 = f32[2,16,512]{2,1,0:T(8,128)} custom-call(bf16[32,16,128]{2,1,0:T(8,128)(2,1)S(1)} %all-to-all-done.1.got, bf16[128,512]{1,0:T(8,128)(2,1)S(1)} %get-tuple-element.33.fold, bf16[1024,128]{1,0:T(8,128)(2,1)S(1)} %get-tuple-element.34.leafs, f32[2,16,512]{2,1,0:T(8,128)S(1)} %local.1.base), custom_call_target="tpu_custom_call" | custom-call | tf_op jit(solution)/shard_map/final/pallas_call | solution.py:436
Async XLA Ops:
  3.0 22.4 %collective-permute-start = (bf16[22,16,128]{2,1,0:T(8,128)(2,1)S(1)}, bf16[22,16,128]{2,1,0:T(8,128)(2,1)S(1)}, u32[]{:S(2)}, u32[]{:S(2)}) collective-permute-start(bf16[22,16,128]{2,1,0:T(8,128)(2,1)S(1)} %pack.1.own), channel_id=1, source_target_pairs={{0,1},{1,0},{2,3},{3,2},{4,5},{5,4},{6,7},{7,6},{8,9},{9,8},{10,11... | collective-permute-start | bytes 270344 | tf_op jit(solution)/shard_map/ppermute | solution.py:466
  5.1 20.3 %collective-permute-start.1 = (bf16[22,16,128]{2,1,0:T(8,128)(2,1)S(1)}, bf16[22,16,128]{2,1,0:T(8,128)(2,1)S(1)}, u32[]{:S(2)}, u32[]{:S(2)}) collective-permute-start(bf16[22,16,128]{2,1,0:T(8,128)(2,1)S(1)} %pack.1.own), channel_id=1, source_target_pairs={{1,2},{2,1},{3,4},{4,3},{5,6},{6,5},{7,8},{8,7},{9,10},{10,9},{11,... | collective-permute-start | bytes 270344 | tf_op jit(solution)/shard_map/ppermute | solution.py:467
  15.0 9.3 %all-to-all-start = ((bf16[8,16,128]{2,1,0:T(8,128)(2,1)}), bf16[8,16,128]{2,1,0:T(8,128)(2,1)S(1)}, u32[]{:S(2)}, u32[]{:S(2)}) async-start(bf16[8,16,128]{2,1,0:T(8,128)(2,1)} %get-tuple-element.21), calls=%async_computation | async-start | bytes 65536 | tf_op jit(solution)/shard_map/all_to_all | solution.py:461
  25.4 14.0 %all-to-all-start.1 = ((bf16[32,16,128]{2,1,0:T(8,128)(2,1)}), bf16[32,16,128]{2,1,0:T(8,128)(2,1)S(1)}, u32[]{:S(2)}, u32[]{:S(2)}) async-start(bf16[32,16,128]{2,1,0:T(8,128)(2,1)} %mid.1), calls=%async_computation.1 | async-start | bytes 262144 | tf_op jit(solution)/shard_map/all_to_all | solution.py:473

commit v7 on v5

--- a/solution.py
+++ b/solution.py
@@ -49,22 +49,25 @@
 
 
 def up_kernel(
-    values, basis, transfer, upper, top, vals, coefs, chain, fan, downs, tops, bas, tra, upp, sem
+    values, basis, transfer, upper, couple, top,
+    vals, coefs, sent, summit, downs, upp, sib, cou, tops, bas, tra, sem,
 ):
     leaf = lax.axis_index("leaf")
+    here = [upper_index(leaf, step) for step in range(DEPTH)]
     firsts = [
-        pltpu.make_async_copy(
-            upper.at[0, upper_index(leaf, step)], upp.at[step], sem.at[4 + step]
-        )
-        for step in range(DEPTH)
-    ]
-    firsts += [
         pltpu.make_async_copy(values, vals, sem.at[0]),
         pltpu.make_async_copy(basis, bas, sem.at[1]),
         pltpu.make_async_copy(transfer, tra, sem.at[2]),
     ]
-    last = pltpu.make_async_copy(top, tops, sem.at[3])
-    for copy in firsts + [last]:
+    lasts = [pltpu.make_async_copy(top, tops, sem.at[3])]
+    for k in range(DEPTH):
+        there = jnp.bitwise_xor(here[k], 1)
+        firsts.append(pltpu.make_async_copy(upper.at[0, here[k]], upp.at[k], sem.at[4 + 3 * k]))
+        lasts.append(pltpu.make_async_copy(upper.at[0, there], sib.at[k], sem.at[5 + 3 * k]))
+        lasts.append(
+            pltpu.make_async_copy(couple.at[:, 0, here[k]], cou.at[k], sem.at[6 + 3 * k])
+        )
+    for copy in firsts + lasts:
         copy.start()
     for copy in firsts:
         copy.wait()
@@ -92,39 +95,39 @@
         begin += len(level)
         level = merged
     root = level[0]
-    chain[0] = packed(root)
-    for step in range(1, DEPTH + 1):
-        part = packed(dot(root, downs[step - 1]).astype(bf16))
-        if step < DEPTH:
-            chain[step] = part
-        else:
-            for b in range(N_BRANCH):
-                fan[b] = part
-    last.wait()
-
-
-def up_call(values, basis, transfer, upper, top):
+    chain = [packed(root)]
+    for step in range(DEPTH):
+        chain.append(packed(dot(root, downs[step]).astype(bf16)))
+    summit[...] = chain[DEPTH]
+    sent[leaf] = chain[0]
+    for i in range(1, N_LEAF):
+        sent[jnp.bitwise_xor(leaf, i)] = chain[i.bit_length() - 1]
+    for copy in lasts:
+        copy.wait()
+
+
+def up_call(values, basis, transfer, upper, couple, top):
     return pl.pallas_call(
         up_kernel,
         out_shape=[
             pltpu.VMEM((2, RHS, LEAVES * R), bf16),
             pltpu.VMEM((LOCAL, 2 * RHS, R), bf16),
-            pltpu.VMEM((DEPTH, RHS, 2 * R), bf16),
-            pltpu.VMEM((N_BRANCH, RHS, 2 * R), bf16),
+            pltpu.VMEM((N_LEAF, RHS, 2 * R), bf16),
+            pltpu.VMEM((RHS, 2 * R), bf16),
             pltpu.VMEM((DEPTH, R, R), bf16),
+            pltpu.VMEM((DEPTH, R, R), bf16),
+            pltpu.VMEM((DEPTH, R, R), bf16),
+            pltpu.VMEM((DEPTH, 2, R, R), bf16),
             pltpu.VMEM((2, 1, N_BRANCH - 1, R, R), bf16),
-        ],
-        in_specs=[ANY] * 5,
-        out_specs=[VMEM] * 6,
-        scratch_shapes=[
             pltpu.VMEM((LEAVES, R, R), bf16),
             pltpu.VMEM((LOCAL, R, R), bf16),
-            pltpu.VMEM((DEPTH, R, R), bf16),
-            pltpu.SemaphoreType.DMA((4 + DEPTH,)),
         ],
+        in_specs=[ANY] * 6,
+        out_specs=[VMEM] * 11,
+        scratch_shapes=[pltpu.SemaphoreType.DMA((4 + 3 * DEPTH,))],
         compiler_params=pltpu.CompilerParams(vmem_limit_bytes=8 * MB),
         name="up",
-    )(*hbm(values, basis, transfer, upper, top))
+    )(*hbm(values, basis, transfer, upper, couple, top))
 
 
 def pack_kernel(vals, coefs, rows):
@@ -152,22 +155,36 @@
     )(vals, coefs)
 
 
-def prep_kernel(couple, downs, basis, transfer, fold, leafs, cou, bas, tra, sem):
-    leaf = lax.axis_index("leaf")
-    copies = [
-        pltpu.make_async_copy(transfer, tra, sem.at[DEPTH]),
-        pltpu.make_async_copy(basis, bas, sem.at[DEPTH + 1]),
-    ]
-    for step in range(DEPTH):
-        copies.append(
-            pltpu.make_async_copy(
-                couple.at[:, 0, upper_index(leaf, step)], cou.at[step], sem.at[step]
-            )
-        )
-    for copy in copies:
-        copy.start()
-    for copy in copies:
-        copy.wait()
+def cast_kernel(own, sib, lift):
+    zero = jnp.zeros((R, R), bf16)
+
+    def place(step, mat):
+        lift[pl.ds(2 * step * R, R), :] = jnp.concatenate([mat, zero], axis=1)
+        lift[pl.ds((2 * step + 1) * R, R), :] = jnp.concatenate([zero, mat], axis=1)
+
+    path = own[DEPTH - 1]
+    place(DEPTH - 1, sib[DEPTH - 1])
+    for step in range(DEPTH - 2, -1, -1):
+        place(step, dot(sib[step], path).astype(bf16))
+        if step:
+            path = dot(own[step], path).astype(bf16)
+
+
+def cast_call(own, sib):
+    return pl.pallas_call(
+        cast_kernel,
+        out_shape=pltpu.VMEM((DEPTH * 2 * R, 2 * R), bf16),
+        in_specs=[VMEM] * 2,
+        out_specs=VMEM,
+        compiler_params=pltpu.CompilerParams(vmem_limit_bytes=8 * MB),
+        cost_estimate=pl.CostEstimate(
+            flops=10**8, bytes_accessed=4 * 10**6, transcendentals=0
+        ),
+        name="cast",
+    )(own, sib)
+
+
+def prep_kernel(cou, tops, downs, bas, tra, fold, leafs):
     zero = jnp.zeros((R, R), bf16)
     tops2 = [tra[12 + t] for t in range(2)]
     tops1 = [dot(tra[8 + t], tops2[t // 2]).astype(bf16) for t in range(4)]
@@ -176,69 +193,61 @@
         full = dot(bas[t], tops0[t]).astype(bf16)
         leafs[pl.ds(t * R, R), :] = jnp.concatenate([full, zero], axis=1)
         leafs[pl.ds((LEAVES + t) * R, R), :] = jnp.concatenate([zero, full], axis=1)
-    for step in range(DEPTH + 1):
+    for step in range(DEPTH + N_BRANCH - 1):
         lanes = pl.ds(step * 2 * R, 2 * R)
         for g in range(2):
-            if step == DEPTH:
-                mat = downs[DEPTH - 1]
-            elif step == 0:
+            if step == 0:
                 mat = cou[step, g]
+            elif step < DEPTH:
+                mat = dot(downs[step - 1], cou[step, g]).astype(bf16)
             else:
-                mat = dot(downs[step - 1], cou[step, g]).astype(bf16)
+                mat = dot(downs[DEPTH - 1], tops[g, 0, step - DEPTH]).astype(bf16)
             pair = [mat, zero] if g == 0 else [zero, mat]
             fold[pl.ds(g * R, R), lanes] = jnp.concatenate(pair, axis=1)
 
 
-def prep_call(couple, downs, basis, transfer):
-    couple, basis, transfer = hbm(couple, basis, transfer)
+def prep_call(cou, tops, downs, bas, tra):
     return pl.pallas_call(
         prep_kernel,
         out_shape=[
-            pltpu.VMEM((2 * R, (DEPTH + 1) * 2 * R), bf16),
+            pltpu.VMEM((2 * R, (DEPTH + N_BRANCH - 1) * 2 * R), bf16),
             pltpu.VMEM((2 * LEAVES * R, 2 * R), bf16),
         ],
-        in_specs=[ANY, VMEM, ANY, ANY],
+        in_specs=[VMEM] * 5,
         out_specs=[VMEM] * 2,
-        scratch_shapes=[
-            pltpu.VMEM((DEPTH, 2, R, R), bf16),
-            pltpu.VMEM((LEAVES, R, R), bf16),
-            pltpu.VMEM((LOCAL, R, R), bf16),
-            pltpu.SemaphoreType.DMA((DEPTH + 2,)),
-        ],
         compiler_params=pltpu.CompilerParams(vmem_limit_bytes=8 * MB),
         cost_estimate=pl.CostEstimate(
             flops=10**8, bytes_accessed=4 * 10**6, transcendentals=0
         ),
         name="prep",
-    )(couple, downs, basis, transfer)
-
-
-def mid_kernel(roots, tops, chain, out):
+    )(cou, tops, downs, bas, tra)
+
+
+def mid_kernel(got, summit, lift, parts, fan):
     leaf = lax.axis_index("leaf")
-    branch = lax.axis_index("branch")
-    others = [roots[(branch + 1 + i) % N_BRANCH] for i in range(N_BRANCH - 1)]
-    parts = []
-    for g in range(2):
-        lanes = slice(g * R, (g + 1) * R)
-        v = jnp.concatenate([other[:, lanes] for other in others], axis=1)
-        m = jnp.concatenate([tops[g, 0, i] for i in range(N_BRANCH - 1)], axis=1)
-        parts.append(dot_nt(v, m))
-    part = jnp.concatenate(parts, axis=1).astype(bf16)
-    for i in range(N_LEAF):
-        to = jnp.bitwise_xor(leaf, i)
-        out[to, 0] = chain[max(i.bit_length() - 1, 0)]
-        out[to, 1] = part
-
-
-def mid_call(roots, tops, chain):
+    for step in range(DEPTH):
+        total = None
+        for i in range(1 << step, 2 << step):
+            v = got[jnp.bitwise_xor(leaf, i)].astype(f32)
+            total = v if total is None else total + v
+        parts[:, pl.ds(step * 2 * R, 2 * R)] = total.astype(bf16)
+    root = (dot(parts[...], lift[...]) + summit[...].astype(f32)).astype(bf16)
+    for b in range(N_BRANCH):
+        fan[b] = root
+
+
+def mid_call(got, summit, lift):
     return pl.pallas_call(
         mid_kernel,
-        out_shape=pltpu.VMEM((N_LEAF, 2, RHS, 2 * R), bf16),
+        out_shape=[
+            pltpu.VMEM((RHS, DEPTH * 2 * R), bf16),
+            pltpu.VMEM((N_BRANCH, RHS, 2 * R), bf16),
+        ],
         in_specs=[VMEM] * 3,
-        out_specs=VMEM,
+        out_specs=[VMEM] * 2,
         compiler_params=pltpu.CompilerParams(vmem_limit_bytes=8 * MB),
         name="mid",
-    )(roots, tops, chain)
+    )(got, summit, lift)
 
 
 def local_kernel(
@@ -370,35 +379,26 @@
     )
 
 
-def final_kernel(got, fold, leafs, base, out):
-    leaf = lax.axis_index("leaf")
-    parts = []
-    for step in range(DEPTH):
-        total = None
-        for i in range(1 << step, 2 << step):
-            v = got[jnp.bitwise_xor(leaf, i), 0].astype(f32)
-            total = v if total is None else total + v
-        parts.append(total.astype(bf16))
-    total = got[0, 1].astype(f32)
-    for i in range(1, N_LEAF):
-        total = total + got[i, 1].astype(f32)
-    parts.append(total.astype(bf16))
-    target = dot_nt(jnp.concatenate(parts, axis=1), fold[...]).astype(bf16)
+def final_kernel(parts, roots, fold, leafs, base, out):
+    branch = lax.axis_index("branch")
+    others = [roots[(branch + 1 + i) % N_BRANCH] for i in range(N_BRANCH - 1)]
+    row = jnp.concatenate([parts[...]] + others, axis=1)
+    target = dot_nt(row, fold[...]).astype(bf16)
     far = dot_nt(target, leafs[...])
     width = LEAVES * R
     for g in range(2):
         out[g] = base[g] + far[:, g * width : (g + 1) * width]
 
 
-def final_call(got, fold, leafs, base):
+def final_call(parts, roots, fold, leafs, base):
     return pl.pallas_call(
         final_kernel,
         out_shape=jax.ShapeDtypeStruct((2, RHS, LEAVES * R), f32),
-        in_specs=[VMEM] * 4,
+        in_specs=[VMEM] * 5,
         out_specs=VMEM,
         compiler_params=pltpu.CompilerParams(vmem_limit_bytes=8 * MB),
         name="final",
-    )(got, fold, leafs, base)
+    )(parts, roots, fold, leafs, base)
 
 
 def per_device(
@@ -413,11 +413,12 @@
     upper_coupling,
     top_coupling,
 ):
-    vals, coefs, chain, fan, downs, tops = up_call(
-        values, leaf_basis, transfer, upper_transfer, top_coupling
-    )
-    roots = lax.all_to_all(fan, "branch", 0, 0, tiled=True)
-    fold, leafs = prep_call(upper_coupling, downs, leaf_basis, transfer)
+    vals, coefs, sent, summit, downs, own, sib, cou, tops, bas, tra = up_call(
+        values, leaf_basis, transfer, upper_transfer, upper_coupling, top_coupling
+    )
+    got = lax.all_to_all(sent, "leaf", 0, 0, tiled=True)
+    lift = cast_call(own, sib)
+    fold, leafs = prep_call(cou, tops, downs, bas, tra)
     rows = pack_call(vals, coefs)
     count = N_BRANCH * N_LEAF
     ring = ("branch", "leaf")
@@ -425,15 +426,16 @@
     odd = lax.ppermute(
         rows, ring, [(i, ((i + 1) ^ 1) - 1) for i in range(1, count - 1)]
     )
-    roots, fold, leafs = lax.optimization_barrier((roots, fold, leafs))
-    sent = mid_call(roots, tops, chain)
-    sent, even, odd = lax.optimization_barrier((sent, even, odd))
-    got = lax.all_to_all(sent, "leaf", 0, 0, tiled=True)
+    parts, fan = mid_call(got, summit, lift)
+    parts, fan, even, odd, fold, leafs = lax.optimization_barrier(
+        (parts, fan, even, odd, fold, leafs)
+    )
+    roots = lax.all_to_all(fan, "branch", 0, 0, tiled=True)
     base = local_call(
         rows, even, odd, coupling_source, near_source, local_coupling, near_field,
         transfer, leaf_basis,
     )
-    return final_call(got, fold, leafs, base)
+    return final_call(parts, roots, fold, leafs, base)
 
 
 def solution(mesh):

time: 42.9 us -> 38.1 us (0.89); the launches traced: 42.2 us -> 37.8 us
  waiting for transfers between devices: 9.81 us -> 1.83 us
  starting transfers between devices: 21.2 us -> 25.3 us
  Pallas kernels: 11.2 us -> 10.6 us
    all_to_all x1, starting transfers between devices: 4.6 us -> 11.9 us  [per_device(): got = lax.all_to_all(sent, 'leaf', 0, 0, tiled=True)]
    all_to_all x1, waiting for transfers between devices: 6.73 us -> 0.3 us  [per_device(): got = lax.all_to_all(sent, 'leaf', 0, 0, tiled=True)]
    all_to_all x1, waiting for transfers between devices: 3.07 us -> 0.22 us  [per_device(): roots = lax.all_to_all(fan, 'branch', 0, 0, tiled=True)]
    ppermute x1, starting transfers between devices: 9.85 us -> 7.67 us  [per_device(): lax.ppermute(rows, ring, [(i, (i + 1 ^ 1) - 1) for i in range(1, count -...]
    ppermute x1, starting transfers between devices: 2.13 us -> 0.09 us  [per_device(): even = lax.ppermute(rows, ring, [(i, i ^ 1) for i in range(count)])]
    ppermute x1, waiting for transfers between devices: 0.01 us -> 1.13 us  [per_device(): lax.ppermute(rows, ring, [(i, (i + 1 ^ 1) - 1) for i in range(1, count -...]
    all_to_all x1, starting transfers between devices: 4.59 us -> 5.67 us  [per_device(): roots = lax.all_to_all(fan, 'branch', 0, 0, tiled=True)]
    pallas_call x2 -> x3, Pallas kernels: 2.66 us -> 1.97 us  [the longest x1 0.79 us: mid_call(): pl.pallas_call(mid_kernel, out_shape=[pltpu.VMEM((RHS, DEPTH * 2 * R), bf...]
  transfers between devices with their start and end apart: 4 -> 4, of which waited for: 2 -> 4; matrix products, arithmetic and copies ran while one was open for 0% -> 0% of each run, Pallas kernels for 17% -> 17%
where the time goes in v7:
time: 38.1 us; the launch traced here: 37.8 us
  starting transfers between devices  25.3 us (66%)
  Pallas kernels  10.6 us (28%)
  waiting for transfers between devices  1.83 us (5%)
    all_to_all x1, starting transfers between devices, per_device(): got = lax.all_to_all(sent, 'leaf', 0, 0, tiled=True)  11.9 us
    ppermute x1, starting transfers between devices, per_device(): lax.ppermute(rows, ring, [(i, (i + 1 ^ 1) - 1) for i in range(1, count -...  7.67 us
    all_to_all x1, starting transfers between devices, per_device(): roots = lax.all_to_all(fan, 'branch', 0, 0, tiled=True)  5.67 us
    pallas_call x1, Pallas kernels, local_call(): pl.pallas_call(local_kernel, out_shape=pltpu.VMEM((2, RHS, LEAVES * R), f...  4.49 us
    pallas_call x1, Pallas kernels, up_call(): pl.pallas_call(up_kernel, out_shape=[pltpu.VMEM((2, RHS, LEAVES * R), bf1...  2.96 us
    ppermute x1, waiting for transfers between devices, per_device(): lax.ppermute(rows, ring, [(i, (i + 1 ^ 1) - 1) for i in range(1, count -...  1.13 us
    pallas_call x1, Pallas kernels, final_call(): pl.pallas_call(final_kernel, out_shape=jax.ShapeDtypeStruct((2, RHS, LEAV...  1.13 us
    pallas_call x1, Pallas kernels, mid_call(): pl.pallas_call(mid_kernel, out_shape=[pltpu.VMEM((RHS, DEPTH * 2 * R), bf...  0.79 us
  transfers between devices with their start and end apart: 4, of which 4 were waited for; matrix products, arithmetic and copies ran while one was open for 0% of the time, Pallas kernels for 17%

profile of v7, /device:TPU:1, one launch (start us, length us, event | category | flops | bytes accessed | tf_op | source)
XLA Modules:
  0.0 37.8 jit_solution(7994680414576633235)
XLA Ops:
  0.0 3.0 %up.1 = (bf16[2,16,512]{2,1,0:T(8,128)(2,1)S(1)}, bf16[14,32,64]{2,1,0:T(8,128)(2,1)S(1)}, bf16[32,16,128]{2,1,0:T(8,128)(2,1)}, bf16[16,128]{1,0:T(8,128)(2,1)S...) custom-call(bf16[2,16,512]{2,1,0:T(8,128)(2,1)} %values.1, ...), custom_call_target="tpu_custom_call" | custom-call | tf_op jit(solution)/shard_map/up/pallas_call | solution.py:110
  3.0 11.9 %all-to-all-start = ((bf16[32,16,128]{2,1,0:T(8,128)(2,1)}), bf16[32,16,128]{2,1,0:T(8,128)(2,1)S(1)}, u32[]{:S(2)}, u32[]{:S(2)}) async-start(bf16[32,16,128]{2,1,0:T(8,128)(2,1)} %get-tuple-element.26), calls=%async_computation | async-start | bytes 262144 | tf_op jit(solution)/shard_map/all_to_all | solution.py:419
  14.9 0.1 pack.1.own
  14.9 7.7 %collective-permute-start.1 = (bf16[22,16,128]{2,1,0:T(8,128)(2,1)S(1)}, bf16[22,16,128]{2,1,0:T(8,128)(2,1)S(1)}, u32[]{:S(2)}, u32[]{:S(2)}) collective-permute-start(bf16[22,16,128]{2,1,0:T(8,128)(2,1)S(1)} %pack.1.own), channel_id=1, source_target_pairs={{1,2},{2,1},{3,4},{4,3},{5,6},{6,5},{7,8},{8,7},{9,10},{10,9},{11,... | collective-permute-start | bytes 270344 | tf_op jit(solution)/shard_map/ppermute | solution.py:426
  22.6 0.1 collective-permute-start
  22.7 0.6 %cast.1.lift = bf16[640,128]{1,0:T(8,128)(2,1)S(1)} custom-call(bf16[5,64,64]{2,1,0:T(8,128)(2,1)S(1)} %get-tuple-element.28.own, bf16[5,64,64]{2,1,0:T(8,128)(2,1)S(1)} %get-tuple-element.29.sib), custom_call_target="tpu_custom_call" | custom-call | flops 100000000 | bytes 4000000 | tf_op jit(solution)/shard_map/cast/pallas_call | solution.py:174
  23.3 0.6 %prep.1 = (bf16[128,1536]{1,0:T(8,128)(2,1)S(1)}, bf16[1024,128]{1,0:T(8,128)(2,1)S(1)}) custom-call(bf16[5,2,64,64]{3,2,1,0:T(8,128)(2,1)S(1)} %get-tuple-element.34.cou, bf16[2,1,7,64,64]{4,3,2,1,0:T(8,128)(2,1)S(1)} %get-tuple-element.35.tops, bf16[5,64,64]{2,1,0:T(8,128)(2,1)S(1)} %get-tuple-element.36.downs, ...), custom_call_target="tpu_custom_call" | custom-call | flops 100000000 | bytes 4000000 | tf_op jit(solution)/shard_map/prep/pallas_call | solution.py:210
  23.9 0.3 all-to-all-done.got
  24.2 0.8 %mid.1 = (bf16[16,640]{1,0:T(8,128)(2,1)S(1)}, bf16[8,16,128]{2,1,0:T(8,128)(2,1)}) custom-call(bf16[32,16,128]{2,1,0:T(8,128)(2,1)S(1)} %all-to-all-done.got, bf16[16,128]{1,0:T(8,128)(2,1)S(1)} %get-tuple-element.27.summit, bf16[640,128]{1,0:T(8,128)(2,1)S(1)} %cast.1.lift), custom_call_target="tpu_custom_call" | custom-call | tf_op jit(solution)/shard_map/mid/pallas_call | solution.py:240
  25.0 1.1 %collective-permute-done.1.odd = bf16[22,16,128]{2,1,0:T(8,128)(2,1)S(1)} collective-permute-done((bf16[22,16,128]{2,1,0:T(8,128)(2,1)S(1)}, bf16[22,16,128]{2,1,0:T(8,128)(2,1)S(1)}, u32[]{:S(2)}, u32[]{:S(2)}) %collective-permute-start.1) | collective-permute-done | bytes 90144 | tf_op jit(solution)/shard_map/ppermute | solution.py:426
  26.1 0.2 collective-permute-done.even
  26.3 5.7 %all-to-all-start.1 = ((bf16[8,16,128]{2,1,0:T(8,128)(2,1)}), bf16[8,16,128]{2,1,0:T(8,128)(2,1)S(1)}, u32[]{:S(2)}, u32[]{:S(2)}) async-start(bf16[8,16,128]{2,1,0:T(8,128)(2,1)} %get-tuple-element.42), calls=%async_computation.1 | async-start | bytes 65536 | tf_op jit(solution)/shard_map/all_to_all | solution.py:433
  32.0 4.5 %local.1.base = f32[2,16,512]{2,1,0:T(8,128)S(1)} custom-call(bf16[22,16,128]{2,1,0:T(8,128)(2,1)S(1)} %pack.1.own, bf16[22,16,128]{2,1,0:T(8,128)(2,1)S(1)} %collective-permute-done.even, bf16[22,16,128]{2,1,0:T(8,128)(2,1)S(1)} %collective-permute-done.1.odd, bf16[2,14,12,64,64]{4,3,2,1,0:T(8,128)(2,1)} %coupling.1, bf16[2,8,12,64,64]{4,3,2,1,0:T(8,128)(2,1)} %near.1, ...), custom_call_target="tpu_custom_call" | custom-call | flops 100000000 | bytes 20000000 | tf_op jit(solution)/shard_map/local/pallas_call | solution.py:354
  36.5 0.2 all-to-all-done.1.roots
  36.7 1.1 %final.1 = f32[2,16,512]{2,1,0:T(8,128)} custom-call(bf16[16,640]{1,0:T(8,128)(2,1)S(1)} %get-tuple-element.41.parts, bf16[8,16,128]{2,1,0:T(8,128)(2,1)S(1)} %all-to-all-done.1.roots, bf16[128,1536]{1,0:T(8,128)(2,1)S(1)} %get-tuple-element.43.fold, bf16[1024,128]{1,0:T(8,128)(2,1)S(1)} %get-tuple-element.44.leafs, f32[2,16,512]{2,1,0:T(8,128)S(1)} %local.1.base), custom_call_target="tpu_custom_call" | custom-call | tf_op jit(solution)/shard_map/final/pallas_call | solution.py:394
Async XLA Ops:
  3.0 21.2 %all-to-all-start = ((bf16[32,16,128]{2,1,0:T(8,128)(2,1)}), bf16[32,16,128]{2,1,0:T(8,128)(2,1)S(1)}, u32[]{:S(2)}, u32[]{:S(2)}) async-start(bf16[32,16,128]{2,1,0:T(8,128)(2,1)} %get-tuple-element.26), calls=%async_computation | async-start | bytes 262144 | tf_op jit(solution)/shard_map/all_to_all | solution.py:419
  14.9 11.2 %collective-permute-start.1 = (bf16[22,16,128]{2,1,0:T(8,128)(2,1)S(1)}, bf16[22,16,128]{2,1,0:T(8,128)(2,1)S(1)}, u32[]{:S(2)}, u32[]{:S(2)}) collective-permute-start(bf16[22,16,128]{2,1,0:T(8,128)(2,1)S(1)} %pack.1.own), channel_id=1, source_target_pairs={{1,2},{2,1},{3,4},{4,3},{5,6},{6,5},{7,8},{8,7},{9,10},{10,9},{11,... | collective-permute-start | bytes 270344 | tf_op jit(solution)/shard_map/ppermute | solution.py:426
  22.6 3.7 %collective-permute-start = (bf16[22,16,128]{2,1,0:T(8,128)(2,1)S(1)}, bf16[22,16,128]{2,1,0:T(8,128)(2,1)S(1)}, u32[]{:S(2)}, u32[]{:S(2)}) collective-permute-start(bf16[22,16,128]{2,1,0:T(8,128)(2,1)S(1)} %pack.1.own), channel_id=1, source_target_pairs={{0,1},{1,0},{2,3},{3,2},{4,5},{5,4},{6,7},{7,6},{8,9},{9,8},{10,11... | collective-permute-start | bytes 270344 | tf_op jit(solution)/shard_map/ppermute | solution.py:425
  26.3 10.4 %all-to-all-start.1 = ((bf16[8,16,128]{2,1,0:T(8,128)(2,1)}), bf16[8,16,128]{2,1,0:T(8,128)(2,1)S(1)}, u32[]{:S(2)}, u32[]{:S(2)}) async-start(bf16[8,16,128]{2,1,0:T(8,128)(2,1)} %get-tuple-element.42), calls=%async_computation.1 | async-start | bytes 65536 | tf_op jit(solution)/shard_map/all_to_all | solution.py:433

commit v8 on v7

--- a/solution.py
+++ b/solution.py
@@ -427,9 +427,7 @@
         rows, ring, [(i, ((i + 1) ^ 1) - 1) for i in range(1, count - 1)]
     )
     parts, fan = mid_call(got, summit, lift)
-    parts, fan, even, odd, fold, leafs = lax.optimization_barrier(
-        (parts, fan, even, odd, fold, leafs)
-    )
+    parts, fan, even, fold, leafs = lax.optimization_barrier((parts, fan, even, fold, leafs))
     roots = lax.all_to_all(fan, "branch", 0, 0, tiled=True)
     base = local_call(
         rows, even, odd, coupling_source, near_source, local_coupling, near_field,

time: 38.1 us -> 37.7 us (0.990)
  waiting for transfers between devices: 1.83 us -> 0.22 us
  starting transfers between devices: 25.3 us -> 26.5 us
    ppermute x1, starting transfers between devices: 0.09 us -> 1.32 us  [per_device(): even = lax.ppermute(rows, ring, [(i, i ^ 1) for i in range(count)])]
    ppermute x1, waiting for transfers between devices: 1.13 us -> 0.01 us  [per_device(): lax.ppermute(rows, ring, [(i, (i + 1 ^ 1) - 1) for i in range(1, count -...]
    ppermute x1, starting transfers between devices: 7.67 us -> 7.28 us  [per_device(): lax.ppermute(rows, ring, [(i, (i + 1 ^ 1) - 1) for i in range(1, count -...]
  transfers between devices with their start and end apart: 4 -> 4, of which waited for: 4 -> 1; matrix products, arithmetic and copies ran while one was open for 0% -> 0% of each run, Pallas kernels for 17% -> 18%
where the time goes in v8:
time: 37.7 us; the launch traced here: 37.4 us
  starting transfers between devices  26.5 us (70%)
  Pallas kernels  10.6 us (28%)
    all_to_all x1, starting transfers between devices, per_device(): got = lax.all_to_all(sent, 'leaf', 0, 0, tiled=True)  11.9 us
    ppermute x1, starting transfers between devices, per_device(): lax.ppermute(rows, ring, [(i, (i + 1 ^ 1) - 1) for i in range(1, count -...  7.28 us
    all_to_all x1, starting transfers between devices, per_device(): roots = lax.all_to_all(fan, 'branch', 0, 0, tiled=True)  5.99 us
    pallas_call x1, Pallas kernels, local_call(): pl.pallas_call(local_kernel, out_shape=pltpu.VMEM((2, RHS, LEAVES * R), f...  4.49 us
    pallas_call x1, Pallas kernels, up_call(): pl.pallas_call(up_kernel, out_shape=[pltpu.VMEM((2, RHS, LEAVES * R), bf1...  2.96 us
    ppermute x1, starting transfers between devices, per_device(): even = lax.ppermute(rows, ring, [(i, i ^ 1) for i in range(count)])  1.32 us
    pallas_call x1, Pallas kernels, final_call(): pl.pallas_call(final_kernel, out_shape=jax.ShapeDtypeStruct((2, RHS, LEAV...  1.13 us
    pallas_call x1, Pallas kernels, mid_call(): pl.pallas_call(mid_kernel, out_shape=[pltpu.VMEM((RHS, DEPTH * 2 * R), bf...  0.8 us
  transfers between devices with their start and end apart: 4, of which 1 were waited for; matrix products, arithmetic and copies ran while one was open for 0% of the time, Pallas kernels for 18%

profile of v8, /device:TPU:1, one launch (start us, length us, event | category | flops | bytes accessed | tf_op | source)
XLA Modules:
  0.0 37.4 jit_solution(4314883916147060318)
XLA Ops:
  0.0 3.0 %up.1 = (bf16[2,16,512]{2,1,0:T(8,128)(2,1)S(1)}, bf16[14,32,64]{2,1,0:T(8,128)(2,1)S(1)}, bf16[32,16,128]{2,1,0:T(8,128)(2,1)}, bf16[16,128]{1,0:T(8,128)(2,1)S...) custom-call(bf16[2,16,512]{2,1,0:T(8,128)(2,1)} %values.1, ...), custom_call_target="tpu_custom_call" | custom-call | tf_op jit(solution)/shard_map/up/pallas_call | solution.py:110
  3.0 11.9 %all-to-all-start = ((bf16[32,16,128]{2,1,0:T(8,128)(2,1)}), bf16[32,16,128]{2,1,0:T(8,128)(2,1)S(1)}, u32[]{:S(2)}, u32[]{:S(2)}) async-start(bf16[32,16,128]{2,1,0:T(8,128)(2,1)} %get-tuple-element.25), calls=%async_computation | async-start | bytes 262144 | tf_op jit(solution)/shard_map/all_to_all | solution.py:419
  14.9 0.1 pack.1.own
  14.9 1.3 %collective-permute-start = (bf16[22,16,128]{2,1,0:T(8,128)(2,1)S(1)}, bf16[22,16,128]{2,1,0:T(8,128)(2,1)S(1)}, u32[]{:S(2)}, u32[]{:S(2)}) collective-permute-start(bf16[22,16,128]{2,1,0:T(8,128)(2,1)S(1)} %pack.1.own), channel_id=1, source_target_pairs={{0,1},{1,0},{2,3},{3,2},{4,5},{5,4},{6,7},{7,6},{8,9},{9,8},{10,11... | collective-permute-start | bytes 270344 | tf_op jit(solution)/shard_map/ppermute | solution.py:425
  16.3 7.3 %collective-permute-start.1 = (bf16[22,16,128]{2,1,0:T(8,128)(2,1)S(1)}, bf16[22,16,128]{2,1,0:T(8,128)(2,1)S(1)}, u32[]{:S(2)}, u32[]{:S(2)}) collective-permute-start(bf16[22,16,128]{2,1,0:T(8,128)(2,1)S(1)} %pack.1.own), channel_id=1, source_target_pairs={{1,2},{2,1},{3,4},{4,3},{5,6},{6,5},{7,8},{8,7},{9,10},{10,9},{11,... | collective-permute-start | bytes 270344 | tf_op jit(solution)/shard_map/ppermute | solution.py:426
  23.6 0.6 %cast.1.lift = bf16[640,128]{1,0:T(8,128)(2,1)S(1)} custom-call(bf16[5,64,64]{2,1,0:T(8,128)(2,1)S(1)} %get-tuple-element.27.own, bf16[5,64,64]{2,1,0:T(8,128)(2,1)S(1)} %get-tuple-element.28.sib), custom_call_target="tpu_custom_call" | custom-call | flops 100000000 | bytes 4000000 | tf_op jit(solution)/shard_map/cast/pallas_call | solution.py:174
  24.1 0.6 %prep.1 = (bf16[128,1536]{1,0:T(8,128)(2,1)S(1)}, bf16[1024,128]{1,0:T(8,128)(2,1)S(1)}) custom-call(bf16[5,2,64,64]{3,2,1,0:T(8,128)(2,1)S(1)} %get-tuple-element.33.cou, bf16[2,1,7,64,64]{4,3,2,1,0:T(8,128)(2,1)S(1)} %get-tuple-element.34.tops, bf16[5,64,64]{2,1,0:T(8,128)(2,1)S(1)} %get-tuple-element.35.downs, ...), custom_call_target="tpu_custom_call" | custom-call | flops 100000000 | bytes 4000000 | tf_op jit(solution)/shard_map/prep/pallas_call | solution.py:210
  24.7 0.0 all-to-all-done.got
  24.7 0.8 %mid.1 = (bf16[16,640]{1,0:T(8,128)(2,1)S(1)}, bf16[8,16,128]{2,1,0:T(8,128)(2,1)}) custom-call(bf16[32,16,128]{2,1,0:T(8,128)(2,1)S(1)} %all-to-all-done.got, bf16[16,128]{1,0:T(8,128)(2,1)S(1)} %get-tuple-element.26.summit, bf16[640,128]{1,0:T(8,128)(2,1)S(1)} %cast.1.lift), custom_call_target="tpu_custom_call" | custom-call | tf_op jit(solution)/shard_map/mid/pallas_call | solution.py:240
  25.5 0.0 collective-permute-done.even
  25.5 6.0 %all-to-all-start.1 = ((bf16[8,16,128]{2,1,0:T(8,128)(2,1)}), bf16[8,16,128]{2,1,0:T(8,128)(2,1)S(1)}, u32[]{:S(2)}, u32[]{:S(2)}) async-start(bf16[8,16,128]{2,1,0:T(8,128)(2,1)} %get-tuple-element.41), calls=%async_computation.1 | async-start | bytes 65536 | tf_op jit(solution)/shard_map/all_to_all | solution.py:431
  31.5 0.0 collective-permute-done.1.odd
  31.5 4.5 %local.1.base = f32[2,16,512]{2,1,0:T(8,128)S(1)} custom-call(bf16[22,16,128]{2,1,0:T(8,128)(2,1)S(1)} %pack.1.own, bf16[22,16,128]{2,1,0:T(8,128)(2,1)S(1)} %collective-permute-done.even, bf16[22,16,128]{2,1,0:T(8,128)(2,1)S(1)} %collective-permute-done.1.odd, bf16[2,14,12,64,64]{4,3,2,1,0:T(8,128)(2,1)} %coupling.1, bf16[2,8,12,64,64]{4,3,2,1,0:T(8,128)(2,1)} %near.1, ...), custom_call_target="tpu_custom_call" | custom-call | flops 100000000 | bytes 20000000 | tf_op jit(solution)/shard_map/local/pallas_call | solution.py:354
  36.0 0.2 all-to-all-done.1.roots
  36.2 1.1 %final.1 = f32[2,16,512]{2,1,0:T(8,128)} custom-call(bf16[16,640]{1,0:T(8,128)(2,1)S(1)} %get-tuple-element.40.parts, bf16[8,16,128]{2,1,0:T(8,128)(2,1)S(1)} %all-to-all-done.1.roots, bf16[128,1536]{1,0:T(8,128)(2,1)S(1)} %get-tuple-element.42.fold, bf16[1024,128]{1,0:T(8,128)(2,1)S(1)} %get-tuple-element.43.leafs, f32[2,16,512]{2,1,0:T(8,128)S(1)} %local.1.base), custom_call_target="tpu_custom_call" | custom-call | tf_op jit(solution)/shard_map/final/pallas_call | solution.py:394
Async XLA Ops:
  3.0 21.8 %all-to-all-start = ((bf16[32,16,128]{2,1,0:T(8,128)(2,1)}), bf16[32,16,128]{2,1,0:T(8,128)(2,1)S(1)}, u32[]{:S(2)}, u32[]{:S(2)}) async-start(bf16[32,16,128]{2,1,0:T(8,128)(2,1)} %get-tuple-element.25), calls=%async_computation | async-start | bytes 262144 | tf_op jit(solution)/shard_map/all_to_all | solution.py:419
  14.9 10.6 %collective-permute-start = (bf16[22,16,128]{2,1,0:T(8,128)(2,1)S(1)}, bf16[22,16,128]{2,1,0:T(8,128)(2,1)S(1)}, u32[]{:S(2)}, u32[]{:S(2)}) collective-permute-start(bf16[22,16,128]{2,1,0:T(8,128)(2,1)S(1)} %pack.1.own), channel_id=1, source_target_pairs={{0,1},{1,0},{2,3},{3,2},{4,5},{5,4},{6,7},{7,6},{8,9},{9,8},{10,11... | collective-permute-start | bytes 270344 | tf_op jit(solution)/shard_map/ppermute | solution.py:425
  16.3 15.3 %collective-permute-start.1 = (bf16[22,16,128]{2,1,0:T(8,128)(2,1)S(1)}, bf16[22,16,128]{2,1,0:T(8,128)(2,1)S(1)}, u32[]{:S(2)}, u32[]{:S(2)}) collective-permute-start(bf16[22,16,128]{2,1,0:T(8,128)(2,1)S(1)} %pack.1.own), channel_id=1, source_target_pairs={{1,2},{2,1},{3,4},{4,3},{5,6},{6,5},{7,8},{8,7},{9,10},{10,9},{11,... | collective-permute-start | bytes 270344 | tf_op jit(solution)/shard_map/ppermute | solution.py:426
  25.5 10.7 %all-to-all-start.1 = ((bf16[8,16,128]{2,1,0:T(8,128)(2,1)}), bf16[8,16,128]{2,1,0:T(8,128)(2,1)S(1)}, u32[]{:S(2)}, u32[]{:S(2)}) async-start(bf16[8,16,128]{2,1,0:T(8,128)(2,1)} %get-tuple-element.41), calls=%async_computation.1 | async-start | bytes 65536 | tf_op jit(solution)/shard_map/all_to_all | solution.py:431

commit v9 on v8

--- a/solution.py
+++ b/solution.py
@@ -46,6 +46,10 @@
 
 def upper_index(leaf, step):
     return 2 * N_LEAF - 2 * (N_LEAF >> step) + jnp.right_shift(leaf, step)
+
+
+def seat(leaf):
+    return N_LEAF - 1 - leaf
 
 
 def up_kernel(
@@ -99,9 +103,9 @@
     for step in range(DEPTH):
         chain.append(packed(dot(root, downs[step]).astype(bf16)))
     summit[...] = chain[DEPTH]
-    sent[leaf] = chain[0]
+    sent[seat(leaf)] = chain[0]
     for i in range(1, N_LEAF):
-        sent[jnp.bitwise_xor(leaf, i)] = chain[i.bit_length() - 1]
+        sent[seat(jnp.bitwise_xor(leaf, i))] = chain[i.bit_length() - 1]
     for copy in lasts:
         copy.wait()
 
@@ -228,7 +232,7 @@
     for step in range(DEPTH):
         total = None
         for i in range(1 << step, 2 << step):
-            v = got[jnp.bitwise_xor(leaf, i)].astype(f32)
+            v = got[seat(jnp.bitwise_xor(leaf, i))].astype(f32)
             total = v if total is None else total + v
         parts[:, pl.ds(step * 2 * R, 2 * R)] = total.astype(bf16)
     root = (dot(parts[...], lift[...]) + summit[...].astype(f32)).astype(bf16)
@@ -416,7 +420,7 @@
     vals, coefs, sent, summit, downs, own, sib, cou, tops, bas, tra = up_call(
         values, leaf_basis, transfer, upper_transfer, upper_coupling, top_coupling
     )
-    got = lax.all_to_all(sent, "leaf", 0, 0, tiled=True)
+    got = lax.all_to_all(sent, "leaf", 0, 0, axis_index_groups=[list(range(N_LEAF - 1, -1, -1))], tiled=True)
     lift = cast_call(own, sib)
     fold, leafs = prep_call(cou, tops, downs, bas, tra)
     rows = pack_call(vals, coefs)

time: 37.7 us -> 34.5 us (0.915)
  starting transfers between devices: 26.5 us -> 23.3 us
    ppermute x1, starting transfers between devices: 7.28 us -> 4.1 us  [per_device(): lax.ppermute(rows, ring, [(i, (i + 1 ^ 1) - 1) for i in range(1, count -...]
    all_to_all x1, starting transfers between devices: 11.9 us -> 12.6 us  [per_device(): lax.all_to_all(sent, 'leaf', 0, 0, axis_index_groups=[list(range(N_LEAF -...]
    ppermute x1, starting transfers between devices: 1.32 us -> 0.66 us  [per_device(): even = lax.ppermute(rows, ring, [(i, i ^ 1) for i in range(count)])]
  transfers between devices with their start and end apart: 4 -> 4, of which waited for: 1 -> 1; matrix products, arithmetic and copies ran while one was open for 0% -> 0% of each run, Pallas kernels for 18% -> 19%
where the time goes in v9:
time: 34.5 us; the launch traced here: 34.2 us
  starting transfers between devices  23.3 us (68%)
  Pallas kernels  10.6 us (31%)
    all_to_all x1, starting transfers between devices, per_device(): lax.all_to_all(sent, 'leaf', 0, 0, axis_index_groups=[list(range(N_LEAF -...  12.6 us
    all_to_all x1, starting transfers between devices, per_device(): roots = lax.all_to_all(fan, 'branch', 0, 0, tiled=True)  5.93 us
    pallas_call x1, Pallas kernels, local_call(): pl.pallas_call(local_kernel, out_shape=pltpu.VMEM((2, RHS, LEAVES * R), f...  4.49 us
    ppermute x1, starting transfers between devices, per_device(): lax.ppermute(rows, ring, [(i, (i + 1 ^ 1) - 1) for i in range(1, count -...  4.1 us
    pallas_call x1, Pallas kernels, up_call(): pl.pallas_call(up_kernel, out_shape=[pltpu.VMEM((2, RHS, LEAVES * R), bf1...  2.96 us
    pallas_call x1, Pallas kernels, final_call(): pl.pallas_call(final_kernel, out_shape=jax.ShapeDtypeStruct((2, RHS, LEAV...  1.13 us
    pallas_call x1, Pallas kernels, mid_call(): pl.pallas_call(mid_kernel, out_shape=[pltpu.VMEM((RHS, DEPTH * 2 * R), bf...  0.8 us
  transfers between devices with their start and end apart: 4, of which 1 were waited for; matrix products, arithmetic and copies ran while one was open for 0% of the time, Pallas kernels for 19%

profile of v9, /device:TPU:1, one launch (start us, length us, event | category | flops | bytes accessed | tf_op | source)
XLA Modules:
  0.0 34.2 jit_solution(4544250626552353709)
XLA Ops:
  0.0 3.0 %up.1 = (bf16[2,16,512]{2,1,0:T(8,128)(2,1)S(1)}, bf16[14,32,64]{2,1,0:T(8,128)(2,1)S(1)}, bf16[32,16,128]{2,1,0:T(8,128)(2,1)}, bf16[16,128]{1,0:T(8,128)(2,1)S...) custom-call(bf16[2,16,512]{2,1,0:T(8,128)(2,1)} %values.1, ...), custom_call_target="tpu_custom_call" | custom-call | tf_op jit(solution)/shard_map/up/pallas_call | solution.py:114
  3.0 12.6 %all-to-all-start = ((bf16[32,16,128]{2,1,0:T(8,128)(2,1)}), bf16[32,16,128]{2,1,0:T(8,128)(2,1)S(1)}, u32[]{:S(2)}, u32[]{:S(2)}) async-start(bf16[32,16,128]{2,1,0:T(8,128)(2,1)} %get-tuple-element.25), calls=%async_computation | async-start | bytes 262144 | tf_op jit(solution)/shard_map/all_to_all | solution.py:423
  15.6 0.1 pack.1.own
  15.7 0.7 %collective-permute-start = (bf16[22,16,128]{2,1,0:T(8,128)(2,1)S(1)}, bf16[22,16,128]{2,1,0:T(8,128)(2,1)S(1)}, u32[]{:S(2)}, u32[]{:S(2)}) collective-permute-start(bf16[22,16,128]{2,1,0:T(8,128)(2,1)S(1)} %pack.1.own), channel_id=1, source_target_pairs={{0,1},{1,0},{2,3},{3,2},{4,5},{5,4},{6,7},{7,6},{8,9},{9,8},{10,11... | collective-permute-start | bytes 270344 | tf_op jit(solution)/shard_map/ppermute | solution.py:429
  16.3 4.1 %collective-permute-start.1 = (bf16[22,16,128]{2,1,0:T(8,128)(2,1)S(1)}, bf16[22,16,128]{2,1,0:T(8,128)(2,1)S(1)}, u32[]{:S(2)}, u32[]{:S(2)}) collective-permute-start(bf16[22,16,128]{2,1,0:T(8,128)(2,1)S(1)} %pack.1.own), channel_id=1, source_target_pairs={{1,2},{2,1},{3,4},{4,3},{5,6},{6,5},{7,8},{8,7},{9,10},{10,9},{11,... | collective-permute-start | bytes 270344 | tf_op jit(solution)/shard_map/ppermute | solution.py:430
  20.4 0.6 %cast.1.lift = bf16[640,128]{1,0:T(8,128)(2,1)S(1)} custom-call(bf16[5,64,64]{2,1,0:T(8,128)(2,1)S(1)} %get-tuple-element.27.own, bf16[5,64,64]{2,1,0:T(8,128)(2,1)S(1)} %get-tuple-element.28.sib), custom_call_target="tpu_custom_call" | custom-call | flops 100000000 | bytes 4000000 | tf_op jit(solution)/shard_map/cast/pallas_call | solution.py:178
  21.0 0.6 %prep.1 = (bf16[128,1536]{1,0:T(8,128)(2,1)S(1)}, bf16[1024,128]{1,0:T(8,128)(2,1)S(1)}) custom-call(bf16[5,2,64,64]{3,2,1,0:T(8,128)(2,1)S(1)} %get-tuple-element.33.cou, bf16[2,1,7,64,64]{4,3,2,1,0:T(8,128)(2,1)S(1)} %get-tuple-element.34.tops, bf16[5,64,64]{2,1,0:T(8,128)(2,1)S(1)} %get-tuple-element.35.downs, ...), custom_call_target="tpu_custom_call" | custom-call | flops 100000000 | bytes 4000000 | tf_op jit(solution)/shard_map/prep/pallas_call | solution.py:214
  21.6 0.0 all-to-all-done.got
  21.6 0.8 %mid.1 = (bf16[16,640]{1,0:T(8,128)(2,1)S(1)}, bf16[8,16,128]{2,1,0:T(8,128)(2,1)}) custom-call(bf16[32,16,128]{2,1,0:T(8,128)(2,1)S(1)} %all-to-all-done.got, bf16[16,128]{1,0:T(8,128)(2,1)S(1)} %get-tuple-element.26.summit, bf16[640,128]{1,0:T(8,128)(2,1)S(1)} %cast.1.lift), custom_call_target="tpu_custom_call" | custom-call | tf_op jit(solution)/shard_map/mid/pallas_call | solution.py:244
  22.4 0.0 collective-permute-done.even
  22.4 5.9 %all-to-all-start.1 = ((bf16[8,16,128]{2,1,0:T(8,128)(2,1)}), bf16[8,16,128]{2,1,0:T(8,128)(2,1)S(1)}, u32[]{:S(2)}, u32[]{:S(2)}) async-start(bf16[8,16,128]{2,1,0:T(8,128)(2,1)} %get-tuple-element.41), calls=%async_computation.1 | async-start | bytes 65536 | tf_op jit(solution)/shard_map/all_to_all | solution.py:435
  28.4 0.0 collective-permute-done.1.odd
  28.4 4.5 %local.1.base = f32[2,16,512]{2,1,0:T(8,128)S(1)} custom-call(bf16[22,16,128]{2,1,0:T(8,128)(2,1)S(1)} %pack.1.own, bf16[22,16,128]{2,1,0:T(8,128)(2,1)S(1)} %collective-permute-done.even, bf16[22,16,128]{2,1,0:T(8,128)(2,1)S(1)} %collective-permute-done.1.odd, bf16[2,14,12,64,64]{4,3,2,1,0:T(8,128)(2,1)} %coupling.1, bf16[2,8,12,64,64]{4,3,2,1,0:T(8,128)(2,1)} %near.1, ...), custom_call_target="tpu_custom_call" | custom-call | flops 100000000 | bytes 20000000 | tf_op jit(solution)/shard_map/local/pallas_call | solution.py:358
  32.9 0.2 all-to-all-done.1.roots
  33.1 1.1 %final.1 = f32[2,16,512]{2,1,0:T(8,128)} custom-call(bf16[16,640]{1,0:T(8,128)(2,1)S(1)} %get-tuple-element.40.parts, bf16[8,16,128]{2,1,0:T(8,128)(2,1)S(1)} %all-to-all-done.1.roots, bf16[128,1536]{1,0:T(8,128)(2,1)S(1)} %get-tuple-element.42.fold, bf16[1024,128]{1,0:T(8,128)(2,1)S(1)} %get-tuple-element.43.leafs, f32[2,16,512]{2,1,0:T(8,128)S(1)} %local.1.base), custom_call_target="tpu_custom_call" | custom-call | tf_op jit(solution)/shard_map/final/pallas_call | solution.py:398
Async XLA Ops:
  3.0 18.6 %all-to-all-start = ((bf16[32,16,128]{2,1,0:T(8,128)(2,1)}), bf16[32,16,128]{2,1,0:T(8,128)(2,1)S(1)}, u32[]{:S(2)}, u32[]{:S(2)}) async-start(bf16[32,16,128]{2,1,0:T(8,128)(2,1)} %get-tuple-element.25), calls=%async_computation | async-start | bytes 262144 | tf_op jit(solution)/shard_map/all_to_all | solution.py:423
  15.7 6.8 %collective-permute-start = (bf16[22,16,128]{2,1,0:T(8,128)(2,1)S(1)}, bf16[22,16,128]{2,1,0:T(8,128)(2,1)S(1)}, u32[]{:S(2)}, u32[]{:S(2)}) collective-permute-start(bf16[22,16,128]{2,1,0:T(8,128)(2,1)S(1)} %pack.1.own), channel_id=1, source_target_pairs={{0,1},{1,0},{2,3},{3,2},{4,5},{5,4},{6,7},{7,6},{8,9},{9,8},{10,11... | collective-permute-start | bytes 270344 | tf_op jit(solution)/shard_map/ppermute | solution.py:429
  16.3 12.0 %collective-permute-start.1 = (bf16[22,16,128]{2,1,0:T(8,128)(2,1)S(1)}, bf16[22,16,128]{2,1,0:T(8,128)(2,1)S(1)}, u32[]{:S(2)}, u32[]{:S(2)}) collective-permute-start(bf16[22,16,128]{2,1,0:T(8,128)(2,1)S(1)} %pack.1.own), channel_id=1, source_target_pairs={{1,2},{2,1},{3,4},{4,3},{5,6},{6,5},{7,8},{8,7},{9,10},{10,9},{11,... | collective-permute-start | bytes 270344 | tf_op jit(solution)/shard_map/ppermute | solution.py:430
  22.4 10.6 %all-to-all-start.1 = ((bf16[8,16,128]{2,1,0:T(8,128)(2,1)}), bf16[8,16,128]{2,1,0:T(8,128)(2,1)S(1)}, u32[]{:S(2)}, u32[]{:S(2)}) async-start(bf16[8,16,128]{2,1,0:T(8,128)(2,1)} %get-tuple-element.41), calls=%async_computation.1 | async-start | bytes 65536 | tf_op jit(solution)/shard_map/all_to_all | solution.py:435

commit v10 on v9

--- a/solution.py
+++ b/solution.py
@@ -267,11 +267,11 @@
     bigs = []
     for n, (source, into, start, count) in enumerate(
         ((coupling, cou, 8, 6), (coupling, cou, 0, 4), (coupling, cou, 4, 4),
-         (near, nea, 0, 4), (near, nea, 4, 4))
+         (near, nea, 0, 4), (near, nea, 4, 2), (near, nea, 6, 2))
     ):
         span = pl.ds(start, count)
         bigs.append(pltpu.make_async_copy(source.at[:, span], into.at[:, span], sem.at[4 + n]))
-    for copy in smalls[:2] + bigs + smalls[2:]:
+    for copy in smalls + bigs:
         copy.start()
     left = lax.broadcasted_iota(jnp.int32, (RHS, 2 * R), 1) < R
     here = jnp.bitwise_and(lax.axis_index("leaf"), 1)
@@ -336,10 +336,6 @@
     each(functools.partial(far_body, 3, 0), 0, 4)
     bigs[2].wait()
     each(functools.partial(far_body, 3, 0), 4, 4)
-    bigs[3].wait()
-    each(near_body, 0, 4)
-    bigs[4].wait()
-    each(near_body, 4, 4)
     for copy in smalls[2:]:
         copy.wait()
     up2 = [sums[12 + t].astype(bf16) for t in range(2)]
@@ -347,7 +343,15 @@
         (sums[8 + t] + dot_nt(up2[t // 2], tra[8 + t])).astype(bf16) for t in range(4)
     ]
     up0 = [(sums[t] + dot_nt(up1[t // 2], tra[t])).astype(bf16) for t in range(8)]
-    full = [cells[t] + dot_nt(up0[t], bas[t]) for t in range(8)]
+    for t in range(LEAVES):
+        sums[t] = dot_nt(up0[t], bas[t])
+    bigs[3].wait()
+    each(near_body, 0, 4)
+    bigs[4].wait()
+    each(near_body, 4, 2)
+    bigs[5].wait()
+    each(near_body, 6, 2)
+    full = [cells[t] + sums[t] for t in range(LEAVES)]
     for pair in range(LEAVES // 2):
         both = jnp.concatenate([full[2 * pair], full[2 * pair + 1]], axis=1)
         for g in range(2):
@@ -370,7 +374,7 @@
             pltpu.SMEM((LEAVES, LINKS), jnp.int32),
             pltpu.VMEM((LOCAL, R, R), bf16),
             pltpu.VMEM((LEAVES, R, R), bf16),
-            pltpu.SemaphoreType.DMA((9,)),
+            pltpu.SemaphoreType.DMA((10,)),
         ],
         compiler_params=pltpu.CompilerParams(vmem_limit_bytes=24 * MB),
         cost_estimate=pl.CostEstimate(

time: 34.5 us -> 34.6 us (level)
  transfers between devices with their start and end apart: 4 -> 4, of which waited for: 1 -> 0; matrix products, arithmetic and copies ran while one was open for 0% -> 0% of each run, Pallas kernels for 19% -> 20%
where the time goes in v10:
time: 34.6 us; the launch traced here: 34.3 us
  starting transfers between devices  23.3 us (67%)
  Pallas kernels  10.9 us (32%)
    all_to_all x1, starting transfers between devices, per_device(): lax.all_to_all(sent, 'leaf', 0, 0, axis_index_groups=[list(range(N_LEAF -...  12.6 us
    all_to_all x1, starting transfers between devices, per_device(): roots = lax.all_to_all(fan, 'branch', 0, 0, tiled=True)  5.93 us
    pallas_call x1, Pallas kernels, local_call(): pl.pallas_call(local_kernel, out_shape=pltpu.VMEM((2, RHS, LEAVES * R), f...  4.77 us
    ppermute x1, starting transfers between devices, per_device(): lax.ppermute(rows, ring, [(i, (i + 1 ^ 1) - 1) for i in range(1, count -...  4.1 us
    pallas_call x1, Pallas kernels, up_call(): pl.pallas_call(up_kernel, out_shape=[pltpu.VMEM((2, RHS, LEAVES * R), bf1...  2.96 us
    pallas_call x1, Pallas kernels, final_call(): pl.pallas_call(final_kernel, out_shape=jax.ShapeDtypeStruct((2, RHS, LEAV...  1.14 us
    pallas_call x1, Pallas kernels, mid_call(): pl.pallas_call(mid_kernel, out_shape=[pltpu.VMEM((RHS, DEPTH * 2 * R), bf...  0.8 us
  transfers between devices with their start and end apart: 4, of which 0 were waited for; matrix products, arithmetic and copies ran while one was open for 0% of the time, Pallas kernels for 20%

profile of v10, /device:TPU:1, one launch (start us, length us, event | category | flops | bytes accessed | tf_op | source)
XLA Modules:
  0.0 34.3 jit_solution(15138208378685639670)
XLA Ops:
  0.0 3.0 %up.1 = (bf16[2,16,512]{2,1,0:T(8,128)(2,1)S(1)}, bf16[14,32,64]{2,1,0:T(8,128)(2,1)S(1)}, bf16[32,16,128]{2,1,0:T(8,128)(2,1)}, bf16[16,128]{1,0:T(8,128)(2,1)S...) custom-call(bf16[2,16,512]{2,1,0:T(8,128)(2,1)} %values.1, ...), custom_call_target="tpu_custom_call" | custom-call | tf_op jit(solution)/shard_map/up/pallas_call | solution.py:114
  3.0 12.6 %all-to-all-start = ((bf16[32,16,128]{2,1,0:T(8,128)(2,1)}), bf16[32,16,128]{2,1,0:T(8,128)(2,1)S(1)}, u32[]{:S(2)}, u32[]{:S(2)}) async-start(bf16[32,16,128]{2,1,0:T(8,128)(2,1)} %get-tuple-element.25), calls=%async_computation | async-start | bytes 262144 | tf_op jit(solution)/shard_map/all_to_all | solution.py:427
  15.6 0.1 pack.1.own
  15.7 0.7 %collective-permute-start = (bf16[22,16,128]{2,1,0:T(8,128)(2,1)S(1)}, bf16[22,16,128]{2,1,0:T(8,128)(2,1)S(1)}, u32[]{:S(2)}, u32[]{:S(2)}) collective-permute-start(bf16[22,16,128]{2,1,0:T(8,128)(2,1)S(1)} %pack.1.own), channel_id=1, source_target_pairs={{0,1},{1,0},{2,3},{3,2},{4,5},{5,4},{6,7},{7,6},{8,9},{9,8},{10,11... | collective-permute-start | bytes 270344 | tf_op jit(solution)/shard_map/ppermute | solution.py:433
  16.3 4.1 %collective-permute-start.1 = (bf16[22,16,128]{2,1,0:T(8,128)(2,1)S(1)}, bf16[22,16,128]{2,1,0:T(8,128)(2,1)S(1)}, u32[]{:S(2)}, u32[]{:S(2)}) collective-permute-start(bf16[22,16,128]{2,1,0:T(8,128)(2,1)S(1)} %pack.1.own), channel_id=1, source_target_pairs={{1,2},{2,1},{3,4},{4,3},{5,6},{6,5},{7,8},{8,7},{9,10},{10,9},{11,... | collective-permute-start | bytes 270344 | tf_op jit(solution)/shard_map/ppermute | solution.py:434
  20.4 0.6 %cast.1.lift = bf16[640,128]{1,0:T(8,128)(2,1)S(1)} custom-call(bf16[5,64,64]{2,1,0:T(8,128)(2,1)S(1)} %get-tuple-element.27.own, bf16[5,64,64]{2,1,0:T(8,128)(2,1)S(1)} %get-tuple-element.28.sib), custom_call_target="tpu_custom_call" | custom-call | flops 100000000 | bytes 4000000 | tf_op jit(solution)/shard_map/cast/pallas_call | solution.py:178
  21.0 0.6 %prep.1 = (bf16[128,1536]{1,0:T(8,128)(2,1)S(1)}, bf16[1024,128]{1,0:T(8,128)(2,1)S(1)}) custom-call(bf16[5,2,64,64]{3,2,1,0:T(8,128)(2,1)S(1)} %get-tuple-element.33.cou, bf16[2,1,7,64,64]{4,3,2,1,0:T(8,128)(2,1)S(1)} %get-tuple-element.34.tops, bf16[5,64,64]{2,1,0:T(8,128)(2,1)S(1)} %get-tuple-element.35.downs, ...), custom_call_target="tpu_custom_call" | custom-call | flops 100000000 | bytes 4000000 | tf_op jit(solution)/shard_map/prep/pallas_call | solution.py:214
  21.6 0.0 all-to-all-done.got
  21.6 0.8 %mid.1 = (bf16[16,640]{1,0:T(8,128)(2,1)S(1)}, bf16[8,16,128]{2,1,0:T(8,128)(2,1)}) custom-call(bf16[32,16,128]{2,1,0:T(8,128)(2,1)S(1)} %all-to-all-done.got, bf16[16,128]{1,0:T(8,128)(2,1)S(1)} %get-tuple-element.26.summit, bf16[640,128]{1,0:T(8,128)(2,1)S(1)} %cast.1.lift), custom_call_target="tpu_custom_call" | custom-call | tf_op jit(solution)/shard_map/mid/pallas_call | solution.py:244
  22.4 0.0 collective-permute-done.even
  22.4 5.9 %all-to-all-start.1 = ((bf16[8,16,128]{2,1,0:T(8,128)(2,1)}), bf16[8,16,128]{2,1,0:T(8,128)(2,1)S(1)}, u32[]{:S(2)}, u32[]{:S(2)}) async-start(bf16[8,16,128]{2,1,0:T(8,128)(2,1)} %get-tuple-element.41), calls=%async_computation.1 | async-start | bytes 65536 | tf_op jit(solution)/shard_map/all_to_all | solution.py:439
  28.4 0.0 collective-permute-done.1.odd
  28.4 4.8 %local.1.base = f32[2,16,512]{2,1,0:T(8,128)S(1)} custom-call(bf16[22,16,128]{2,1,0:T(8,128)(2,1)S(1)} %pack.1.own, bf16[22,16,128]{2,1,0:T(8,128)(2,1)S(1)} %collective-permute-done.even, bf16[22,16,128]{2,1,0:T(8,128)(2,1)S(1)} %collective-permute-done.1.odd, bf16[2,14,12,64,64]{4,3,2,1,0:T(8,128)(2,1)} %coupling.1, bf16[2,8,12,64,64]{4,3,2,1,0:T(8,128)(2,1)} %near.1, ...), custom_call_target="tpu_custom_call" | custom-call | flops 100000000 | bytes 20000000 | tf_op jit(solution)/shard_map/local/pallas_call | solution.py:362
  33.1 0.0 all-to-all-done.1.roots
  33.1 1.1 %final.1 = f32[2,16,512]{2,1,0:T(8,128)} custom-call(bf16[16,640]{1,0:T(8,128)(2,1)S(1)} %get-tuple-element.40.parts, bf16[8,16,128]{2,1,0:T(8,128)(2,1)S(1)} %all-to-all-done.1.roots, bf16[128,1536]{1,0:T(8,128)(2,1)S(1)} %get-tuple-element.42.fold, bf16[1024,128]{1,0:T(8,128)(2,1)S(1)} %get-tuple-element.43.leafs, f32[2,16,512]{2,1,0:T(8,128)S(1)} %local.1.base), custom_call_target="tpu_custom_call" | custom-call | tf_op jit(solution)/shard_map/final/pallas_call | solution.py:402
Async XLA Ops:
  3.0 18.6 %all-to-all-start = ((bf16[32,16,128]{2,1,0:T(8,128)(2,1)}), bf16[32,16,128]{2,1,0:T(8,128)(2,1)S(1)}, u32[]{:S(2)}, u32[]{:S(2)}) async-start(bf16[32,16,128]{2,1,0:T(8,128)(2,1)} %get-tuple-element.25), calls=%async_computation | async-start | bytes 262144 | tf_op jit(solution)/shard_map/all_to_all | solution.py:427
  15.7 6.8 %collective-permute-start = (bf16[22,16,128]{2,1,0:T(8,128)(2,1)S(1)}, bf16[22,16,128]{2,1,0:T(8,128)(2,1)S(1)}, u32[]{:S(2)}, u32[]{:S(2)}) collective-permute-start(bf16[22,16,128]{2,1,0:T(8,128)(2,1)S(1)} %pack.1.own), channel_id=1, source_target_pairs={{0,1},{1,0},{2,3},{3,2},{4,5},{5,4},{6,7},{7,6},{8,9},{9,8},{10,11... | collective-permute-start | bytes 270344 | tf_op jit(solution)/shard_map/ppermute | solution.py:433
  16.3 12.0 %collective-permute-start.1 = (bf16[22,16,128]{2,1,0:T(8,128)(2,1)S(1)}, bf16[22,16,128]{2,1,0:T(8,128)(2,1)S(1)}, u32[]{:S(2)}, u32[]{:S(2)}) collective-permute-start(bf16[22,16,128]{2,1,0:T(8,128)(2,1)S(1)} %pack.1.own), channel_id=1, source_target_pairs={{1,2},{2,1},{3,4},{4,3},{5,6},{6,5},{7,8},{8,7},{9,10},{10,9},{11,... | collective-permute-start | bytes 270344 | tf_op jit(solution)/shard_map/ppermute | solution.py:434
  22.4 10.7 %all-to-all-start.1 = ((bf16[8,16,128]{2,1,0:T(8,128)(2,1)}), bf16[8,16,128]{2,1,0:T(8,128)(2,1)S(1)}, u32[]{:S(2)}, u32[]{:S(2)}) async-start(bf16[8,16,128]{2,1,0:T(8,128)(2,1)} %get-tuple-element.41), calls=%async_computation.1 | async-start | bytes 65536 | tf_op jit(solution)/shard_map/all_to_all | solution.py:439

commit v11 on v9

--- a/solution.py
+++ b/solution.py
@@ -338,8 +338,6 @@
     each(functools.partial(far_body, 3, 0), 4, 4)
     bigs[3].wait()
     each(near_body, 0, 4)
-    bigs[4].wait()
-    each(near_body, 4, 4)
     for copy in smalls[2:]:
         copy.wait()
     up2 = [sums[12 + t].astype(bf16) for t in range(2)]
@@ -347,7 +345,11 @@
         (sums[8 + t] + dot_nt(up2[t // 2], tra[8 + t])).astype(bf16) for t in range(4)
     ]
     up0 = [(sums[t] + dot_nt(up1[t // 2], tra[t])).astype(bf16) for t in range(8)]
-    full = [cells[t] + dot_nt(up0[t], bas[t]) for t in range(8)]
+    for t in range(LEAVES):
+        sums[t] = dot_nt(up0[t], bas[t])
+    bigs[4].wait()
+    each(near_body, 4, 4)
+    full = [cells[t] + sums[t] for t in range(LEAVES)]
     for pair in range(LEAVES // 2):
         both = jnp.concatenate([full[2 * pair], full[2 * pair + 1]], axis=1)
         for g in range(2):

time: 34.5 us -> 34.5 us (level)
  no operation moved by 1% of the time
where the time goes in v11:
time: 34.5 us; the launch traced here: 34.2 us
  starting transfers between devices  23.3 us (68%)
  Pallas kernels  10.7 us (31%)
    all_to_all x1, starting transfers between devices, per_device(): lax.all_to_all(sent, 'leaf', 0, 0, axis_index_groups=[list(range(N_LEAF -...  12.6 us
    all_to_all x1, starting transfers between devices, per_device(): roots = lax.all_to_all(fan, 'branch', 0, 0, tiled=True)  5.93 us
    pallas_call x1, Pallas kernels, local_call(): pl.pallas_call(local_kernel, out_shape=pltpu.VMEM((2, RHS, LEAVES * R), f...  4.5 us
    ppermute x1, starting transfers between devices, per_device(): lax.ppermute(rows, ring, [(i, (i + 1 ^ 1) - 1) for i in range(1, count -...  4.1 us
    pallas_call x1, Pallas kernels, up_call(): pl.pallas_call(up_kernel, out_shape=[pltpu.VMEM((2, RHS, LEAVES * R), bf1...  2.96 us
    pallas_call x1, Pallas kernels, final_call(): pl.pallas_call(final_kernel, out_shape=jax.ShapeDtypeStruct((2, RHS, LEAV...  1.13 us
    pallas_call x1, Pallas kernels, mid_call(): pl.pallas_call(mid_kernel, out_shape=[pltpu.VMEM((RHS, DEPTH * 2 * R), bf...  0.8 us
  transfers between devices with their start and end apart: 4, of which 1 were waited for; matrix products, arithmetic and copies ran while one was open for 0% of the time, Pallas kernels for 19%

profile of v11, /device:TPU:1, one launch (start us, length us, event | category | flops | bytes accessed | tf_op | source)
XLA Modules:
  0.0 34.2 jit_solution(684774205350107918)
XLA Ops:
  0.0 3.0 %up.1 = (bf16[2,16,512]{2,1,0:T(8,128)(2,1)S(1)}, bf16[14,32,64]{2,1,0:T(8,128)(2,1)S(1)}, bf16[32,16,128]{2,1,0:T(8,128)(2,1)}, bf16[16,128]{1,0:T(8,128)(2,1)S...) custom-call(bf16[2,16,512]{2,1,0:T(8,128)(2,1)} %values.1, ...), custom_call_target="tpu_custom_call" | custom-call | tf_op jit(solution)/shard_map/up/pallas_call | solution.py:114
  3.0 12.6 %all-to-all-start = ((bf16[32,16,128]{2,1,0:T(8,128)(2,1)}), bf16[32,16,128]{2,1,0:T(8,128)(2,1)S(1)}, u32[]{:S(2)}, u32[]{:S(2)}) async-start(bf16[32,16,128]{2,1,0:T(8,128)(2,1)} %get-tuple-element.25), calls=%async_computation | async-start | bytes 262144 | tf_op jit(solution)/shard_map/all_to_all | solution.py:425
  15.6 0.1 pack.1.own
  15.7 0.7 %collective-permute-start = (bf16[22,16,128]{2,1,0:T(8,128)(2,1)S(1)}, bf16[22,16,128]{2,1,0:T(8,128)(2,1)S(1)}, u32[]{:S(2)}, u32[]{:S(2)}) collective-permute-start(bf16[22,16,128]{2,1,0:T(8,128)(2,1)S(1)} %pack.1.own), channel_id=1, source_target_pairs={{0,1},{1,0},{2,3},{3,2},{4,5},{5,4},{6,7},{7,6},{8,9},{9,8},{10,11... | collective-permute-start | bytes 270344 | tf_op jit(solution)/shard_map/ppermute | solution.py:431
  16.3 4.1 %collective-permute-start.1 = (bf16[22,16,128]{2,1,0:T(8,128)(2,1)S(1)}, bf16[22,16,128]{2,1,0:T(8,128)(2,1)S(1)}, u32[]{:S(2)}, u32[]{:S(2)}) collective-permute-start(bf16[22,16,128]{2,1,0:T(8,128)(2,1)S(1)} %pack.1.own), channel_id=1, source_target_pairs={{1,2},{2,1},{3,4},{4,3},{5,6},{6,5},{7,8},{8,7},{9,10},{10,9},{11,... | collective-permute-start | bytes 270344 | tf_op jit(solution)/shard_map/ppermute | solution.py:432
  20.4 0.6 %cast.1.lift = bf16[640,128]{1,0:T(8,128)(2,1)S(1)} custom-call(bf16[5,64,64]{2,1,0:T(8,128)(2,1)S(1)} %get-tuple-element.27.own, bf16[5,64,64]{2,1,0:T(8,128)(2,1)S(1)} %get-tuple-element.28.sib), custom_call_target="tpu_custom_call" | custom-call | flops 100000000 | bytes 4000000 | tf_op jit(solution)/shard_map/cast/pallas_call | solution.py:178
  21.0 0.6 %prep.1 = (bf16[128,1536]{1,0:T(8,128)(2,1)S(1)}, bf16[1024,128]{1,0:T(8,128)(2,1)S(1)}) custom-call(bf16[5,2,64,64]{3,2,1,0:T(8,128)(2,1)S(1)} %get-tuple-element.33.cou, bf16[2,1,7,64,64]{4,3,2,1,0:T(8,128)(2,1)S(1)} %get-tuple-element.34.tops, bf16[5,64,64]{2,1,0:T(8,128)(2,1)S(1)} %get-tuple-element.35.downs, ...), custom_call_target="tpu_custom_call" | custom-call | flops 100000000 | bytes 4000000 | tf_op jit(solution)/shard_map/prep/pallas_call | solution.py:214
  21.6 0.0 all-to-all-done.got
  21.6 0.8 %mid.1 = (bf16[16,640]{1,0:T(8,128)(2,1)S(1)}, bf16[8,16,128]{2,1,0:T(8,128)(2,1)}) custom-call(bf16[32,16,128]{2,1,0:T(8,128)(2,1)S(1)} %all-to-all-done.got, bf16[16,128]{1,0:T(8,128)(2,1)S(1)} %get-tuple-element.26.summit, bf16[640,128]{1,0:T(8,128)(2,1)S(1)} %cast.1.lift), custom_call_target="tpu_custom_call" | custom-call | tf_op jit(solution)/shard_map/mid/pallas_call | solution.py:244
  22.4 0.0 collective-permute-done.even
  22.4 5.9 %all-to-all-start.1 = ((bf16[8,16,128]{2,1,0:T(8,128)(2,1)}), bf16[8,16,128]{2,1,0:T(8,128)(2,1)S(1)}, u32[]{:S(2)}, u32[]{:S(2)}) async-start(bf16[8,16,128]{2,1,0:T(8,128)(2,1)} %get-tuple-element.41), calls=%async_computation.1 | async-start | bytes 65536 | tf_op jit(solution)/shard_map/all_to_all | solution.py:437
  28.4 0.0 collective-permute-done.1.odd
  28.4 4.5 %local.1.base = f32[2,16,512]{2,1,0:T(8,128)S(1)} custom-call(bf16[22,16,128]{2,1,0:T(8,128)(2,1)S(1)} %pack.1.own, bf16[22,16,128]{2,1,0:T(8,128)(2,1)S(1)} %collective-permute-done.even, bf16[22,16,128]{2,1,0:T(8,128)(2,1)S(1)} %collective-permute-done.1.odd, bf16[2,14,12,64,64]{4,3,2,1,0:T(8,128)(2,1)} %coupling.1, bf16[2,8,12,64,64]{4,3,2,1,0:T(8,128)(2,1)} %near.1, ...), custom_call_target="tpu_custom_call" | custom-call | flops 100000000 | bytes 20000000 | tf_op jit(solution)/shard_map/local/pallas_call | solution.py:360
  32.9 0.2 all-to-all-done.1.roots
  33.1 1.1 %final.1 = f32[2,16,512]{2,1,0:T(8,128)} custom-call(bf16[16,640]{1,0:T(8,128)(2,1)S(1)} %get-tuple-element.40.parts, bf16[8,16,128]{2,1,0:T(8,128)(2,1)S(1)} %all-to-all-done.1.roots, bf16[128,1536]{1,0:T(8,128)(2,1)S(1)} %get-tuple-element.42.fold, bf16[1024,128]{1,0:T(8,128)(2,1)S(1)} %get-tuple-element.43.leafs, f32[2,16,512]{2,1,0:T(8,128)S(1)} %local.1.base), custom_call_target="tpu_custom_call" | custom-call | tf_op jit(solution)/shard_map/final/pallas_call | solution.py:400
Async XLA Ops:
  3.0 18.6 %all-to-all-start = ((bf16[32,16,128]{2,1,0:T(8,128)(2,1)}), bf16[32,16,128]{2,1,0:T(8,128)(2,1)S(1)}, u32[]{:S(2)}, u32[]{:S(2)}) async-start(bf16[32,16,128]{2,1,0:T(8,128)(2,1)} %get-tuple-element.25), calls=%async_computation | async-start | bytes 262144 | tf_op jit(solution)/shard_map/all_to_all | solution.py:425
  15.7 6.8 %collective-permute-start = (bf16[22,16,128]{2,1,0:T(8,128)(2,1)S(1)}, bf16[22,16,128]{2,1,0:T(8,128)(2,1)S(1)}, u32[]{:S(2)}, u32[]{:S(2)}) collective-permute-start(bf16[22,16,128]{2,1,0:T(8,128)(2,1)S(1)} %pack.1.own), channel_id=1, source_target_pairs={{0,1},{1,0},{2,3},{3,2},{4,5},{5,4},{6,7},{7,6},{8,9},{9,8},{10,11... | collective-permute-start | bytes 270344 | tf_op jit(solution)/shard_map/ppermute | solution.py:431
  16.3 12.0 %collective-permute-start.1 = (bf16[22,16,128]{2,1,0:T(8,128)(2,1)S(1)}, bf16[22,16,128]{2,1,0:T(8,128)(2,1)S(1)}, u32[]{:S(2)}, u32[]{:S(2)}) collective-permute-start(bf16[22,16,128]{2,1,0:T(8,128)(2,1)S(1)} %pack.1.own), channel_id=1, source_target_pairs={{1,2},{2,1},{3,4},{4,3},{5,6},{6,5},{7,8},{8,7},{9,10},{10,9},{11,... | collective-permute-start | bytes 270344 | tf_op jit(solution)/shard_map/ppermute | solution.py:432
  22.4 10.6 %all-to-all-start.1 = ((bf16[8,16,128]{2,1,0:T(8,128)(2,1)}), bf16[8,16,128]{2,1,0:T(8,128)(2,1)S(1)}, u32[]{:S(2)}, u32[]{:S(2)}) async-start(bf16[8,16,128]{2,1,0:T(8,128)(2,1)} %get-tuple-element.41), calls=%async_computation.1 | async-start | bytes 65536 | tf_op jit(solution)/shard_map/all_to_all | solution.py:437
